TPU v7x, 128 devices: a whole 4x4x4 slice. The times are simulated.
128 devices in a mesh: geno: 16 (over y, z_lo, core), trial: 8 (over x, z_hi).
Axes of the slice: x: 4, y: 4, z: 4 (z_hi: 2, z_lo: 2; z = z_hi * 2 + z_lo), core: 2. Of those that a mesh axis runs over, the one named last changes fastest.
Arguments:
- right_side: float32 [12288, 1, 2048], P('geno', None, 'trial'), may hold values from -6 to 6
- observed: int32 [12288, 2048], P('geno', 'trial'), may hold values from 0 to 1, as said below
- row_length: int32 [2048], P('trial'), may hold values from 2 to 16
- field_coef: float32 [2048], P('trial'), may hold values from 0.5 to 4
- kernel_geno: bfloat16 [12288, 12288], P('geno'), may hold values from -1 to 3, as said below
- kernel_trial: bfloat16 [2048, 2048], P('trial'), may hold values from -1 to 3, as said below
Outputs:
- solution_field: float32 [12288, 1, 2048], P('geno', None, 'trial')
- residual: float32 [12288, 1, 2048], P('geno', None, 'trial')
Inputs may be any that keep to these rules, and one draw needn't show every extreme that they name: kernel_geno is symmetric. kernel_trial is symmetric. 1 marks an observed cell, 0 a missing one.
All inputs are finite; a program needn't handle non-finite values.
Results may differ from a plain program's by a relative error of at most 0.0028.
Values may be sent and summed in bfloat16 or wider, within the bound.
No kernel may reach another device: no remote copies, remote signals or barrier semaphores. Data moves between devices by JAX's collectives and lax.ppermute only.
A program may use at most 128 MiB of HBM per device.

v0:
```python
import jax
import jax.numpy as jnp
from jax import lax
from jax.sharding import PartitionSpec as P

ITERS = 2


def padded_2(cells, sides, width):
    for axis, dim in sides:
        count = lax.axis_size(axis)
        ends = count - 1
        head = lax.slice_in_dim(cells, 0, width, axis=dim)
        tail = lax.slice_in_dim(cells, cells.shape[dim] - width, cells.shape[dim], axis=dim)
        cells = jnp.concatenate(
            [
                lax.ppermute(tail, axis, [(i, (i + 1) % count) for i in range(ends)]),
                cells,
                lax.ppermute(head, axis, [((i + 1) % count, i) for i in range(ends)]),
            ],
            axis=dim,
        )
    return cells


def on_device(right_side, observed, row_length, field_coef, kernel_geno, kernel_trial):
    geno_rows = right_side.shape[0]
    sides = right_side.shape[1]
    trial_cols = right_side.shape[2]
    observed_f = observed.astype(jnp.float32)[:, None, :]
    total_rows = geno_rows * lax.axis_size("geno")
    position = lax.axis_index("geno") * geno_rows - 1 + lax.iota(jnp.int32, geno_rows + 1)
    position = position[:, None]
    keep = (
        (position >= 0) & (position + 1 < total_rows) & ((position + 1) % row_length[None, :] != 0)
    )
    links = keep.astype(jnp.float32)[:, None, :]
    coef = field_coef[None, None, :]

    def squares(vector):
        return lax.psum(jnp.sum(vector * vector, axis=(0, 2)), ("geno", "trial"))

    solution_field = jnp.zeros_like(right_side)
    residual = right_side
    direction = right_side
    norm_now = squares(residual)
    for step in range(ITERS):
        masked = (observed_f * direction).astype(jnp.bfloat16)
        flat = masked.reshape(geno_rows, sides * trial_cols)
        mixed = lax.psum_scatter(
            jnp.einsum("jc,jx->cx", kernel_geno, flat, preferred_element_type=jnp.float32),
            "geno",
            scatter_dimension=0,
            tiled=True,
        )
        mixed = mixed.reshape(geno_rows, sides, trial_cols)
        mixed = mixed.astype(jnp.bfloat16)
        crossed = jnp.einsum(
            "grn,fn->grf",
            lax.all_gather(mixed, "trial", axis=2, tiled=True),
            kernel_trial,
            preferred_element_type=jnp.float32,
        )
        padded = padded_2(direction, (("geno", 0),), 1)
        flux = links * (padded[1:] - padded[:-1])
        field = direction - coef * (flux[1:] - flux[:-1])
        image = observed_f * crossed + field
        product = lax.psum(jnp.sum(direction * image, axis=(0, 2)), ("geno", "trial"))
        alpha = (norm_now / product)[None, :, None]
        solution_field = solution_field + alpha * direction
        residual = residual - alpha * image
        norm_next = squares(residual)
        direction = residual + (norm_next / norm_now)[None, :, None] * direction
        norm_now = norm_next
    return (solution_field, residual)


def solution(mesh):
    return jax.shard_map(
        on_device,
        mesh=mesh,
        in_specs=(
            P("geno", None, "trial"),
            P("geno", "trial"),
            P("trial"),
            P("trial"),
            P("geno", None),
            P("trial", None),
        ),
        out_specs=(P("geno", None, "trial"), P("geno", None, "trial")),
        check_vma=False,
    )
```

profile of v0, /device:TPU:1, one launch (start us, length us, event | category | flops | bytes accessed | tf_op | source)
XLA Modules:
  0.0 658.1 jit_solution(12127938514824939140)
XLA Ops:
  7.2 0.0 copy-start
  7.2 0.0 reduce-scatter.3.cloned.1.call-start
  7.2 12.2 %convolution_bitcast_fusion.1 = f32[12288,256]{0,1:T(8,128)} fusion(bf16[768,12288]{1,0:T(8,128)(2,1)} %param.10, s32[768,256]{1,0:T(8,128)} %param.7, f32[768,1,256]{2,1,0:T(1,128)} %param.6), kind=kOutput, calls=%fused_computation.1 | convolution fusion | flops 4832428032 | bytes 33030144 | tf_op jit(solution)/shard_map/jc,jx->cx/dot_general | solution.py:51
  19.4 0.0 copy-start.1
  19.4 0.0 copy-start.3
  19.4 0.0 copy-start.2
  19.4 0.0 copy-start.4
  19.5 0.0 reduce-scatter.3.cloned.1.call-update
  19.5 0.0 all-gather.5.cloned.1.call-start
  19.5 141.9 %reduce-scatter.3.cloned.1.call-done = f32[768,256]{0,1:T(8,128)} async-done(((f32[12288,256]{0,1:T(8,128)}), f32[768,256]{0,1:T(8,128)}) %reduce-scatter.3.cloned.1.call-update) | async-done | bytes 786448 | tf_op jit(solution)/shard_map/reduce_scatter | solution.py:50
  161.4 1.9 convert_element_type.25
  163.3 0.0 all-gather.5.cloned.1.call-update
  163.4 0.0 reduce-scatter.5.cloned.1.call-start
  163.4 0.0 copy-done.1
  163.4 1.9 collective-permute-start
  165.4 3.6 collective-permute-start.1
  169.0 2.2 multiply_reduce_fusion.3
  171.3 0.0 copy-done.3
  171.3 0.1 copy.14
  171.3 0.0 collective-permute-done
  171.4 0.0 collective-permute-done.1
  171.4 9.3 %fusion.5 = f32[769,1,256]{2,0,1:T(8,128)} fusion(f32[1,1,256]{2,0,1:T(1,128)S(1)} %collective-permute-done, f32[768,1,256]{2,0,1:T(8,128)S(1)} %copy.14, f32[1,1,256]{2,0,1:T(1,128)S(1)} %collective-permute-done.1, pred[256]{0:T(512)(128)(4,1)S(1)} %broadcast_compare_fusion, s32[256]{0:T(256)S(1)} %compare_select_fusion, s32[769]{0:T(1024)S(1)} %fusion.20, ...), kind=kLoop, calls=%fused_computation.14 | loop fusion | flops 2559232 | bytes 1581061 | tf_op jit(solution)/shard_map/mul | solution.py:65
  180.7 46.5 %all-gather.5.cloned.1.call-done = bf16[768,2048]{0,1:T(8,128)(2,1)} async-done(((bf16[768,256]{0,1:T(8,128)(2,1)}), bf16[768,2048]{0,1:T(8,128)(2,1)}) %all-gather.5.cloned.1.call-update) | async-done | bytes 3145744 | tf_op jit(solution)/shard_map/all_gather | solution.py:60
  227.2 0.0 copy-done
  227.2 0.0 copy-done.2
  227.2 0.0 copy-done.4
  227.2 4.0 multiply_reduce_fusion.2
  231.2 64.5 %all-reduce = (f32[1]{0:T(128)}, f32[1]{0:T(128)}) all-reduce(f32[1]{0:T(128)} %bitcast, f32[1]{0:T(128)} %bitcast.7), channel_id=1, replica_groups=mesh['geno'=16,'trial'=8] {'geno','trial'}, use_global_device_ids=true, to_apply=%region_1.2 | all-reduce | flops 2 | bytes 16 | tf_op jit(solution)/shard_map/psum | solution.py:41
  297.1 0.8 multiply_reduce_fusion.1
  297.9 62.8 %psum.30 = f32[1]{0:T(128)} all-reduce(f32[1]{0:T(128)} %bitcast.9), channel_id=1, replica_groups=mesh['geno'=16,'trial'=8] {'geno','trial'}, use_global_device_ids=true, to_apply=%region_6.7 | all-reduce | flops 1 | bytes 8 | tf_op jit(solution)/shard_map/psum | solution.py:41
  362.0 0.1 multiply_add_fusion.1
  362.1 11.9 %convolution_bitcast_fusion = f32[12288,256]{0,1:T(8,128)} fusion(bf16[768,12288]{1,0:T(8,128)(2,1)} %param.10, f32[768,1,256]{2,0,1:T(8,128)S(1)} %multiply_add_fusion.1, s32[768,256]{1,0:T(8,128)} %param.7), kind=kOutput, calls=%fused_computation | convolution fusion | flops 4832428032 | bytes 33030144 | tf_op jit(solution)/shard_map/jc,jx->cx/dot_general | solution.py:51
  374.0 0.0 reduce-scatter.5.cloned.1.call-update
  374.0 0.0 all-gather.7.cloned.1.call-start
  374.1 135.9 %reduce-scatter.5.cloned.1.call-done = f32[768,256]{0,1:T(8,128)} async-done(((f32[12288,256]{0,1:T(8,128)}), f32[768,256]{0,1:T(8,128)}) %reduce-scatter.5.cloned.1.call-update) | async-done | bytes 786448 | tf_op jit(solution)/shard_map/reduce_scatter | solution.py:50
  510.0 1.9 convert_element_type.28
  511.9 0.0 all-gather.7.cloned.1.call-update
  512.0 1.9 collective-permute-start.2
  513.9 3.6 collective-permute-start.3
  517.5 0.0 collective-permute-done.2
  517.5 0.7 collective-permute-done.3
  518.2 9.3 %fusion.6 = f32[769,1,256]{2,0,1:T(8,128)} fusion(f32[1,1,256]{2,0,1:T(1,128)S(1)} %collective-permute-done.2, f32[768,1,256]{2,0,1:T(8,128)S(1)} %multiply_add_fusion.1, f32[1,1,256]{2,0,1:T(1,128)S(1)} %collective-permute-done.3, pred[256]{0:T(512)(128)(4,1)S(1)} %broadcast_compare_fusion, s32[256]{0:T(256)S(1)} %compare_select_fusion, ...), kind=kLoop, calls=%fused_computation.16 | loop fusion | flops 2559232 | bytes 1581061 | tf_op jit(solution)/shard_map/mul | solution.py:65
  527.5 48.1 %all-gather.7.cloned.1.call-done = bf16[768,2048]{0,1:T(8,128)(2,1)} async-done(((bf16[768,256]{0,1:T(8,128)(2,1)}), bf16[768,2048]{0,1:T(8,128)(2,1)}) %all-gather.7.cloned.1.call-update) | async-done | bytes 3145744 | tf_op jit(solution)/shard_map/all_gather | solution.py:60
  575.6 5.1 multiply_reduce_fusion
  580.7 64.8 %psum.31 = f32[1]{0:T(128)} all-reduce(f32[1]{0:T(128)} %bitcast.14), channel_id=1, replica_groups=mesh['geno'=16,'trial'=8] {'geno','trial'}, use_global_device_ids=true, to_apply=%region_9.10 | all-reduce | flops 1 | bytes 8 | tf_op jit(solution)/shard_map/psum | solution.py:68
  646.8 1.3 multiply_subtract_fusion
  648.2 1.7 copy.18
  649.8 1.7 copy.19
  (6 shorter events, 0.0 us)
Async XLA Ops:
  7.2 220.0 %copy-start = (bf16[256,2048]{1,0:T(8,128)(2,1)S(1)}, bf16[256,2048]{1,0:T(8,128)(2,1)}, u32[]{:S(2)}) copy-start(bf16[256,2048]{1,0:T(8,128)(2,1)} %param.11) | copy-start | bytes 3145732
  7.2 154.2 %reduce-scatter.3.cloned.1.call-start = ((), (), s32[]{:S(2)}) async-start(), calls=%async_computation.2 | async-start | bytes 13369344 | tf_op jit(solution)/shard_map/reduce_scatter | solution.py:50
  19.4 144.0 %copy-start.1 = (f32[768,1,256]{2,1,0:T(1,128)S(1)}, f32[768,1,256]{2,1,0:T(1,128)}, u32[]{:S(2)}) copy-start(f32[768,1,256]{2,1,0:T(1,128)} %param.6) | copy-start | bytes 2359300
  19.4 151.8 %copy-start.3 = (s32[256]{0:T(256)S(1)}, s32[256]{0:T(256)}, u32[]{:S(2)}) copy-start(s32[256]{0:T(256)} %param.8) | copy-start | bytes 3076
  19.4 207.7 %copy-start.2 = (s32[768,256]{1,0:T(8,128)S(1)}, s32[768,256]{1,0:T(8,128)}, u32[]{:S(2)}) copy-start(s32[768,256]{1,0:T(8,128)} %param.7) | copy-start | bytes 2359300
  19.4 207.7 %copy-start.4 = (f32[256]{0:T(256)S(1)}, f32[256]{0:T(256)}, u32[]{:S(2)}) copy-start(f32[256]{0:T(256)} %param.9) | copy-start | bytes 3076
  19.5 207.7 %all-gather.5.cloned.1.call-start = ((), (), s32[]{:S(2)}) async-start(), calls=%async_computation.4 | async-start | bytes 3538944 | tf_op jit(solution)/shard_map/all_gather | solution.py:60
  163.4 346.6 %reduce-scatter.5.cloned.1.call-start = ((), (), s32[]{:S(2)}) async-start(), calls=%async_computation.3 | async-start | bytes 13369344 | tf_op jit(solution)/shard_map/reduce_scatter | solution.py:50
  163.4 7.9 %collective-permute-start = (f32[1,1,256]{2,0,1:T(1,128)S(1)}, f32[1,1,256]{2,0,1:T(1,128)S(1)}, u32[]{:S(2)}, u32[]{:S(2)}) collective-permute-start(f32[1,1,256]{2,0,1:T(1,128)S(1)} %get-tuple-element.11), channel_id=1, source_target_pairs={{8,0},{16,8},{24,16},{32,24},{40,32},{48,40},{56,48},{64,56},{72,6... | collective-permute-start | bytes 3080 | tf_op jit(solution)/shard_map/ppermute | solution.py:19
  165.4 6.0 collective-permute-start.1
  374.0 201.5 %all-gather.7.cloned.1.call-start = ((), (), s32[]{:S(2)}) async-start(), calls=%async_computation.5 | async-start | bytes 3538944 | tf_op jit(solution)/shard_map/all_gather | solution.py:60
  512.0 5.6 collective-permute-start.2
  513.9 4.4 collective-permute-start.3
Sparse Core Ops, SparseCore 0:
  19.6 141.7 reduce-scatter.2
  164.3 62.7 all-gather.4
  374.2 135.7 reduce-scatter.4
  512.7 62.8 all-gather.6
where the time goes:
time: 659 us; the launch traced here: 658 us
  waiting for transfers between devices  373 us (57%)
  blocking collectives  192 us (29%)
  matrix products  33.3 us (5%)
  other arithmetic  26.9 us (4%)
  between operations  17.9 us (3%)
  starting transfers between devices  11.3 us (2%)
    reduce_scatter x2, waiting for transfers between devices, on_device(): lax.psum_scatter(jnp.einsum('jc,jx->cx', kernel_geno, flat, preferred_ele...  278 us
    psum x2, blocking collectives, squares(): return lax.psum(jnp.sum(vector * vector, axis=(0, 2)), ('geno', 'trial'))  127 us
    all_gather x2, waiting for transfers between devices, on_device(): lax.all_gather(mixed, 'trial', axis=2, tiled=True)  94.6 us
    psum x1, blocking collectives, on_device(): lax.psum(jnp.sum(direction * image, axis=(0, 2)), ('geno', 'trial'))  64.8 us
    dot_general x2, matrix products, on_device(): jnp.einsum('jc,jx->cx', kernel_geno, flat, preferred_element_type=jnp.flo...  24.1 us
    mul x2, other arithmetic, on_device(): flux = links * (padded[1:] - padded[:-1])  18.6 us
  transfers between devices with their start and end apart: 8, of which 5 were waited for; matrix products, arithmetic and copies ran while one was open for 3% of the time, Pallas kernels for 0%

commit v1 on v0

v1 whole, which is shorter than its diff:
```python
import jax
import jax.numpy as jnp
from jax import lax
from jax.experimental import pallas as pl
from jax.experimental.pallas import tpu as pltpu
from jax.sharding import PartitionSpec as P

BOTH = ("geno", "trial")
RING, PAIR, CORES = 4, 2, 2
F32, BF16 = jnp.float32, jnp.bfloat16
SMEM = pl.BlockSpec(memory_space=pltpu.SMEM)
VMEM = pl.BlockSpec(memory_space=pltpu.VMEM)
ANY = pl.BlockSpec(memory_space=pl.ANY)
HBM = pl.BlockSpec(memory_space=pltpu.HBM)


def place(index):
    geno, trial = divmod(index, RING * PAIR)
    return (geno // 4, geno // 2 % 2, geno % 2, trial // 2, trial % 2)


def hop(cells, **by):
    step = [by.get(name, 0) for name in ("y", "z", "core", "x", "far")]
    pairs = []
    for index in range(RING * PAIR * CORES * RING * PAIR):
        y, z, core, x, far = (a + b for a, b in zip(place(index), step))
        geno = ((y % RING) * PAIR + z % PAIR) * CORES + core % CORES
        pairs.append((index, geno * RING * PAIR + (x % RING) * PAIR + far % PAIR))
    return lax.ppermute(cells, BOTH, pairs)


def spread(cells, ring, pair, direct):
    side = hop(cells, **{pair: 1})
    up = hop(cells, **{ring: 1})
    down = hop(cells, **{ring: -1})
    across = hop(cells, **{ring: 2})
    side_up = hop(side, **{ring: 1})
    side_down = hop(side, **{ring: -1})
    side_across = hop(side, **{ring: 2}) if direct else hop(across, **{pair: 1})
    return [
        (0, 0, cells),
        (0, 1, side),
        (1, 0, up),
        (-1, 0, down),
        (1, 1, side_up),
        (-1, 1, side_down),
        (2, 0, across),
        (2, 1, side_across),
    ]


def gather_geno(cells, direct):
    geno = lax.axis_index("geno")
    y, z, core = geno // 4, geno // 2 % 2, geno % 2
    pieces, order = [], []
    for a, b, piece in spread(cells, "y", "z", direct):
        base = (((y - a) % RING) * PAIR + (z + b) % PAIR) * CORES
        pieces += [piece, hop(piece, core=1)]
        order += [base + core, base + 1 - core]
    return pieces, jnp.stack(order).astype(jnp.int32)


STRIP = 5


def split(values, count):
    terms = []
    for _ in range(count):
        terms.append(values.astype(BF16))
        values = values - terms[-1].astype(F32)
    return terms


def pack(core, trial, right, observed, coef, length, kernel_trial):
    rows, cols = right.shape
    count = kernel_trial.shape[1] // cols
    part, half = rows // count, kernel_trial.shape[0] // 2

    def body(core_ref, trial_ref, right_ref, seen_ref, coef_ref, length_ref, kernel_ref, slab_ref, strip_ref):
        below = pl.multiple_of(core_ref[0] * half, half)
        for r in range(STRIP):
            at = pl.multiple_of(lax.rem(trial_ref[0] + r, count) * cols, cols)
            block = kernel_ref[pl.ds(below, half), pl.ds(at, cols)]
            for t in range(count):
                strip_ref[t, r] = block
        line = lax.broadcasted_iota(jnp.int32, (16, cols), 0)
        extra = jnp.zeros((16, cols), F32)
        values = coef_ref[...]
        for k in range(3):
            term = values.astype(BF16).astype(F32)
            extra = jnp.where(line == k, term, extra)
            values = values - term
        extra = jnp.where(line == 3, length_ref[...].astype(F32), extra).astype(BF16)
        for t in range(count):
            at = slice(t * part, (t + 1) * part)
            high, low = split(right_ref[at], 2)
            slab_ref[t, :part] = high
            slab_ref[t, part : 2 * part] = low
            slab_ref[t, 2 * part : 3 * part] = seen_ref[at].astype(F32).astype(BF16)
            slab_ref[t, 3 * part :] = extra

    return pl.pallas_call(
        body,
        out_shape=[
            jax.ShapeDtypeStruct((count, 3 * part + 16, cols), BF16),
            jax.ShapeDtypeStruct((count, STRIP, half, cols), BF16),
        ],
        in_specs=[SMEM] * 2 + [VMEM] * 5,
        out_specs=[VMEM] * 2,
        compiler_params=pltpu.CompilerParams(vmem_limit_bytes=24 << 20),
    )(core, trial, right, observed, coef, length, kernel_trial)


def swap(slabs):
    return lax.all_to_all(slabs, "trial", split_axis=0, concat_axis=0, tiled=True)


def totals(row):
    devices = lax.axis_size("geno") * lax.axis_size("trial")
    copies = jnp.broadcast_to(row[None], (devices,) + row.shape)
    return jnp.sum(lax.all_to_all(copies, BOTH, 0, 0, tiled=True), axis=(0, 1))


def mix(kernel, pieces, order, kind):
    count = len(pieces)
    rows, cols = pieces[0].shape

    def body(order_ref, kernel_ref, *refs):
        out_ref, total = refs[count], refs[count + 1]
        for k in range(count):
            at = pl.ds(pl.multiple_of(order_ref[k] * rows, rows), rows)
            for m in range(0, rows, 256):
                term = jnp.dot(
                    kernel_ref[m : m + 256, at], refs[k][...], preferred_element_type=F32
                )
                if k == 0:
                    total[m : m + 256] = term
                elif k < count - 1:
                    total[m : m + 256] += term
                else:
                    out_ref[m : m + 256] = (total[m : m + 256] + term).astype(out_ref.dtype)

    return pl.pallas_call(
        body,
        out_shape=jax.ShapeDtypeStruct((rows, cols), kind),
        in_specs=[SMEM] + [VMEM] * (1 + count),
        out_specs=VMEM,
        scratch_shapes=[pltpu.VMEM((rows, cols), F32)],
        compiler_params=pltpu.CompilerParams(vmem_limit_bytes=32 << 20),
        cost_estimate=pl.CostEstimate(
            flops=2 * rows * rows * cols * count,
            bytes_accessed=(rows * rows + rows * cols) * 2 * count,
            transcendentals=0,
        ),
    )(order, kernel, *pieces)


def fetch(core_ref, strip_refs, held, sems):
    copies = []
    half = strip_refs[0].shape[2]
    for side, strip_ref in enumerate(strip_refs):
        here = core_ref[0] if side == 0 else 1 - core_ref[0]
        at = pl.ds(pl.multiple_of(here * half, half), half)
        for t in range(strip_ref.shape[0]):
            copies.append(
                pltpu.make_async_copy(strip_ref.at[t], held.at[t, :, at], sems.at[side, t])
            )
    for copy in copies:
        copy.start()
    return copies


def multiply(left_ref, copies, held, total):
    total[...] = jnp.zeros_like(total)
    count = left_ref.shape[0]
    for t in range(count):
        copies[t].wait()
        copies[count + t].wait()
        for r in range(STRIP):
            other = (t + r) % count
            block = held[t, r]
            total[other] += jnp.dot(left_ref[t], block, preferred_element_type=F32)
            if 0 < r < STRIP - 1:
                total[t] += lax.dot_general(
                    left_ref[other], block, (((1,), (1,)), ((), ())), preferred_element_type=F32
                )


def cross_call(body, operands, strips, shapes, scratch):
    count, part, cols = operands[-1].shape
    return pl.pallas_call(
        body,
        out_shape=shapes,
        in_specs=[SMEM if x.ndim == 1 else VMEM for x in operands] + [ANY] * 2,
        out_specs=[VMEM] * len(shapes),
        scratch_shapes=scratch
        + [
            pltpu.VMEM((count, part, cols), F32),
            pltpu.VMEM((count, STRIP, cols, cols), BF16),
            pltpu.SemaphoreType.DMA((2, count)),
        ],
        compiler_params=pltpu.CompilerParams(vmem_limit_bytes=32 << 20),
        cost_estimate=pl.CostEstimate(
            flops=2 * part * (count * cols) ** 2,
            bytes_accessed=2 * (count * cols) ** 2,
            transcendentals=0,
        ),
    )(*operands, *strips)


def cross_first(core, mixed, seen, field, right, strips):
    count, part, cols = right.shape

    def body(core_ref, mixed_ref, seen_ref, field_ref, right_ref, *refs):
        image_ref, sums_ref, total, held, sems = refs[2:]
        multiply(mixed_ref, fetch(core_ref, refs[:2], held, sems), held, total)
        sums = [jnp.zeros((part, cols), F32) for _ in range(3)]
        for t in range(count):
            image = seen_ref[t].astype(F32) * total[t] + field_ref[t]
            image_ref[t] = image
            right_t = right_ref[t]
            terms = (right_t * right_t, right_t * image, image * image)
            sums = [a + b for a, b in zip(sums, terms)]
        lane = lax.broadcasted_iota(jnp.int32, (1, 128), 1)
        row = jnp.zeros((1, 128), F32)
        for k in range(3):
            row = jnp.where(lane == k, jnp.sum(sums[k]), row)
        sums_ref[...] = row

    shapes = [jax.ShapeDtypeStruct(right.shape, F32), jax.ShapeDtypeStruct((1, 128), F32)]
    return cross_call(body, [core, mixed, seen, field, right], strips, shapes, [])


def cross_second(core, factors, seen, right, image, strips):
    count, part, cols = right.shape

    def body(core_ref, factor_ref, seen_ref, right_ref, image_ref, *refs):
        out_ref, left, total, held, sems = refs[2:]
        copies = fetch(core_ref, refs[:2], held, sems)
        for t in range(count):
            right_t = right_ref[t]
            direction = right_t - factor_ref[0] * image_ref[t] + factor_ref[1] * right_t
            high, low = split(image_ref[t], 2)
            out_ref[t, part : 2 * part] = high
            out_ref[t, 2 * part :] = low
            left[t] = (seen_ref[t].astype(F32) * direction).astype(BF16)
        multiply(left, copies, held, total)
        for t in range(count):
            out_ref[t, :part] = total[t].astype(BF16)

    shapes = [jax.ShapeDtypeStruct((count, 3 * part, cols), BF16)]
    return cross_call(
        body,
        [core, factors, seen, right, image],
        strips,
        shapes,
        [pltpu.VMEM(right.shape, BF16)],
    )[0]


def links_of(first, rows, row_length, total_rows):
    position = (first - 1 + lax.iota(jnp.int32, rows + 1))[:, None]
    length = row_length.astype(F32)
    later = (position + 1).astype(F32)
    whole_rows = jnp.floor((later + 0.5) / length) * length
    keep = (position >= 0) & (position + 1 < total_rows) & (later != whole_rows)
    return keep.astype(F32)


def field_of(cells, above, below, links, coef):
    padded = jnp.concatenate([above, cells, below], axis=-2)
    flux = links * (padded[..., 1:, :] - padded[..., :-1, :])
    return cells - coef * (flux[..., 1:, :] - flux[..., :-1, :])


def on_device(right_side, observed, row_length, field_coef, kernel_geno, kernel_trial):
    count = lax.axis_size("trial")
    rows, cols = observed.shape
    part = rows // count
    genos = lax.axis_size("geno")
    total_rows = rows * genos
    geno, trial = lax.axis_index("geno"), lax.axis_index("trial")
    right = right_side[:, 0, :]
    seen = observed.astype(F32)

    core = (geno % CORES).astype(jnp.int32)[None]
    pieces, order = gather_geno((seen * right).astype(BF16), True)
    slabs, strips = pack(
        core, trial[None], right, observed, field_coef[None], row_length[None], kernel_trial
    )
    slabs, strips, pieces[2] = lax.optimization_barrier((slabs, strips, pieces[2]))
    strips = swap(strips)
    strips = [strips, hop(strips, core=1)]
    slabs = swap(slabs)
    mixed = mix(kernel_geno, pieces, order, BF16)

    right_r = slabs[:, :part].astype(F32) + slabs[:, part : 2 * part].astype(F32)
    seen_r = slabs[:, 2 * part : 3 * part]
    extra = slabs[:, 3 * part :].astype(F32)
    coef_r = extra[:, 0:1] + extra[:, 1:2] + extra[:, 2:3]
    length_r = extra[:, 3:4]
    devices = count * genos
    above = lax.ppermute(right_r[:, -1:], BOTH, [(i, i + 1) for i in range(devices - 1)])
    below = lax.ppermute(right_r[:, :1], BOTH, [(i + 1, i) for i in range(devices - 1)])
    links_r = links_of(geno * rows + trial * part, part, length_r, total_rows)
    field_r = field_of(right_r, above, below, links_r, coef_r)

    mixed_r = swap(mixed.reshape(count, part, cols))
    image_r, sums = cross_first(core, mixed_r, seen_r, field_r, right_r, strips)
    sums = totals(sums)
    rr, ri, ii = sums[0], sums[1], sums[2]
    alpha = rr / ri
    new = rr - 2.0 * alpha * ri + alpha * alpha * ii
    beta = new / rr

    factors = jnp.stack([alpha, beta])
    turned = swap(cross_second(core, factors, seen_r, right_r, image_r, strips))
    pieces, order = gather_geno(turned[:, :part].reshape(rows, cols), False)
    crossed = mix(kernel_geno, pieces, order, F32)
    image = turned[:, part : 2 * part].astype(F32) + turned[:, 2 * part :].astype(F32)
    image = image.reshape(rows, cols)
    residual = right - alpha * image
    direction = residual + beta * right
    above = lax.ppermute(direction[-1:], "geno", [(i, i + 1) for i in range(genos - 1)])
    below = lax.ppermute(direction[:1], "geno", [(i + 1, i) for i in range(genos - 1)])
    links = links_of(geno * rows, rows, row_length[None], total_rows)
    field = field_of(direction, above, below, links, field_coef[None])
    image = seen * crossed + field
    product = jnp.zeros((1, 128), F32).at[0, 0].set(jnp.sum(direction * image))
    product = totals(product)[0]
    step = new / product
    solution_field = alpha * right + step * direction
    residual = residual - step * image
    return solution_field[:, None, :], residual[:, None, :]


def solution(mesh):
    return jax.shard_map(
        on_device,
        mesh=mesh,
        in_specs=(
            P("geno", None, "trial"),
            P("geno", "trial"),
            P("trial"),
            P("trial"),
            P("geno", None),
            P("trial", None),
        ),
        out_specs=(P("geno", None, "trial"), P("geno", None, "trial")),
        check_vma=False,
    )
```

time: 659 us -> 256 us (0.39)
  waiting for transfers between devices: 373 us -> 46.8 us
  blocking collectives: 192 us -> 49 us
  starting transfers between devices: 11.3 us -> 73.6 us
  Pallas kernels: 0 us -> 36.5 us
  matrix products: 33.3 us -> 0 us
  local copies, waits for them, and re-layouts: 3.46 us -> 26 us
  between operations: 17.9 us -> 6.1 us
  other arithmetic: 26.9 us -> 17 us
    reduce_scatter x2 -> x0, waiting for transfers between devices: 278 us -> none  [on_device(): lax.psum_scatter(jnp.einsum('jc,jx->cx', kernel_geno, flat, preferred_ele...]
    psum x3 -> x0, blocking collectives: 192 us -> none  [the longest x2 127 us: squares(): return lax.psum(jnp.sum(vector * vector, axis=(0, 2)), ('geno', 'trial'))]
    all_gather x2 -> x0, waiting for transfers between devices: 94.6 us -> none  [on_device(): lax.all_gather(mixed, 'trial', axis=2, tiled=True)]
    all_to_all x0 -> x3, blocking collectives: none -> 49 us  [the longest x2 28.9 us: totals(): return jnp.sum(lax.all_to_all(copies, BOTH, 0, 0, tiled=True), axis=(0, 1))]
    ppermute x4 -> x35, starting transfers between devices: 11.1 us -> 56 us  [the longest x31 40.2 us: hop(): return lax.ppermute(cells, BOTH, pairs)]
    ppermute x4 -> x35, waiting for transfers between devices: 0.7 us -> 37.3 us  [the longest x31 33.5 us: hop(): return lax.ppermute(cells, BOTH, pairs)]
    pallas_call x0 -> x5, Pallas kernels: none -> 36.5 us  [the longest x2 25.6 us: mix(): pl.pallas_call(body, out_shape=jax.ShapeDtypeStruct((rows, cols), kind),...]
    dot_general x4 -> x0, matrix products: 33.3 us -> none  [the longest x2 24.1 us: on_device(): jnp.einsum('jc,jx->cx', kernel_geno, flat, preferred_element_type=jnp.flo...]
  transfers between devices with their start and end apart: 8 -> 38, of which waited for: 5 -> 12; matrix products, arithmetic and copies ran while one was open for 3% -> 4% of each run, Pallas kernels for 0% -> 5%
where the time goes in v1:
time: 256 us; the launch traced here: 255 us
  starting transfers between devices  73.6 us (29%)
  blocking collectives  49 us (19%)
  waiting for transfers between devices  46.8 us (18%)
  Pallas kernels  36.5 us (14%)
  local copies, waits for them, and re-layouts  26 us (10%)
  other arithmetic  17 us (7%)
  between operations  6.1 us (2%)
    ppermute x31, starting transfers between devices, hop(): return lax.ppermute(cells, BOTH, pairs)  40.2 us
    ppermute x31, waiting for transfers between devices, hop(): return lax.ppermute(cells, BOTH, pairs)  33.5 us
    all_to_all x2, blocking collectives, totals(): return jnp.sum(lax.all_to_all(copies, BOTH, 0, 0, tiled=True), axis=(0, 1))  28.9 us
    pallas_call x2, Pallas kernels, mix(): pl.pallas_call(body, out_shape=jax.ShapeDtypeStruct((rows, cols), kind),...  25.6 us
    unnamed x80, local copies, waits for them, and re-layouts  23.4 us
    all_to_all x1, blocking collectives, swap(): lax.all_to_all(slabs, 'trial', split_axis=0, concat_axis=0, tiled=True)  20.1 us
    all_to_all x3, starting transfers between devices, swap(): lax.all_to_all(slabs, 'trial', split_axis=0, concat_axis=0, tiled=True)  17.6 us
    pallas_call x2, Pallas kernels, cross_call(): pl.pallas_call(body, out_shape=shapes, in_specs=[SMEM if x.ndim == 1 else...  10.6 us
  transfers between devices with their start and end apart: 38, of which 12 were waited for; matrix products, arithmetic and copies ran while one was open for 4% of the time, Pallas kernels for 5%

profile of v1, /device:TPU:1, one launch (start us, length us, event | category | flops | bytes accessed | tf_op | source)
XLA Modules:
  0.0 254.9 jit_solution(16427874083459187803)
XLA Ops:
  0.6 1.6 multiply_convert_fusion.refs_0_
  2.2 2.5 collective-permute-start.1
  4.8 1.2 copy.33
  6.4 1.5 copy-done.5
  7.8 5.8 %collective-permute-done.1.refs_2_ = bf16[768,256]{1,0:T(8,128)(2,1)S(1)} collective-permute-done((bf16[768,256]{1,0:T(8,128)(2,1)S(1)}, bf16[768,256]{1,0:T(8,128)(2,1)S(1)}, u32[]{:S(2)}, u32[]{:S(2)}) %collective-permute-start.1) | collective-permute-done | bytes 393248 | tf_op jit(solution)/shard_map/ppermute | solution.py:29
  13.6 6.9 %all-to-all-start.2 = ((bf16[8,5,128,256]{3,2,1,0:T(8,128)(2,1)}), bf16[8,5,128,256]{3,2,1,0:T(8,128)(2,1)S(1)}, u32[]{:S(2)}, u32[]{:S(2)}) async-start(bf16[8,5,128,256]{3,2,1,0:T(8,128)(2,1)} %copy-done.5), calls=%async_computation.2 | async-start | bytes 5242880 | tf_op jit(solution)/shard_map/all_to_all | solution.py:115
  20.5 1.3 collective-permute-start.3
  21.8 1.5 collective-permute-start.5
  23.3 2.3 collective-permute-start
  25.5 1.7 collective-permute-start.11
  27.5 3.1 %collective-permute-done.3.refs_4_ = bf16[768,256]{1,0:T(8,128)(2,1)S(1)} collective-permute-done((bf16[768,256]{1,0:T(8,128)(2,1)S(1)}, bf16[768,256]{1,0:T(8,128)(2,1)S(1)}, u32[]{:S(2)}, u32[]{:S(2)}) %collective-permute-start.3) | collective-permute-done | bytes 393248 | tf_op jit(solution)/shard_map/ppermute | solution.py:29
  30.6 3.9 %collective-permute-start.4 = (bf16[768,256]{1,0:T(8,128)(2,1)S(1)}, bf16[768,256]{1,0:T(8,128)(2,1)S(1)}, u32[]{:S(2)}, u32[]{:S(2)}) collective-permute-start(bf16[768,256]{1,0:T(8,128)(2,1)S(1)} %collective-permute-done.3.refs_4_), channel_id=1, source_target_pairs={{0,8},{1,9},{2,10},{3,11},{4,12},{5,13},{6,14},{7,15},{8,0},{9,1},... | collective-permute-start | bytes 1179656 | tf_op jit(solution)/shard_map/ppermute | solution.py:29
  34.4 0.8 copy-done.10
  35.2 5.9 %collective-permute-start.6 = (bf16[768,256]{1,0:T(8,128)(2,1)}, bf16[768,256]{1,0:T(8,128)(2,1)}, u32[]{:S(2)}, u32[]{:S(2)}) collective-permute-start(bf16[768,256]{1,0:T(8,128)(2,1)} %collective-permute-done.5.refs_6_), channel_id=1, source_target_pairs={{0,8},{1,9},{2,10},{3,11},{4,12},{5,13},{6,14},{7,15},{8,0},{9,1},... | collective-permute-start | bytes 1179656 | tf_op jit(solution)/shard_map/ppermute | solution.py:29
  41.8 3.6 %collective-permute-start.9 = (bf16[768,256]{1,0:T(8,128)(2,1)S(1)}, bf16[768,256]{1,0:T(8,128)(2,1)}, u32[]{:S(2)}, u32[]{:S(2)}) collective-permute-start(bf16[768,256]{1,0:T(8,128)(2,1)S(1)} %collective-permute-done.1.refs_2_), channel_id=1, source_target_pairs={{0,96},{1,97},{2,98},{3,99},{4,100},{5,101},{6,102},{7,103},{8,104... | collective-permute-start | bytes 1179656 | tf_op jit(solution)/shard_map/ppermute | solution.py:29
  46.1 1.2 collective-permute-start.13
  47.3 0.8 copy-done.18
  48.1 9.4 %all-to-all-done.2.refs_0_ = bf16[8,5,128,256]{3,2,1,0:T(8,128)(2,1)S(1)} async-done(((bf16[8,5,128,256]{3,2,1,0:T(8,128)(2,1)}), bf16[8,5,128,256]{3,2,1,0:T(8,128)(2,1)S(1)}, u32[]{:S(2)}, u32[]{:S(2)}) %all-to-all-start.2) | async-done | bytes 2621472 | tf_op jit(solution)/shard_map/all_to_all | solution.py:115
  57.5 2.0 collective-permute-start.17
  59.5 4.3 %all-to-all-start.1 = ((bf16[8,304,256]{2,1,0:T(8,128)(2,1)}), bf16[8,304,256]{2,1,0:T(8,128)(2,1)}, u32[]{:S(2)}, u32[]{:S(2)}) async-start(bf16[8,304,256]{2,1,0:T(8,128)(2,1)} %copy-done.6), calls=%async_computation.1 | async-start | bytes 2490368 | tf_op jit(solution)/shard_map/all_to_all | solution.py:115
  67.6 1.0 copy-done.11
  68.6 1.0 copy-done.13
  69.6 1.0 copy-done.15
  70.6 1.0 copy-done.17
  71.6 1.0 copy-done.19
  72.6 13.3 %shard_map.78 = bf16[768,256]{1,0:T(8,128)(2,1)} custom-call(s32[16]{0:T(128)S(1)} %stack.93.order_ref, bf16[768,12288]{1,0:T(8,128)(2,1)} %kernel_ref.5, bf16[768,256]{1,0:T(8,128)(2,1)S(1)} %multiply_convert_fusion.refs_0_, bf16[768,256]{1,0:T(8,128)(2,1)S(1)} %copy-done.13, bf16[768,256]{1,0:T(8,128)(2,1)S(1)} %collective-permute-done.1.refs_2_, ...), custom_call_target="tpu_custom_call" | custom-call | flops 4831838208 | bytes 25165824 | tf_op jit(solution)/shard_map/pallas_call | solution.py:143
  85.9 6.5 %all-to-all-start = ((bf16[8,96,256]{2,1,0:T(8,128)(2,1)}), bf16[8,96,256]{2,1,0:T(8,128)(2,1)}, u32[]{:S(2)}, u32[]{:S(2)}) async-start(bf16[8,96,256]{2,1,0:T(8,128)(2,1)} %bitcast.20), calls=%async_computation | async-start | bytes 786432 | tf_op jit(solution)/shard_map/all_to_all | solution.py:115
  92.4 1.2 convert_add_fusion.right_ref
  93.6 7.7 %collective-permute-start.15 = (f32[8,1,256]{2,1,0:T(1,128)S(1)}, f32[8,1,256]{2,1,0:T(1,128)S(1)}, u32[]{:S(2)}, u32[]{:S(2)}) collective-permute-start(f32[8,1,256]{2,1,0:T(1,128)S(1)} %get-tuple-element.39), channel_id=1, source_target_pairs={{1,0},{2,1},{3,2},{4,3},{5,4},{6,5},{7,6},{8,7},{9,8},{10,9},{11,1... | collective-permute-start | bytes 24584 | tf_op jit(solution)/shard_map/ppermute | solution.py:304
  101.3 2.1 collective-permute-start.16
  103.4 0.9 slice_convert_fusion
  104.3 1.8 slice.116.seen_ref
  106.1 3.8 %collective-permute-done.16 = f32[8,1,256]{2,1,0:T(1,128)S(1)} collective-permute-done((f32[8,1,256]{2,1,0:T(1,128)S(1)}, f32[8,1,256]{2,1,0:T(1,128)S(1)}, u32[]{:S(2)}, u32[]{:S(2)}) %collective-permute-start.16) | collective-permute-done | bytes 8224 | tf_op jit(solution)/shard_map/ppermute | solution.py:303
  110.3 2.2 fusion.12.field_ref
  112.6 1.0 copy-done.2
  113.6 1.1 copy-done.4
  114.7 5.6 %shard_map.79 = (f32[8,96,256]{2,1,0:T(8,128)S(1)}, f32[1,128]{1,0:T(1,128)S(1)}) custom-call(s32[1]{0:T(128)} %bitcast.core_ref, bf16[8,96,256]{2,1,0:T(8,128)(2,1)} %all-to-all-done.mixed_ref, bf16[8,96,256]{2,1,0:T(8,128)(2,1)S(1)} %copy-done.2, f32[8,96,256]{2,1,0:T(8,128)S(1)} %copy-done.4, f32[8,96,256]{2,1,0:T(8,128)S(1)} %convert_add_fusion.right_ref, ...), custom_call_target="tpu_custom_call" | custom-call | flops 805306368 | bytes 8388608 | tf_op jit(solution)/shard_map/pallas_call | solution.py:191
  120.3 0.9 copy-done.8
  121.2 15.4 %all_to_all.30 = f32[128,1,128]{2,1,0:T(1,128)S(1)} all-to-all(f32[128,1,128]{2,1,0:T(1,128)S(1)} %broadcast_in_dim.45), channel_id=1, replica_groups=mesh['geno'=16,'trial'=8] {'geno','trial'}, dimensions={0} | all-to-all | bytes 131072 | tf_op jit(solution)/shard_map/all_to_all | solution.py:121
  140.9 1.0 copy-done.3
  141.9 1.1 copy-done.9
  143.0 5.0 %shard_map.80 = bf16[8,288,256]{2,1,0:T(8,128)(2,1)S(1)} custom-call(s32[1]{0:T(128)} %bitcast.core_ref, f32[2]{0:T(128)S(1)} %pad_maximum_fusion.factor_ref, bf16[8,96,256]{2,1,0:T(8,128)(2,1)S(1)} %copy-done.3, f32[8,96,256]{2,1,0:T(8,128)S(1)} %convert_add_fusion.right_ref, f32[8,96,256]{2,1,0:T(8,128)S(1)} %copy-done.9, ...), custom_call_target="tpu_custom_call" | custom-call | flops 805306368 | bytes 8388608 | tf_op jit(solution)/shard_map/pallas_call | solution.py:191
  148.0 20.1 %all_to_all.31 = bf16[8,288,256]{2,1,0:T(8,128)(2,1)S(1)} all-to-all(bf16[8,288,256]{2,1,0:T(8,128)(2,1)S(1)} %shard_map.80), channel_id=1, replica_groups=mesh['geno'=16,'trial'=8] {'trial'}, dimensions={0} | all-to-all | bytes 2359296 | tf_op jit(solution)/shard_map/all_to_all | solution.py:115
  168.2 1.0 copy-done.32
  169.4 4.1 %collective-permute-start.33 = (f32[1,256]{1,0:T(1,128)S(1)}, f32[1,256]{1,0:T(1,128)S(1)}, u32[]{:S(2)}, u32[]{:S(2)}) collective-permute-start(f32[1,256]{1,0:T(1,128)S(1)} %get-tuple-element.37), channel_id=1, source_target_pairs={{8,0},{16,8},{24,16},{32,24},{40,32},{48,40},{56,48},{64,56},{72,6... | collective-permute-start | bytes 3080 | tf_op jit(solution)/shard_map/ppermute | solution.py:325
  173.5 1.9 collective-permute-start.34
  175.5 1.5 collective-permute-start.19
  177.2 2.4 collective-permute-start.23
  180.1 5.6 %collective-permute-done.19.refs_2_ = bf16[768,256]{1,0:T(8,128)(2,1)S(1)} collective-permute-done((bf16[768,256]{1,0:T(8,128)(2,1)S(1)}, bf16[768,256]{1,0:T(8,128)(2,1)S(1)}, u32[]{:S(2)}, u32[]{:S(2)}) %collective-permute-start.19) | collective-permute-done | bytes 393248 | tf_op jit(solution)/shard_map/ppermute | solution.py:29
  185.8 1.3 collective-permute-start.20
  187.1 10.4 %collective-permute-done.21.refs_4_ = bf16[768,256]{1,0:T(8,128)(2,1)S(1)} collective-permute-done((bf16[768,256]{1,0:T(8,128)(2,1)S(1)}, bf16[768,256]{1,0:T(8,128)(2,1)S(1)}, u32[]{:S(2)}, u32[]{:S(2)}) %collective-permute-start.21) | collective-permute-done | bytes 393248 | tf_op jit(solution)/shard_map/ppermute | solution.py:29
  199.4 2.7 %collective-permute-start.27 = (bf16[768,256]{1,0:T(8,128)(2,1)S(1)}, bf16[768,256]{1,0:T(8,128)(2,1)}, u32[]{:S(2)}, u32[]{:S(2)}) collective-permute-start(bf16[768,256]{1,0:T(8,128)(2,1)S(1)} %collective-permute-done.19.refs_2_), channel_id=1, source_target_pairs={{0,96},{1,97},{2,98},{3,99},{4,100},{5,101},{6,102},{7,103},{8,104... | collective-permute-start | bytes 1179656 | tf_op jit(solution)/shard_map/ppermute | solution.py:29
  203.2 0.9 collective-permute-start.30
  205.6 5.7 %collective-permute-done.25.refs_8_ = bf16[768,256]{1,0:T(8,128)(2,1)} collective-permute-done((bf16[768,256]{1,0:T(8,128)(2,1)S(1)}, bf16[768,256]{1,0:T(8,128)(2,1)}, u32[]{:S(2)}, u32[]{:S(2)}) %collective-permute-start.25) | collective-permute-done | bytes 393248 | tf_op jit(solution)/shard_map/ppermute | solution.py:29
  211.3 0.9 collective-permute-start.26
  212.9 1.6 collective-permute-start.32
  215.2 1.8 fusion.6
  217.1 1.0 copy-done.29
  218.1 12.3 %shard_map.81 = f32[768,256]{1,0:T(8,128)S(1)} custom-call(s32[16]{0:T(128)S(1)} %stack.93.order_ref, bf16[768,12288]{1,0:T(8,128)(2,1)} %kernel_ref.5, bf16[768,256]{1,0:T(8,128)(2,1)S(1)} %bitcast.63, bf16[768,256]{1,0:T(8,128)(2,1)S(1)} %copy-done.25, bf16[768,256]{1,0:T(8,128)(2,1)S(1)} %copy-done.21, bf16[768,256]{1,0:T(8,128)(2,1)} %collective-permute-done.20.refs_3_, ...), custom_call_target="tpu_custom_call" | custom-call | flops 4831838208 | bytes 25165824 | tf_op jit(solution)/shard_map/pallas_call | solution.py:143
  230.4 1.8 multiply_reduce_fusion
  233.6 13.5 %all_to_all.32 = f32[128,1,128]{2,1,0:T(1,128)S(1)} all-to-all(f32[128,1,128]{2,1,0:T(1,128)S(1)} %broadcast_in_dim.47), channel_id=1, replica_groups=mesh['geno'=16,'trial'=8] {'geno','trial'}, dimensions={0} | all-to-all | bytes 131072 | tf_op jit(solution)/shard_map/all_to_all | solution.py:121
  247.2 4.7 %multiply_add_fusion = f32[768,1,256]{2,1,0:T(1,128)} fusion(f32[768,1,256]{2,1,0:T(1,128)S(1)} %copy-done.33, f32[768,1,256]{2,0,1:T(8,128)S(1)} %bitcast.67, f32[]{:T(128)} %div.65, f32[]{:T(128)S(6)} %div.69, f32[]{:T(128)} %div.64), kind=kLoop, calls=%fused_computation.24 | loop fusion | flops 1179648 | bytes 2359308 | tf_op jit(solution)/shard_map/add | solution.py:332
  251.9 1.3 subtract_bitcast_fusion
  253.3 1.7 copy.15
  (132 shorter events, 14.1 us)
Async XLA Ops:
  0.6 5.4 %copy-start.7 = (bf16[256,2048]{1,0:T(8,128)(2,1)S(1)}, bf16[256,2048]{1,0:T(8,128)(2,1)}, u32[]{:S(2)}) copy-start(bf16[256,2048]{1,0:T(8,128)(2,1)} %kernel_ref.3) | copy-start | bytes 3145732
  2.2 3.8 %copy-start = (s32[768,256]{1,0:T(8,128)S(1)}, s32[768,256]{1,0:T(8,128)}, u32[]{:S(2)}) copy-start(s32[768,256]{1,0:T(8,128)} %seen_ref.1) | copy-start | bytes 2359300
  2.2 3.8 %copy-start.30 = (s32[256]{0:T(256)S(1)}, s32[256]{0:T(256)}, u32[]{:S(2)}) copy-start(s32[256]{0:T(256)} %param.10) | copy-start | bytes 3076
  2.2 3.8 %copy-start.31 = (f32[256]{0:T(256)S(1)}, f32[256]{0:T(256)}, u32[]{:S(2)}) copy-start(f32[256]{0:T(256)} %param.11) | copy-start | bytes 3076
  2.2 11.4 %collective-permute-start.1 = (bf16[768,256]{1,0:T(8,128)(2,1)S(1)}, bf16[768,256]{1,0:T(8,128)(2,1)S(1)}, u32[]{:S(2)}, u32[]{:S(2)}) collective-permute-start(bf16[768,256]{1,0:T(8,128)(2,1)S(1)} %multiply_convert_fusion.refs_0_), channel_id=1, source_target_pairs={{0,16},{1,17},{2,18},{3,19},{4,20},{5,21},{6,22},{7,23},{8,24},{9,... | collective-permute-start | bytes 1179656 | tf_op jit(solution)/shard_map/ppermute | solution.py:29
  6.4 1.5 copy-start.5
  7.8 5.8 %copy-start.6 = (bf16[8,304,256]{2,1,0:T(8,128)(2,1)}, bf16[8,304,256]{2,1,0:T(8,128)(2,1)S(1)}, u32[]{:S(2)}) copy-start(bf16[8,304,256]{2,1,0:T(8,128)(2,1)S(1)} %get-tuple-element.24) | copy-start | bytes 3735556
  13.6 43.9 %all-to-all-start.2 = ((bf16[8,5,128,256]{3,2,1,0:T(8,128)(2,1)}), bf16[8,5,128,256]{3,2,1,0:T(8,128)(2,1)S(1)}, u32[]{:S(2)}, u32[]{:S(2)}) async-start(bf16[8,5,128,256]{3,2,1,0:T(8,128)(2,1)} %copy-done.5), calls=%async_computation.2 | async-start | bytes 5242880 | tf_op jit(solution)/shard_map/all_to_all | solution.py:115
  20.5 10.1 %collective-permute-start.3 = (bf16[768,256]{1,0:T(8,128)(2,1)S(1)}, bf16[768,256]{1,0:T(8,128)(2,1)S(1)}, u32[]{:S(2)}, u32[]{:S(2)}) collective-permute-start(bf16[768,256]{1,0:T(8,128)(2,1)S(1)} %multiply_convert_fusion.refs_0_), channel_id=1, source_target_pairs={{0,32},{1,33},{2,34},{3,35},{4,36},{5,37},{6,38},{7,39},{8,40},{9,... | collective-permute-start | bytes 1179656 | tf_op jit(solution)/shard_map/ppermute | solution.py:29
  21.8 13.5 %collective-permute-start.5 = (bf16[768,256]{1,0:T(8,128)(2,1)S(1)}, bf16[768,256]{1,0:T(8,128)(2,1)}, u32[]{:S(2)}, u32[]{:S(2)}) collective-permute-start(bf16[768,256]{1,0:T(8,128)(2,1)S(1)} %multiply_convert_fusion.refs_0_), channel_id=1, source_target_pairs={{0,96},{1,97},{2,98},{3,99},{4,100},{5,101},{6,102},{7,103},{8,104... | collective-permute-start | bytes 1179656 | tf_op jit(solution)/shard_map/ppermute | solution.py:29
  23.3 17.8 %collective-permute-start = (bf16[768,256]{1,0:T(8,128)(2,1)S(1)}, bf16[768,256]{1,0:T(8,128)(2,1)S(1)}, u32[]{:S(2)}, u32[]{:S(2)}) collective-permute-start(bf16[768,256]{1,0:T(8,128)(2,1)S(1)} %multiply_convert_fusion.refs_0_), channel_id=1, source_target_pairs={{0,8},{1,9},{2,10},{3,11},{4,12},{5,13},{6,14},{7,15},{8,0},{9,1},... | collective-permute-start | bytes 1179656 | tf_op jit(solution)/shard_map/ppermute | solution.py:29
  25.5 16.3 %collective-permute-start.11 = (bf16[768,256]{1,0:T(8,128)(2,1)S(1)}, bf16[768,256]{1,0:T(8,128)(2,1)S(1)}, u32[]{:S(2)}, u32[]{:S(2)}) collective-permute-start(bf16[768,256]{1,0:T(8,128)(2,1)S(1)} %multiply_convert_fusion.refs_0_), channel_id=1, source_target_pairs={{0,64},{1,65},{2,66},{3,67},{4,68},{5,69},{6,70},{7,71},{8,72},{9,... | collective-permute-start | bytes 1179656 | tf_op jit(solution)/shard_map/ppermute | solution.py:29
  27.2 18.1 %collective-permute-start.2 = (bf16[768,256]{1,0:T(8,128)(2,1)S(1)}, bf16[768,256]{1,0:T(8,128)(2,1)S(1)}, u32[]{:S(2)}, u32[]{:S(2)}) collective-permute-start(bf16[768,256]{1,0:T(8,128)(2,1)S(1)} %collective-permute-done.1.refs_2_), channel_id=1, source_target_pairs={{0,8},{1,9},{2,10},{3,11},{4,12},{5,13},{6,14},{7,15},{8,0},{9,1},... | collective-permute-start | bytes 1179656 | tf_op jit(solution)/shard_map/ppermute | solution.py:29
  30.6 16.7 %collective-permute-start.4 = (bf16[768,256]{1,0:T(8,128)(2,1)S(1)}, bf16[768,256]{1,0:T(8,128)(2,1)S(1)}, u32[]{:S(2)}, u32[]{:S(2)}) collective-permute-start(bf16[768,256]{1,0:T(8,128)(2,1)S(1)} %collective-permute-done.3.refs_4_), channel_id=1, source_target_pairs={{0,8},{1,9},{2,10},{3,11},{4,12},{5,13},{6,14},{7,15},{8,0},{9,1},... | collective-permute-start | bytes 1179656 | tf_op jit(solution)/shard_map/ppermute | solution.py:29
  35.2 28.5 %collective-permute-start.6 = (bf16[768,256]{1,0:T(8,128)(2,1)}, bf16[768,256]{1,0:T(8,128)(2,1)}, u32[]{:S(2)}, u32[]{:S(2)}) collective-permute-start(bf16[768,256]{1,0:T(8,128)(2,1)} %collective-permute-done.5.refs_6_), channel_id=1, source_target_pairs={{0,8},{1,9},{2,10},{3,11},{4,12},{5,13},{6,14},{7,15},{8,0},{9,1},... | collective-permute-start | bytes 1179656 | tf_op jit(solution)/shard_map/ppermute | solution.py:29
  41.8 22.0 %collective-permute-start.7 = (bf16[768,256]{1,0:T(8,128)(2,1)S(1)}, bf16[768,256]{1,0:T(8,128)(2,1)}, u32[]{:S(2)}, u32[]{:S(2)}) collective-permute-start(bf16[768,256]{1,0:T(8,128)(2,1)S(1)} %collective-permute-done.1.refs_2_), channel_id=1, source_target_pairs={{0,32},{1,33},{2,34},{3,35},{4,36},{5,37},{6,38},{7,39},{8,40},{9,... | collective-permute-start | bytes 1179656 | tf_op jit(solution)/shard_map/ppermute | solution.py:29
  41.8 5.5 %copy-start.14 = (bf16[768,256]{1,0:T(8,128)(2,1)}, bf16[768,256]{1,0:T(8,128)(2,1)S(1)}, u32[]{:S(2)}) copy-start(bf16[768,256]{1,0:T(8,128)(2,1)S(1)} %collective-permute-done.11.refs_12_) | copy-start | bytes 1179652
  41.8 22.5 %collective-permute-start.9 = (bf16[768,256]{1,0:T(8,128)(2,1)S(1)}, bf16[768,256]{1,0:T(8,128)(2,1)}, u32[]{:S(2)}, u32[]{:S(2)}) collective-permute-start(bf16[768,256]{1,0:T(8,128)(2,1)S(1)} %collective-permute-done.1.refs_2_), channel_id=1, source_target_pairs={{0,96},{1,97},{2,98},{3,99},{4,100},{5,101},{6,102},{7,103},{8,104... | collective-permute-start | bytes 1179656 | tf_op jit(solution)/shard_map/ppermute | solution.py:29
  46.1 18.3 %collective-permute-start.13 = (bf16[768,256]{1,0:T(8,128)(2,1)S(1)}, bf16[768,256]{1,0:T(8,128)(2,1)}, u32[]{:S(2)}, u32[]{:S(2)}) collective-permute-start(bf16[768,256]{1,0:T(8,128)(2,1)S(1)} %collective-permute-done.1.refs_2_), channel_id=1, source_target_pairs={{0,64},{1,65},{2,66},{3,67},{4,68},{5,69},{6,70},{7,71},{8,72},{9,... | collective-permute-start | bytes 1179656 | tf_op jit(solution)/shard_map/ppermute | solution.py:29
  57.5 55.0 %collective-permute-start.17 = (bf16[8,5,128,256]{3,2,1,0:T(8,128)(2,1)S(1)}, bf16[8,5,128,256]{3,2,1,0:T(8,128)(2,1)}, u32[]{:S(2)}, u32[]{:S(2)}) collective-permute-start(bf16[8,5,128,256]{3,2,1,0:T(8,128)(2,1)S(1)} %all-to-all-done.2.refs_0_), channel_id=1, source_target_pairs={{0,8},{1,9},{2,10},{3,11},{4,12},{5,13},{6,14},{7,15},{8,0},{9,1},... | collective-permute-start | bytes 7864328 | tf_op jit(solution)/shard_map/ppermute | solution.py:29
  59.5 26.5 %all-to-all-start.1 = ((bf16[8,304,256]{2,1,0:T(8,128)(2,1)}), bf16[8,304,256]{2,1,0:T(8,128)(2,1)}, u32[]{:S(2)}, u32[]{:S(2)}) async-start(bf16[8,304,256]{2,1,0:T(8,128)(2,1)} %copy-done.6), calls=%async_computation.1 | async-start | bytes 2490368 | tf_op jit(solution)/shard_map/all_to_all | solution.py:115
  63.8 2.1 collective-permute-start.12
  63.9 2.6 %collective-permute-start.8 = (bf16[768,256]{1,0:T(8,128)(2,1)}, bf16[768,256]{1,0:T(8,128)(2,1)}, u32[]{:S(2)}, u32[]{:S(2)}) collective-permute-start(bf16[768,256]{1,0:T(8,128)(2,1)} %collective-permute-done.7.refs_8_), channel_id=1, source_target_pairs={{0,8},{1,9},{2,10},{3,11},{4,12},{5,13},{6,14},{7,15},{8,0},{9,1},... | collective-permute-start | bytes 1179656 | tf_op jit(solution)/shard_map/ppermute | solution.py:29
  64.4 2.7 %collective-permute-start.10 = (bf16[768,256]{1,0:T(8,128)(2,1)}, bf16[768,256]{1,0:T(8,128)(2,1)}, u32[]{:S(2)}, u32[]{:S(2)}) collective-permute-start(bf16[768,256]{1,0:T(8,128)(2,1)} %collective-permute-done.9.refs_10_), channel_id=1, source_target_pairs={{0,8},{1,9},{2,10},{3,11},{4,12},{5,13},{6,14},{7,15},{8,0},{9,1},... | collective-permute-start | bytes 1179656 | tf_op jit(solution)/shard_map/ppermute | solution.py:29
  64.5 3.1 %collective-permute-start.14 = (bf16[768,256]{1,0:T(8,128)(2,1)}, bf16[768,256]{1,0:T(8,128)(2,1)}, u32[]{:S(2)}, u32[]{:S(2)}) collective-permute-start(bf16[768,256]{1,0:T(8,128)(2,1)} %collective-permute-done.13.refs_14_), channel_id=1, source_target_pairs={{0,8},{1,9},{2,10},{3,11},{4,12},{5,13},{6,14},{7,15},{8,0},{9,1},... | collective-permute-start | bytes 1179656 | tf_op jit(solution)/shard_map/ppermute | solution.py:29
  67.6 1.0 copy-start.11
  68.6 1.0 copy-start.13
  69.6 1.0 copy-start.15
  85.9 26.6 %all-to-all-start = ((bf16[8,96,256]{2,1,0:T(8,128)(2,1)}), bf16[8,96,256]{2,1,0:T(8,128)(2,1)}, u32[]{:S(2)}, u32[]{:S(2)}) async-start(bf16[8,96,256]{2,1,0:T(8,128)(2,1)} %bitcast.20), calls=%async_computation | async-start | bytes 786432 | tf_op jit(solution)/shard_map/all_to_all | solution.py:115
  93.6 12.5 %collective-permute-start.15 = (f32[8,1,256]{2,1,0:T(1,128)S(1)}, f32[8,1,256]{2,1,0:T(1,128)S(1)}, u32[]{:S(2)}, u32[]{:S(2)}) collective-permute-start(f32[8,1,256]{2,1,0:T(1,128)S(1)} %get-tuple-element.39), channel_id=1, source_target_pairs={{1,0},{2,1},{3,2},{4,3},{5,4},{6,5},{7,6},{8,7},{9,8},{10,9},{11,1... | collective-permute-start | bytes 24584 | tf_op jit(solution)/shard_map/ppermute | solution.py:304
  101.3 8.6 %collective-permute-start.16 = (f32[8,1,256]{2,1,0:T(1,128)S(1)}, f32[8,1,256]{2,1,0:T(1,128)S(1)}, u32[]{:S(2)}, u32[]{:S(2)}) collective-permute-start(f32[8,1,256]{2,1,0:T(1,128)S(1)} %get-tuple-element.38), channel_id=1, source_target_pairs={{0,1},{1,2},{2,3},{3,4},{4,5},{5,6},{6,7},{7,8},{8,9},{9,10},{10,1... | collective-permute-start | bytes 24584 | tf_op jit(solution)/shard_map/ppermute | solution.py:303
  112.6 1.0 copy-start.2
  113.6 1.1 copy-start.4
  140.9 1.0 copy-start.3
  141.9 1.1 copy-start.9
  168.1 1.1 copy-start.32
  169.3 6.2 %copy-start.34 = (f32[8,96,256]{2,1,0:T(8,128)}, f32[8,96,256]{2,1,0:T(8,128)S(1)}, u32[]{:S(2)}) copy-start(f32[8,96,256]{2,1,0:T(8,128)S(1)} %add_multiply_fusion) | copy-start | bytes 2359300
  169.4 6.1 %copy-start.36 = (f32[768,256]{1,0:T(8,128)}, f32[768,256]{1,0:T(8,128)S(1)}, u32[]{:S(2)}) copy-start(f32[768,256]{1,0:T(8,128)S(1)} %multiply_add_fusion.1) | copy-start | bytes 2359300
  169.4 7.8 %collective-permute-start.33 = (f32[1,256]{1,0:T(1,128)S(1)}, f32[1,256]{1,0:T(1,128)S(1)}, u32[]{:S(2)}, u32[]{:S(2)}) collective-permute-start(f32[1,256]{1,0:T(1,128)S(1)} %get-tuple-element.37), channel_id=1, source_target_pairs={{8,0},{16,8},{24,16},{32,24},{40,32},{48,40},{56,48},{64,56},{72,6... | collective-permute-start | bytes 3080 | tf_op jit(solution)/shard_map/ppermute | solution.py:325
  173.5 6.2 %collective-permute-start.34 = (f32[1,256]{1,0:T(1,128)S(1)}, f32[1,256]{1,0:T(1,128)S(1)}, u32[]{:S(2)}, u32[]{:S(2)}) collective-permute-start(f32[1,256]{1,0:T(1,128)S(1)} %get-tuple-element.36), channel_id=1, source_target_pairs={{0,8},{8,16},{16,24},{24,32},{32,40},{40,48},{48,56},{56,64},{64,7... | collective-permute-start | bytes 3080 | tf_op jit(solution)/shard_map/ppermute | solution.py:324
  175.5 10.3 %collective-permute-start.19 = (bf16[768,256]{1,0:T(8,128)(2,1)S(1)}, bf16[768,256]{1,0:T(8,128)(2,1)S(1)}, u32[]{:S(2)}, u32[]{:S(2)}) collective-permute-start(bf16[768,256]{1,0:T(8,128)(2,1)S(1)} %bitcast.58), channel_id=1, source_target_pairs={{0,16},{1,17},{2,18},{3,19},{4,20},{5,21},{6,22},{7,23},{8,24},{9,... | collective-permute-start | bytes 1179656 | tf_op jit(solution)/shard_map/ppermute | solution.py:29
  177.0 20.5 %collective-permute-start.21 = (bf16[768,256]{1,0:T(8,128)(2,1)S(1)}, bf16[768,256]{1,0:T(8,128)(2,1)S(1)}, u32[]{:S(2)}, u32[]{:S(2)}) collective-permute-start(bf16[768,256]{1,0:T(8,128)(2,1)S(1)} %bitcast.59), channel_id=1, source_target_pairs={{0,32},{1,33},{2,34},{3,35},{4,36},{5,37},{6,38},{7,39},{8,40},{9,... | collective-permute-start | bytes 1179656 | tf_op jit(solution)/shard_map/ppermute | solution.py:29
  177.2 21.4 %collective-permute-start.18 = (bf16[768,256]{1,0:T(8,128)(2,1)S(1)}, bf16[768,256]{1,0:T(8,128)(2,1)S(1)}, u32[]{:S(2)}, u32[]{:S(2)}) collective-permute-start(bf16[768,256]{1,0:T(8,128)(2,1)S(1)} %bitcast.60), channel_id=1, source_target_pairs={{0,8},{1,9},{2,10},{3,11},{4,12},{5,13},{6,14},{7,15},{8,0},{9,1},... | collective-permute-start | bytes 1179656 | tf_op jit(solution)/shard_map/ppermute | solution.py:29
  177.2 22.2 %collective-permute-start.23 = (bf16[768,256]{1,0:T(8,128)(2,1)S(1)}, bf16[768,256]{1,0:T(8,128)(2,1)S(1)}, u32[]{:S(2)}, u32[]{:S(2)}) collective-permute-start(bf16[768,256]{1,0:T(8,128)(2,1)S(1)} %bitcast.61), channel_id=1, source_target_pairs={{0,96},{1,97},{2,98},{3,99},{4,100},{5,101},{6,102},{7,103},{8,104... | collective-permute-start | bytes 1179656 | tf_op jit(solution)/shard_map/ppermute | solution.py:29
  179.7 23.1 %collective-permute-start.29 = (bf16[768,256]{1,0:T(8,128)(2,1)S(1)}, bf16[768,256]{1,0:T(8,128)(2,1)S(1)}, u32[]{:S(2)}, u32[]{:S(2)}) collective-permute-start(bf16[768,256]{1,0:T(8,128)(2,1)S(1)} %bitcast.62), channel_id=1, source_target_pairs={{0,64},{1,65},{2,66},{3,67},{4,68},{5,69},{6,70},{7,71},{8,72},{9,... | collective-permute-start | bytes 1179656 | tf_op jit(solution)/shard_map/ppermute | solution.py:29
  185.8 17.4 %collective-permute-start.20 = (bf16[768,256]{1,0:T(8,128)(2,1)S(1)}, bf16[768,256]{1,0:T(8,128)(2,1)}, u32[]{:S(2)}, u32[]{:S(2)}) collective-permute-start(bf16[768,256]{1,0:T(8,128)(2,1)S(1)} %collective-permute-done.19.refs_2_), channel_id=1, source_target_pairs={{0,8},{1,9},{2,10},{3,11},{4,12},{5,13},{6,14},{7,15},{8,0},{9,1},... | collective-permute-start | bytes 1179656 | tf_op jit(solution)/shard_map/ppermute | solution.py:29
  197.5 7.3 %collective-permute-start.22 = (bf16[768,256]{1,0:T(8,128)(2,1)S(1)}, bf16[768,256]{1,0:T(8,128)(2,1)}, u32[]{:S(2)}, u32[]{:S(2)}) collective-permute-start(bf16[768,256]{1,0:T(8,128)(2,1)S(1)} %collective-permute-done.21.refs_4_), channel_id=1, source_target_pairs={{0,8},{1,9},{2,10},{3,11},{4,12},{5,13},{6,14},{7,15},{8,0},{9,1},... | collective-permute-start | bytes 1179656 | tf_op jit(solution)/shard_map/ppermute | solution.py:29
  199.4 11.9 %collective-permute-start.25 = (bf16[768,256]{1,0:T(8,128)(2,1)S(1)}, bf16[768,256]{1,0:T(8,128)(2,1)}, u32[]{:S(2)}, u32[]{:S(2)}) collective-permute-start(bf16[768,256]{1,0:T(8,128)(2,1)S(1)} %collective-permute-done.19.refs_2_), channel_id=1, source_target_pairs={{0,32},{1,33},{2,34},{3,35},{4,36},{5,37},{6,38},{7,39},{8,40},{9,... | collective-permute-start | bytes 1179656 | tf_op jit(solution)/shard_map/ppermute | solution.py:29
  199.4 17.6 %copy-start.25 = (bf16[768,256]{1,0:T(8,128)(2,1)S(1)}, bf16[768,256]{1,0:T(8,128)(2,1)}, u32[]{:S(2)}) copy-start(bf16[768,256]{1,0:T(8,128)(2,1)} %copy-done.24) | copy-start | bytes 1179652
  199.4 12.8 %collective-permute-start.27 = (bf16[768,256]{1,0:T(8,128)(2,1)S(1)}, bf16[768,256]{1,0:T(8,128)(2,1)}, u32[]{:S(2)}, u32[]{:S(2)}) collective-permute-start(bf16[768,256]{1,0:T(8,128)(2,1)S(1)} %collective-permute-done.19.refs_2_), channel_id=1, source_target_pairs={{0,96},{1,97},{2,98},{3,99},{4,100},{5,101},{6,102},{7,103},{8,104... | collective-permute-start | bytes 1179656 | tf_op jit(solution)/shard_map/ppermute | solution.py:29
  202.8 14.2 %copy-start.21 = (bf16[768,256]{1,0:T(8,128)(2,1)S(1)}, bf16[768,256]{1,0:T(8,128)(2,1)}, u32[]{:S(2)}) copy-start(bf16[768,256]{1,0:T(8,128)(2,1)} %copy-done.20) | copy-start | bytes 1179652
  202.8 10.1 %collective-permute-start.31 = (bf16[768,256]{1,0:T(8,128)(2,1)S(1)}, bf16[768,256]{1,0:T(8,128)(2,1)}, u32[]{:S(2)}, u32[]{:S(2)}) collective-permute-start(bf16[768,256]{1,0:T(8,128)(2,1)S(1)} %collective-permute-done.29.refs_12_), channel_id=1, source_target_pairs={{0,16},{1,17},{2,18},{3,19},{4,20},{5,21},{6,22},{7,23},{8,24},{9,... | collective-permute-start | bytes 1179656 | tf_op jit(solution)/shard_map/ppermute | solution.py:29
  203.2 13.9 %copy-start.23 = (bf16[768,256]{1,0:T(8,128)(2,1)S(1)}, bf16[768,256]{1,0:T(8,128)(2,1)}, u32[]{:S(2)}) copy-start(bf16[768,256]{1,0:T(8,128)(2,1)} %copy-done.22) | copy-start | bytes 1179652
  203.2 13.8 %collective-permute-start.30 = (bf16[768,256]{1,0:T(8,128)(2,1)S(1)}, bf16[768,256]{1,0:T(8,128)(2,1)S(1)}, u32[]{:S(2)}, u32[]{:S(2)}) collective-permute-start(bf16[768,256]{1,0:T(8,128)(2,1)S(1)} %collective-permute-done.29.refs_12_), channel_id=1, source_target_pairs={{0,8},{1,9},{2,10},{3,11},{4,12},{5,13},{6,14},{7,15},{8,0},{9,1},... | collective-permute-start | bytes 1179656 | tf_op jit(solution)/shard_map/ppermute | solution.py:29
  204.9 12.1 %collective-permute-start.24 = (bf16[768,256]{1,0:T(8,128)(2,1)S(1)}, bf16[768,256]{1,0:T(8,128)(2,1)S(1)}, u32[]{:S(2)}, u32[]{:S(2)}) collective-permute-start(bf16[768,256]{1,0:T(8,128)(2,1)S(1)} %collective-permute-done.23.refs_6_), channel_id=1, source_target_pairs={{0,8},{1,9},{2,10},{3,11},{4,12},{5,13},{6,14},{7,15},{8,0},{9,1},... | collective-permute-start | bytes 1179656 | tf_op jit(solution)/shard_map/ppermute | solution.py:29
  211.3 5.8 %copy-start.27 = (bf16[768,256]{1,0:T(8,128)(2,1)S(1)}, bf16[768,256]{1,0:T(8,128)(2,1)}, u32[]{:S(2)}) copy-start(bf16[768,256]{1,0:T(8,128)(2,1)} %copy-done.26) | copy-start | bytes 1179652
  211.3 5.7 %collective-permute-start.26 = (bf16[768,256]{1,0:T(8,128)(2,1)}, bf16[768,256]{1,0:T(8,128)(2,1)S(1)}, u32[]{:S(2)}, u32[]{:S(2)}) collective-permute-start(bf16[768,256]{1,0:T(8,128)(2,1)} %collective-permute-done.25.refs_8_), channel_id=1, source_target_pairs={{0,8},{1,9},{2,10},{3,11},{4,12},{5,13},{6,14},{7,15},{8,0},{9,1},... | collective-permute-start | bytes 1179656 | tf_op jit(solution)/shard_map/ppermute | solution.py:29
  212.2 4.8 %collective-permute-start.28 = (bf16[768,256]{1,0:T(8,128)(2,1)}, bf16[768,256]{1,0:T(8,128)(2,1)S(1)}, u32[]{:S(2)}, u32[]{:S(2)}) collective-permute-start(bf16[768,256]{1,0:T(8,128)(2,1)} %collective-permute-done.27.refs_10_), channel_id=1, source_target_pairs={{0,8},{1,9},{2,10},{3,11},{4,12},{5,13},{6,14},{7,15},{8,0},{9,1},... | collective-permute-start | bytes 1179656 | tf_op jit(solution)/shard_map/ppermute | solution.py:29
  212.9 4.1 %collective-permute-start.32 = (bf16[768,256]{1,0:T(8,128)(2,1)}, bf16[768,256]{1,0:T(8,128)(2,1)S(1)}, u32[]{:S(2)}, u32[]{:S(2)}) collective-permute-start(bf16[768,256]{1,0:T(8,128)(2,1)} %collective-permute-done.31.refs_14_), channel_id=1, source_target_pairs={{0,8},{1,9},{2,10},{3,11},{4,12},{5,13},{6,14},{7,15},{8,0},{9,1},... | collective-permute-start | bytes 1179656 | tf_op jit(solution)/shard_map/ppermute | solution.py:29
  217.0 13.4 %copy-start.1 = (s32[768,256]{1,0:T(8,128)S(1)}, s32[768,256]{1,0:T(8,128)}, u32[]{:S(2)}) copy-start(s32[768,256]{1,0:T(8,128)} %seen_ref.1) | copy-start | bytes 2359300
  217.1 1.1 copy-start.29
  218.1 12.3 %copy-start.37 = (f32[768,256]{1,0:T(8,128)S(1)}, f32[768,256]{1,0:T(8,128)}, u32[]{:S(2)}) copy-start(f32[768,256]{1,0:T(8,128)} %copy-done.36) | copy-start | bytes 2359300
  230.4 16.8 %copy-start.33 = (f32[768,1,256]{2,1,0:T(1,128)S(1)}, f32[768,1,256]{2,1,0:T(1,128)}, u32[]{:S(2)}) copy-start(f32[768,1,256]{2,1,0:T(1,128)} %param.8) | copy-start | bytes 2359300
  230.4 16.8 %copy-start.35 = (f32[8,96,256]{2,1,0:T(8,128)S(1)}, f32[8,96,256]{2,1,0:T(8,128)}, u32[]{:S(2)}) copy-start(f32[8,96,256]{2,1,0:T(8,128)} %copy-done.34) | copy-start | bytes 2359300
  (12 other events, 9.7 us)

commit v2 on v0

v2 whole, which is shorter than its diff:
```python
import jax
import jax.numpy as jnp
from jax import lax
from jax.experimental import pallas as pl
from jax.experimental.pallas import tpu as pltpu
from jax.sharding import PartitionSpec as P

BOTH = ("geno", "trial")
RING, PAIR, CORES = 4, 2, 2
F32, BF16 = jnp.float32, jnp.bfloat16
SMEM = pl.BlockSpec(memory_space=pltpu.SMEM)
VMEM = pl.BlockSpec(memory_space=pltpu.VMEM)
HBM = pl.BlockSpec(memory_space=pltpu.HBM)


def place(index):
    geno, trial = divmod(index, RING * PAIR)
    return (geno // 4, geno // 2 % 2, geno % 2, trial // 2, trial % 2)


def hop(cells, **by):
    step = [by.get(name, 0) for name in ("y", "z", "core", "x", "far")]
    pairs = []
    for index in range(RING * PAIR * CORES * RING * PAIR):
        y, z, core, x, far = (a + b for a, b in zip(place(index), step))
        geno = ((y % RING) * PAIR + z % PAIR) * CORES + core % CORES
        pairs.append((index, geno * RING * PAIR + (x % RING) * PAIR + far % PAIR))
    return lax.ppermute(cells, BOTH, pairs)


def together(*arrays):
    return lax.optimization_barrier(arrays)


STEPS = [(0, 0), (0, 1), (1, 0), (-1, 0), (2, 0), (1, 1), (-1, 1), (2, 1)]


def gather_geno(cells, kernel, *waiting, strip=None):
    geno = lax.axis_index("geno")
    y, z, core = geno // 4, geno // 2 % 2, geno % 2
    side, up = hop(cells, z=1), hop(cells, y=1)
    down, across = hop(cells, y=-1), hop(cells, y=2)
    strips, later = [], []
    if strip is not None:
        strips = [hop(strip, **{name: by}) for name, by in (("far", 1), ("x", 1), ("x", -1), ("x", 2))]
    side, up, down, across, kernel, *rest = together(
        side, up, down, across, kernel, *waiting, *strips
    )
    waiting, strips = rest[: len(waiting)], rest[len(waiting) :]
    if strip is not None:
        waiting = [swap(cells) for cells in waiting]
        later = [hop(strips[0], x=by) for by in (1, -1, 2)] + waiting
        side_across = hop(side, y=2)
    else:
        side_across = hop(across, z=1)
    side_up, side_down = hop(side, y=1), hop(side, y=-1)
    others = [hop(piece, core=1) for piece in (cells, side, up, down, across)]
    order = []
    for a, b in STEPS:
        base = (((y - a) % RING) * PAIR + (z + b) % PAIR) * CORES
        order += [base + core, base + 1 - core]
    order = jnp.stack(order).astype(jnp.int32)
    pieces = [cells, others[0], side, others[1], up, others[2], down, others[3], across, others[4]]
    carry = mix_part(kernel, pieces, order[:10], None, F32)
    carry, side_up, side_down, side_across, *later = together(
        carry, side_up, side_down, side_across, *later
    )
    pieces = []
    for piece in (side_up, side_down, side_across):
        pieces += [piece, hop(piece, core=1)]
    gathered = (kernel, pieces, order[10:], carry)
    if strip is None:
        return gathered, waiting
    return gathered, later[3:], [strip] + strips + later[:3]


STRIP = 5


def split(values, count):
    terms = []
    for _ in range(count):
        terms.append(values.astype(BF16))
        values = values - terms[-1].astype(F32)
    return terms


def strip_of(core, trial, kernel):
    half, width = kernel.shape[0] // 2, STRIP * kernel.shape[0]
    rows = lax.dynamic_slice_in_dim(kernel, core * half, half, axis=0)
    rows = jnp.concatenate([rows, rows[:, : width - kernel.shape[0]]], axis=1)
    return lax.dynamic_slice_in_dim(rows, trial * kernel.shape[0], width, axis=1)


def pack(count, right, observed, coef, length, above, below):
    rows, cols = right.shape
    part = rows // count

    def body(right_ref, seen_ref, coef_ref, length_ref, above_ref, below_ref, out_ref):
        line = lax.broadcasted_iota(jnp.int32, (16, cols), 0)

        def put(extra, first, values, terms):
            for k in range(terms):
                term = values.astype(BF16).astype(F32)
                extra = jnp.where(line == first + k, term, extra)
                values = values - term
            return extra

        common = put(jnp.zeros((16, cols), F32), 0, coef_ref[...], 3)
        common = put(common, 3, length_ref[...].astype(F32), 1)
        for t in range(count):
            first, last = t * part, (t + 1) * part
            before = right_ref[first - 1 : first] if t else above_ref[...]
            behind = right_ref[last : last + 1] if last < rows else below_ref[...]
            extra = put(put(common, 4, before, 2), 6, behind, 2)
            high, low = split(right_ref[first:last], 2)
            seen = seen_ref[first:last].astype(F32).astype(BF16)
            for k, piece in enumerate((high, low, seen, extra.astype(BF16))):
                out_ref[t, k * part : k * part + piece.shape[0]] = piece

    return pl.pallas_call(
        body,
        out_shape=jax.ShapeDtypeStruct((count, 3 * part + 16, cols), BF16),
        in_specs=[VMEM] * 6,
        out_specs=VMEM,
        compiler_params=pltpu.CompilerParams(vmem_limit_bytes=10 << 20),
    )(right, observed, coef, length, above, below)


def right_of(slab_ref, t, part):
    return slab_ref[t, :part].astype(F32) + slab_ref[t, part : 2 * part].astype(F32)


def seen_of(slab_ref, t, part):
    return slab_ref[t, 2 * part : 3 * part].astype(F32)


def swap(slabs):
    return lax.all_to_all(slabs, "trial", split_axis=0, concat_axis=0, tiled=True)


def exchange(rows):
    return lax.all_to_all(rows, BOTH, 0, 0, tiled=True)


def lanes(values):
    lane = lax.broadcasted_iota(jnp.int32, (1, 128), 1)
    row = jnp.zeros((1, 128), F32)
    for k, value in enumerate(values):
        row = jnp.where(lane == k, value, row)
    return row


def in_hbm(arrays):
    return [pltpu.with_memory_space_constraint(cells, pltpu.HBM) for cells in arrays]


def mix(kernel, pieces, order, finish, carry, others, shapes):
    count = len(pieces)
    rows, cols = pieces[0].shape
    others = ([] if carry is None else [carry]) + others

    def body(order_ref, kernel_ref, *refs):
        piece_refs, rest = refs[:count], refs[count:-4]
        blocks, cells, total, sems = refs[-4:]
        copies = []
        for k in range(count):
            at = pl.ds(pl.multiple_of(order_ref[k] * rows, rows), rows)
            copies.append(
                (
                    pltpu.make_async_copy(kernel_ref.at[:, at], blocks.at[k], sems.at[k, 0]),
                    pltpu.make_async_copy(piece_refs[k], cells.at[k], sems.at[k, 1]),
                )
            )
        for pair in copies:
            for copy in pair:
                copy.start()
        if carry is not None:
            total[...] = rest[0][...]
            rest = rest[1:]
        for k in range(count):
            for copy in copies[k]:
                copy.wait()
            for m in range(0, rows, 256):
                term = jnp.dot(blocks[k, m : m + 256], cells[k], preferred_element_type=F32)
                if carry is None and k == 0:
                    total[m : m + 256] = term
                else:
                    total[m : m + 256] += term
        finish(total, *rest)

    return pl.pallas_call(
        body,
        out_shape=shapes,
        in_specs=[SMEM] + [HBM] * (1 + count) + [VMEM] * len(others),
        out_specs=[VMEM] * len(shapes),
        scratch_shapes=[
            pltpu.VMEM((count, rows, rows), BF16),
            pltpu.VMEM((count, rows, cols), BF16),
            pltpu.VMEM((rows, cols), F32),
            pltpu.SemaphoreType.DMA((count, 2)),
        ],
        compiler_params=pltpu.CompilerParams(vmem_limit_bytes=26 << 20),
    )(order, *in_hbm([kernel, *pieces]), *others)


def mix_part(kernel, pieces, order, carry, kind):
    def finish(total, out_ref):
        out_ref[...] = total[...].astype(kind)

    shapes = [jax.ShapeDtypeStruct(pieces[0].shape, kind)]
    return mix(kernel, pieces, order, finish, carry, [], shapes)[0]


def mix_second(kernel, pieces, order, carry, seen, field, direction, devices):
    rows, cols = seen.shape

    def finish(total, seen_ref, field_ref, direction_ref, image_ref, sums_ref):
        part = 128
        product = jnp.zeros((8, cols), F32)
        for m in range(0, rows, part):
            at = slice(m, m + part)
            image = seen_ref[at].astype(F32) * total[at] + field_ref[at]
            image_ref[at] = image
            terms = direction_ref[at] * image
            product += jnp.sum(terms.reshape(part // 8, 8, cols), axis=0)
        sums_ref[...] = jnp.broadcast_to(lanes([jnp.sum(product)])[None], sums_ref.shape)

    shapes = [
        jax.ShapeDtypeStruct((rows, cols), F32),
        jax.ShapeDtypeStruct((devices, 1, 128), F32),
    ]
    return mix(kernel, pieces, order, finish, carry, [seen, field, direction], shapes)


def fetch(order_ref, strip_refs, held, sems):
    copies = []
    for k, strip_ref in enumerate(strip_refs):
        here = order_ref[8] if k % 2 == 0 else 1 - order_ref[8]
        target = held.at[k // 2, here]
        copies.append(pltpu.make_async_copy(strip_ref, target, sems.at[k // 2, k % 2]))
    for copy in copies:
        copy.start()
    return copies


def multiply(order_ref, left_ref, copies, held, total):
    total[...] = jnp.zeros_like(total)
    count = left_ref.shape[0]
    cols = held.shape[3] // STRIP
    for slot in range(count):
        for side in range(2):
            copies[2 * slot + side].wait()
        t = order_ref[slot]
        for r in range(STRIP):
            other = lax.rem(t + r, count)
            at = slice(r * cols, (r + 1) * cols)
            block = jnp.concatenate([held[slot, 0, :, at], held[slot, 1, :, at]], axis=0)
            total[other] += jnp.dot(left_ref[t], block, preferred_element_type=F32)
            if 0 < r < STRIP - 1:
                total[t] += lax.dot_general(
                    left_ref[other], block, (((1,), (1,)), ((), ())), preferred_element_type=F32
                )


def cross_call(body, size, operands, strips, shapes, scratch):
    count, part, cols = size
    return pl.pallas_call(
        body,
        out_shape=shapes,
        in_specs=[SMEM if x.ndim == 1 else VMEM for x in operands] + [HBM] * len(strips),
        out_specs=[VMEM] * len(shapes),
        scratch_shapes=scratch
        + [
            pltpu.VMEM((count, part, cols), F32),
            pltpu.VMEM((count, 2) + strips[0].shape, BF16),
            pltpu.SemaphoreType.DMA((count, 2)),
        ],
        compiler_params=pltpu.CompilerParams(vmem_limit_bytes=14 << 20),
        cost_estimate=pl.CostEstimate(
            flops=2 * part * (count * cols) ** 2,
            bytes_accessed=2 * (count * cols) ** 2,
            transcendentals=0,
        ),
    )(*operands, *in_hbm(strips))


def cross_first(order, mixed, slabs, strips, total_rows, devices):
    count, part, cols = mixed.shape

    def body(order_ref, mixed_ref, slab_ref, *refs):
        image_ref, sums_ref, total, held, sems = refs[16:]
        multiply(order_ref, mixed_ref, fetch(order_ref, refs[:16], held, sems), held, total)
        sums = [jnp.zeros((part, cols), F32) for _ in range(3)]
        line = lax.broadcasted_iota(jnp.int32, (part, cols), 0)
        first = order_ref[9]
        for t in range(count):
            right = right_of(slab_ref, t, part)
            extra = slab_ref[t, 3 * part :].astype(F32)
            coef = extra[0:1] + extra[1:2] + extra[2:3]
            length = extra[3:4]
            above = jnp.where(line == 0, extra[4:5] + extra[5:6], pltpu.roll(right, 1, 0))
            below = jnp.where(
                line == part - 1, extra[6:7] + extra[7:8], pltpu.roll(right, part - 1, 0)
            )
            flux = linked(first + line, length, total_rows) * (below - right)
            flux -= linked(first + line - 1, length, total_rows) * (right - above)
            image = seen_of(slab_ref, t, part) * total[t] + (right - coef * flux)
            image_ref[t] = image
            terms = (right * right, right * image, image * image)
            sums = [a + b for a, b in zip(sums, terms)]
        row = lanes([jnp.sum(total) for total in sums])
        sums_ref[...] = jnp.broadcast_to(row[None], sums_ref.shape)

    shapes = [
        jax.ShapeDtypeStruct(mixed.shape, F32),
        jax.ShapeDtypeStruct((devices, 1, 128), F32),
    ]
    return cross_call(body, mixed.shape, [order, mixed, slabs], strips, shapes, [])


def cross_second(order, sums, slabs, image, strips):
    count, part, cols = image.shape

    def body(order_ref, sums_ref, slab_ref, image_ref, *refs):
        out_ref, factor_ref, left, total, held, sems = refs[16:]
        copies = fetch(order_ref, refs[:16], held, sems)
        sums = jnp.sum(sums_ref[...], axis=0)
        rr, ri, ii = sums[:, 0:1], sums[:, 1:2], sums[:, 2:3]
        alpha = rr / ri
        new = rr - 2.0 * alpha * ri + alpha * alpha * ii
        beta = new / rr
        factor_ref[...] = lanes([alpha, beta, new])
        for t in range(count):
            right = right_of(slab_ref, t, part)
            direction = right - alpha * image_ref[t] + beta * right
            high, low = split(image_ref[t], 2)
            out_ref[t, part : 2 * part] = high
            out_ref[t, 2 * part :] = low
            left[t] = (seen_of(slab_ref, t, part) * direction).astype(BF16)
        multiply(order_ref, left, copies, held, total)
        for t in range(count):
            out_ref[t, :part] = total[t].astype(BF16)

    shapes = [
        jax.ShapeDtypeStruct((count, 3 * part, cols), BF16),
        jax.ShapeDtypeStruct((1, 128), F32),
    ]
    scratch = [pltpu.VMEM(image.shape, BF16)]
    return cross_call(body, image.shape, [order, sums, slabs, image], strips, shapes, scratch)


def conclude(sums, factors, right, direction, residual, image):
    rows, cols = right.shape

    def body(sums_ref, factor_ref, right_ref, direction_ref, residual_ref, image_ref, *outs):
        product = jnp.sum(sums_ref[...], axis=0)[:, 0:1]
        alpha, new = factor_ref[:, 0:1], factor_ref[:, 2:3]
        step = new / product
        part = 128
        for m in range(0, rows, part):
            at = slice(m, m + part)
            field = alpha * right_ref[at] + step * direction_ref[at]
            outs[0][at] = field[:, None, :]
            outs[1][at] = (residual_ref[at] - step * image_ref[at])[:, None, :]

    return pl.pallas_call(
        body,
        out_shape=[jax.ShapeDtypeStruct((rows, 1, cols), F32)] * 2,
        in_specs=[VMEM] * 6,
        out_specs=[VMEM] * 2,
        compiler_params=pltpu.CompilerParams(vmem_limit_bytes=10 << 20),
    )(sums, factors, right, direction, residual, image)


def linked(position, length, total_rows):
    later = (position + 1).astype(F32)
    whole_rows = jnp.floor((later + 0.5) / length) * length
    keep = (position >= 0) & (position + 1 < total_rows) & (later != whole_rows)
    return jnp.where(keep, 1.0, 0.0)


def field_of(cells, above, below, links, coef):
    padded = jnp.concatenate([above, cells, below], axis=-2)
    flux = links * (padded[..., 1:, :] - padded[..., :-1, :])
    return cells - coef * (flux[..., 1:, :] - flux[..., :-1, :])


def on_device(right_side, observed, row_length, field_coef, kernel_geno, kernel_trial):
    count = lax.axis_size("trial")
    rows, cols = observed.shape
    part = rows // count
    genos = lax.axis_size("geno")
    total_rows = rows * genos
    geno, trial = lax.axis_index("geno"), lax.axis_index("trial")
    right = right_side[:, 0, :]
    seen = observed.astype(F32)

    core = geno % CORES
    devices = count * genos
    following = [(i, i + 1) for i in range(genos - 1)]
    previous = [(i + 1, i) for i in range(genos - 1)]
    above = lax.ppermute(right[-1:], "geno", following)
    below = lax.ppermute(right[:1], "geno", previous)
    slabs = pack(count, right, observed, field_coef[None], row_length[None], above, below)
    strip = strip_of(core, trial, kernel_trial)
    gathered, (slabs,), strips = gather_geno(
        (seen * right).astype(BF16), kernel_geno, slabs, strip=strip
    )
    mixed = mix_part(*gathered, BF16)
    mixed, *strips = together(mixed, *strips)
    mixed_r = swap(mixed.reshape(count, part, cols))
    strips = [piece for own in strips for piece in (own, hop(own, core=1))]
    x, far = trial // PAIR, trial % PAIR
    order = [((x - a) % RING) * PAIR + (far + b) % PAIR for a, b in STEPS]
    order = jnp.stack(order + [core, geno * rows + trial * part]).astype(jnp.int32)

    image_r, sums = cross_first(order, mixed_r, slabs, strips, total_rows, devices)
    turned, factors = cross_second(order, exchange(sums), slabs, image_r, strips)
    turned = swap(turned)
    gathered, (turned,) = gather_geno(
        turned[:, :part].reshape(rows, cols), kernel_geno, turned
    )

    alpha, beta, new = factors[:, 0:1], factors[:, 1:2], factors[:, 2:3]
    image = turned[:, part : 2 * part].astype(F32) + turned[:, 2 * part :].astype(F32)
    image = image.reshape(rows, cols)
    residual = right - alpha * image
    direction = residual + beta * right
    above = lax.ppermute(direction[-1:], "geno", following)
    below = lax.ppermute(direction[:1], "geno", previous)
    position = (geno * rows - 1 + lax.iota(jnp.int32, rows + 1))[:, None]
    links = linked(position, row_length[None].astype(F32), total_rows)
    field = field_of(direction, above, below, links, field_coef[None])
    image, sums = mix_second(*gathered, seen.astype(BF16), field, direction, devices)
    return conclude(exchange(sums), factors, right, direction, residual, image)


def solution(mesh):
    return jax.shard_map(
        on_device,
        mesh=mesh,
        in_specs=(
            P("geno", None, "trial"),
            P("geno", "trial"),
            P("trial"),
            P("trial"),
            P("geno", None),
            P("trial", None),
        ),
        out_specs=(P("geno", None, "trial"), P("geno", None, "trial")),
        check_vma=False,
    )
```

time: 659 us -> 237 us (0.36)
  waiting for transfers between devices: 373 us -> 57.1 us
  blocking collectives: 192 us -> 52.4 us
  starting transfers between devices: 11.3 us -> 70.6 us
  Pallas kernels: 0 us -> 38.6 us
  matrix products: 33.3 us -> 0 us
  other arithmetic: 26.9 us -> 5.09 us
  between operations: 17.9 us -> 1.19 us
  local copies, waits for them, and re-layouts: 3.46 us -> 11.9 us
    reduce_scatter x2 -> x0, waiting for transfers between devices: 278 us -> none  [on_device(): lax.psum_scatter(jnp.einsum('jc,jx->cx', kernel_geno, flat, preferred_ele...]
    psum x3 -> x0, blocking collectives: 192 us -> none  [the longest x2 127 us: squares(): return lax.psum(jnp.sum(vector * vector, axis=(0, 2)), ('geno', 'trial'))]
    all_gather x2 -> x0, waiting for transfers between devices: 94.6 us -> none  [on_device(): lax.all_gather(mixed, 'trial', axis=2, tiled=True)]
    all_to_all x0 -> x3, blocking collectives: none -> 52.4 us  [the longest x2 31.9 us: exchange(): return lax.all_to_all(rows, BOTH, 0, 0, tiled=True)]
    ppermute x4 -> x49, waiting for transfers between devices: 0.7 us -> 51.5 us  [the longest x45 50.6 us: hop(): return lax.ppermute(cells, BOTH, pairs)]
    ppermute x4 -> x49, starting transfers between devices: 11.1 us -> 60.3 us  [the longest x45 48.8 us: hop(): return lax.ppermute(cells, BOTH, pairs)]
    pallas_call x0 -> x8, Pallas kernels: none -> 38.6 us  [the longest x4 25.5 us: mix(): pl.pallas_call(body, out_shape=shapes, in_specs=[SMEM] + [HBM] * (1 + cou...]
    dot_general x4 -> x0, matrix products: 33.3 us -> none  [the longest x2 24.1 us: on_device(): jnp.einsum('jc,jx->cx', kernel_geno, flat, preferred_element_type=jnp.flo...]
  transfers between devices with their start and end apart: 8 -> 51, of which waited for: 5 -> 22; matrix products, arithmetic and copies ran while one was open for 3% -> 2% of each run, Pallas kernels for 0% -> 6%
where the time goes in v2:
time: 237 us
  starting transfers between devices  70.6 us (30%)
  waiting for transfers between devices  57.1 us (24%)
  blocking collectives  52.4 us (22%)
  Pallas kernels  38.6 us (16%)
  local copies, waits for them, and re-layouts  11.9 us (5%)
  other arithmetic  5.09 us (2%)
    ppermute x45, waiting for transfers between devices, hop(): return lax.ppermute(cells, BOTH, pairs)  50.6 us
    ppermute x45, starting transfers between devices, hop(): return lax.ppermute(cells, BOTH, pairs)  48.8 us
    all_to_all x2, blocking collectives, exchange(): return lax.all_to_all(rows, BOTH, 0, 0, tiled=True)  31.9 us
    pallas_call x4, Pallas kernels, mix(): pl.pallas_call(body, out_shape=shapes, in_specs=[SMEM] + [HBM] * (1 + cou...  25.5 us
    all_to_all x1, blocking collectives, swap(): lax.all_to_all(slabs, 'trial', split_axis=0, concat_axis=0, tiled=True)  20.4 us
    pallas_call x2, Pallas kernels, cross_call(): pl.pallas_call(body, out_shape=shapes, in_specs=[SMEM if x.ndim == 1 else...  11 us
    all_to_all x2, starting transfers between devices, swap(): lax.all_to_all(slabs, 'trial', split_axis=0, concat_axis=0, tiled=True)  10.3 us
    unnamed x71, local copies, waits for them, and re-layouts  9.17 us
  transfers between devices with their start and end apart: 51, of which 22 were waited for; matrix products, arithmetic and copies ran while one was open for 2% of the time, Pallas kernels for 6%

profile of v2, /device:TPU:1, one launch (start us, length us, event | category | flops | bytes accessed | tf_op | source)
XLA Modules:
  0.0 236.8 jit_solution(10469029625974690312)
XLA Ops:
  0.7 1.2 copy-done
  1.9 0.8 constant_dynamic-slice_fusion.1
  2.7 1.8 fusion.6.refs_0_
  4.6 4.4 %collective-permute-start.6 = (bf16[128,1280]{1,0:T(8,128)(2,1)}, bf16[128,1280]{1,0:T(8,128)(2,1)}, u32[]{:S(2)}, u32[]{:S(2)}) collective-permute-start(bf16[128,1280]{1,0:T(8,128)(2,1)} %fusion.6.refs_0_), channel_id=1, source_target_pairs={{0,1},{1,0},{2,3},{3,2},{4,5},{5,4},{6,7},{7,6},{8,9},{9,8},{10,11... | collective-permute-start | bytes 983048 | tf_op jit(solution)/shard_map/ppermute | solution.py:28
  9.0 1.2 collective-permute-start.7
  10.2 1.5 collective-permute-start.8
  11.7 4.0 %collective-permute-start.4 = (f32[1,256]{1,0:T(1,128)S(1)}, f32[1,256]{1,0:T(1,128)S(1)}, u32[]{:S(2)}, u32[]{:S(2)}) collective-permute-start(f32[1,256]{1,0:T(1,128)S(1)} %get-tuple-element.93), channel_id=1, source_target_pairs={{0,8},{8,16},{16,24},{24,32},{32,40},{40,48},{48,56},{56,64},{64,7... | collective-permute-start | bytes 3080 | tf_op jit(solution)/shard_map/ppermute | solution.py:403
  15.7 1.9 collective-permute-start.5
  17.8 1.8 collective-permute-start
  19.7 0.9 collective-permute-done.5.below_ref
  20.6 1.3 collective-permute-start.1
  21.9 1.4 collective-permute-start.2
  23.4 1.6 collective-permute-start.3
  25.0 1.8 collective-permute-start.9
  26.8 8.0 %collective-permute-done.9.refs_8_ = bf16[128,1280]{1,0:T(8,128)(2,1)S(1)} collective-permute-done((bf16[128,1280]{1,0:T(8,128)(2,1)}, bf16[128,1280]{1,0:T(8,128)(2,1)S(1)}, u32[]{:S(2)}, u32[]{:S(2)}) %collective-permute-start.9) | collective-permute-done | bytes 327712 | tf_op jit(solution)/shard_map/ppermute | solution.py:28
  34.8 0.7 copy-done.15
  35.5 2.1 collective-permute-start.10
  37.9 0.6 copy-done.2
  38.5 1.0 copy-done.4
  39.6 0.7 copy-done.17
  40.5 0.8 copy-done.19
  41.3 0.7 collective-permute-done.3.refs_8_
  42.0 3.7 %all-to-all-start = ((bf16[8,304,256]{2,1,0:T(8,128)(2,1)}), bf16[8,304,256]{2,1,0:T(8,128)(2,1)S(1)}, u32[]{:S(2)}, u32[]{:S(2)}) async-start(bf16[8,304,256]{2,1,0:T(8,128)(2,1)} %copy-done.4), calls=%async_computation | async-start | bytes 2490368 | tf_op jit(solution)/shard_map/all_to_all | solution.py:139
  45.7 1.1 collective-permute-start.11
  47.3 1.6 collective-permute-start.18
  49.1 19.7 %collective-permute-done.18.refs_10_ = bf16[128,1280]{1,0:T(8,128)(2,1)} collective-permute-done((bf16[128,1280]{1,0:T(8,128)(2,1)}, bf16[128,1280]{1,0:T(8,128)(2,1)}, u32[]{:S(2)}, u32[]{:S(2)}) %collective-permute-start.18) | collective-permute-done | bytes 327712 | tf_op jit(solution)/shard_map/ppermute | solution.py:28
  68.9 1.6 collective-permute-start.15
  70.5 1.0 collective-permute-start.16
  71.6 0.8 collective-permute-start.17
  72.4 2.8 %collective-permute-start.19 = (bf16[128,1280]{1,0:T(8,128)(2,1)}, bf16[128,1280]{1,0:T(8,128)(2,1)S(1)}, u32[]{:S(2)}, u32[]{:S(2)}) collective-permute-start(bf16[128,1280]{1,0:T(8,128)(2,1)} %collective-permute-done.6.refs_2_), channel_id=1, source_target_pairs={{0,6},{1,7},{2,0},{3,1},{4,2},{5,3},{6,4},{7,5},{8,14},{9,15},{10,... | collective-permute-start | bytes 983048 | tf_op jit(solution)/shard_map/ppermute | solution.py:28
  75.2 0.8 copy-done.23
  76.0 7.2 %shard_map.78.refs_6_ = f32[768,256]{1,0:T(8,128)S(1)} custom-call(s32[10]{0:T(128)S(1)} %stack.131.order_ref, bf16[768,12288]{1,0:T(8,128)(2,1)} %kernel_ref.3, bf16[768,256]{1,0:T(8,128)(2,1)} %copy-done.13, bf16[768,256]{1,0:T(8,128)(2,1)} %collective-permute-done.10.refs_1_, bf16[768,256]{1,0:T(8,128)(2,1)} %copy-done.17, bf16[768,256]{1,0:T(8,128)(2,1)} %copy-done.20, ...), custom_call_target="tpu_custom_call" | custom-call | tf_op jit(solution)/shard_map/pallas_call | solution.py:192
  83.2 0.9 copy-done.5
  84.3 1.8 collective-permute-done.17.refs_4_
  86.2 4.4 %collective-permute-start.21 = (bf16[768,256]{1,0:T(8,128)(2,1)}, bf16[768,256]{1,0:T(8,128)(2,1)}, u32[]{:S(2)}, u32[]{:S(2)}) collective-permute-start(bf16[768,256]{1,0:T(8,128)(2,1)} %collective-permute-done.15.refs_0_), channel_id=1, source_target_pairs={{0,8},{1,9},{2,10},{3,11},{4,12},{5,13},{6,14},{7,15},{8,0},{9,1},... | collective-permute-start | bytes 1179656 | tf_op jit(solution)/shard_map/ppermute | solution.py:28
  91.1 1.1 collective-permute-done.21.refs_1_
  93.4 1.1 copy-done.6
  94.5 5.9 %shard_map.79 = bf16[768,256]{1,0:T(8,128)(2,1)} custom-call(s32[6]{0:T(128)S(1)} %stack.109.order_ref, bf16[768,12288]{1,0:T(8,128)(2,1)} %kernel_ref.3, bf16[768,256]{1,0:T(8,128)(2,1)} %collective-permute-done.15.refs_0_, bf16[768,256]{1,0:T(8,128)(2,1)} %collective-permute-done.21.refs_1_, bf16[768,256]{1,0:T(8,128)(2,1)} %collective-permute-done.16.refs_2_, ...), custom_call_target="tpu_custom_call" | custom-call | tf_op jit(solution)/shard_map/pallas_call | solution.py:192
  101.3 6.6 %all-to-all-start.1 = ((bf16[8,96,256]{2,1,0:T(8,128)(2,1)}), bf16[8,96,256]{2,1,0:T(8,128)(2,1)S(1)}, u32[]{:S(2)}, u32[]{:S(2)}) async-start(bf16[8,96,256]{2,1,0:T(8,128)(2,1)} %bitcast.30), calls=%async_computation.1 | async-start | bytes 786432 | tf_op jit(solution)/shard_map/all_to_all | solution.py:139
  111.8 5.6 %all-to-all-done.1.mixed_ref = bf16[8,96,256]{2,1,0:T(8,128)(2,1)S(1)} async-done(((bf16[8,96,256]{2,1,0:T(8,128)(2,1)}), bf16[8,96,256]{2,1,0:T(8,128)(2,1)S(1)}, u32[]{:S(2)}, u32[]{:S(2)}) %all-to-all-start.1) | async-done | bytes 393248 | tf_op jit(solution)/shard_map/all_to_all | solution.py:139
  117.4 6.1 %shard_map.80 = (f32[8,96,256]{2,1,0:T(8,128)S(1)}, f32[128,1,128]{2,1,0:T(1,128)S(1)}) custom-call(s32[10]{0:T(128)S(1)} %stack.120.order_ref, bf16[8,96,256]{2,1,0:T(8,128)(2,1)S(1)} %all-to-all-done.1.mixed_ref, bf16[8,304,256]{2,1,0:T(8,128)(2,1)S(1)} %all-to-all-done.slab_ref, bf16[128,1280]{1,0:T(8,128)(2,1)} %fusion.6.refs_0_, ...), custom_call_target="tpu_custom_call" | custom-call | flops 805306368 | bytes 8388608 | tf_op jit(solution)/shard_map/pallas_call | solution.py:268
  123.5 17.2 %all_to_all.25.sums_ref = f32[128,1,128]{2,1,0:T(1,128)S(1)} all-to-all(f32[128,1,128]{2,1,0:T(1,128)S(1)} %get-tuple-element.72), channel_id=1, replica_groups=mesh['geno'=16,'trial'=8] {'geno','trial'}, dimensions={0} | all-to-all | bytes 131072 | tf_op jit(solution)/shard_map/all_to_all | solution.py:143
  140.7 4.9 %shard_map.81 = (bf16[8,288,256]{2,1,0:T(8,128)(2,1)S(1)}, f32[1,128]{1,0:T(1,128)S(1)}) custom-call(s32[10]{0:T(128)S(1)} %stack.120.order_ref, f32[128,1,128]{2,1,0:T(1,128)S(1)} %all_to_all.25.sums_ref, bf16[8,304,256]{2,1,0:T(8,128)(2,1)S(1)} %all-to-all-done.slab_ref, f32[8,96,256]{2,1,0:T(8,128)S(1)} %get-tuple-element.73.image_ref, ...), custom_call_target="tpu_custom_call" | custom-call | flops 805306368 | bytes 8388608 | tf_op jit(solution)/shard_map/pallas_call | solution.py:268
  145.5 20.4 %all_to_all.26 = bf16[8,288,256]{2,1,0:T(8,128)(2,1)} all-to-all(bf16[8,288,256]{2,1,0:T(8,128)(2,1)S(1)} %get-tuple-element.74), channel_id=1, replica_groups=mesh['geno'=16,'trial'=8] {'trial'}, dimensions={0} | all-to-all | bytes 2359296 | tf_op jit(solution)/shard_map/all_to_all | solution.py:139
  165.9 1.0 slice.66
  167.0 1.3 collective-permute-start.32
  168.7 2.2 collective-permute-start.34
  171.0 2.4 %collective-permute-start.36 = (bf16[768,256]{1,0:T(8,128)(2,1)S(1)}, bf16[768,256]{1,0:T(8,128)(2,1)S(1)}, u32[]{:S(2)}, u32[]{:S(2)}) collective-permute-start(bf16[768,256]{1,0:T(8,128)(2,1)S(1)} %bitcast.59), channel_id=1, source_target_pairs={{0,8},{1,9},{2,10},{3,11},{4,12},{5,13},{6,14},{7,15},{8,0},{9,1},... | collective-permute-start | bytes 1179656 | tf_op jit(solution)/shard_map/ppermute | solution.py:28
  173.4 2.3 collective-permute-done.32.refs_2_
  175.7 3.2 %collective-permute-done.33.refs_4_ = bf16[768,256]{1,0:T(8,128)(2,1)} collective-permute-done((bf16[768,256]{1,0:T(8,128)(2,1)S(1)}, bf16[768,256]{1,0:T(8,128)(2,1)}, u32[]{:S(2)}, u32[]{:S(2)}) %collective-permute-start.33) | collective-permute-done | bytes 393248 | tf_op jit(solution)/shard_map/ppermute | solution.py:28
  178.8 7.6 %collective-permute-done.35.refs_8_ = bf16[768,256]{1,0:T(8,128)(2,1)} collective-permute-done((bf16[768,256]{1,0:T(8,128)(2,1)S(1)}, bf16[768,256]{1,0:T(8,128)(2,1)}, u32[]{:S(2)}, u32[]{:S(2)}) %collective-permute-start.35) | collective-permute-done | bytes 393248 | tf_op jit(solution)/shard_map/ppermute | solution.py:28
  186.4 3.1 %collective-permute-start.37 = (bf16[768,256]{1,0:T(8,128)(2,1)}, bf16[768,256]{1,0:T(8,128)(2,1)S(1)}, u32[]{:S(2)}, u32[]{:S(2)}) collective-permute-start(bf16[768,256]{1,0:T(8,128)(2,1)} %collective-permute-done.32.refs_2_), channel_id=1, source_target_pairs={{0,8},{1,9},{2,10},{3,11},{4,12},{5,13},{6,14},{7,15},{8,0},{9,1},... | collective-permute-start | bytes 1179656 | tf_op jit(solution)/shard_map/ppermute | solution.py:28
  190.7 2.2 collective-permute-start.42
  192.9 1.8 add_multiply_fusion
  194.7 1.1 collective-permute-start.40
  196.5 0.7 bitcast_subtract_fusion
  197.3 0.8 collective-permute-done.39.refs_7_
  198.1 2.3 collective-permute-start.47
  200.4 3.3 %collective-permute-start.48 = (f32[1,256]{1,0:T(1,128)S(1)}, f32[1,256]{1,0:T(1,128)S(1)}, u32[]{:S(2)}, u32[]{:S(2)}) collective-permute-start(f32[1,256]{1,0:T(1,128)S(1)} %get-tuple-element.90), channel_id=1, source_target_pairs={{0,8},{8,16},{16,24},{24,32},{32,40},{40,48},{48,56},{56,64},{64,7... | collective-permute-start | bytes 3080 | tf_op jit(solution)/shard_map/ppermute | solution.py:430
  203.7 7.2 %shard_map.82.refs_6_ = f32[768,256]{1,0:T(8,128)S(1)} custom-call(s32[10]{0:T(128)S(1)} %stack.131.order_ref, bf16[768,12288]{1,0:T(8,128)(2,1)} %kernel_ref.3, bf16[768,256]{1,0:T(8,128)(2,1)} %bitcast.60, bf16[768,256]{1,0:T(8,128)(2,1)} %copy-done.24, bf16[768,256]{1,0:T(8,128)(2,1)} %collective-permute-done.32.refs_2_, bf16[768,256]{1,0:T(8,128)(2,1)} %copy-done.25, ...), custom_call_target="tpu_custom_call" | custom-call | tf_op jit(solution)/shard_map/pallas_call | solution.py:192
  214.1 0.7 copy-done.34
  214.8 5.3 %shard_map.83 = (f32[768,256]{1,0:T(8,128)S(1)}, f32[128,1,128]{2,1,0:T(1,128)S(1)}) custom-call(s32[6]{0:T(128)S(1)} %stack.109.order_ref, bf16[768,12288]{1,0:T(8,128)(2,1)} %kernel_ref.3, bf16[768,256]{1,0:T(8,128)(2,1)} %copy-done.29, bf16[768,256]{1,0:T(8,128)(2,1)} %copy-done.32, bf16[768,256]{1,0:T(8,128)(2,1)} %copy-done.30, ...), custom_call_target="tpu_custom_call" | custom-call | tf_op jit(solution)/shard_map/pallas_call | solution.py:192
  220.1 14.8 %all_to_all.27.sums_ref = f32[128,1,128]{2,1,0:T(1,128)S(1)} all-to-all(f32[128,1,128]{2,1,0:T(1,128)S(1)} %get-tuple-element.86), channel_id=1, replica_groups=mesh['geno'=16,'trial'=8] {'geno','trial'}, dimensions={0} | all-to-all | bytes 131072 | tf_op jit(solution)/shard_map/all_to_all | solution.py:143
  234.9 1.9 shard_map.84
  (140 shorter events, 13.9 us)
Async XLA Ops:
  1.9 9.8 %copy-start.9 = (f32[768,1,256]{2,1,0:T(1,128)S(1)}, f32[768,1,256]{2,1,0:T(1,128)}, u32[]{:S(2)}) copy-start(f32[768,1,256]{2,1,0:T(1,128)} %param.6) | copy-start | bytes 2359300
  1.9 15.8 %copy-start.1 = (s32[768,256]{1,0:T(8,128)S(1)}, s32[768,256]{1,0:T(8,128)}, u32[]{:S(2)}) copy-start(s32[768,256]{1,0:T(8,128)} %seen_ref.1) | copy-start | bytes 2359300
  4.6 33.0 %copy-start.10 = (f32[768,1,256]{2,1,0:T(1,128)S(1)}, f32[768,1,256]{2,1,0:T(1,128)}, u32[]{:S(2)}) copy-start(f32[768,1,256]{2,1,0:T(1,128)} %param.6) | copy-start | bytes 2359300
  4.6 17.3 %collective-permute-start.6 = (bf16[128,1280]{1,0:T(8,128)(2,1)}, bf16[128,1280]{1,0:T(8,128)(2,1)}, u32[]{:S(2)}, u32[]{:S(2)}) collective-permute-start(bf16[128,1280]{1,0:T(8,128)(2,1)} %fusion.6.refs_0_), channel_id=1, source_target_pairs={{0,1},{1,0},{2,3},{3,2},{4,5},{5,4},{6,7},{7,6},{8,9},{9,8},{10,11... | collective-permute-start | bytes 983048 | tf_op jit(solution)/shard_map/ppermute | solution.py:28
  9.0 14.4 %collective-permute-start.7 = (bf16[128,1280]{1,0:T(8,128)(2,1)}, bf16[128,1280]{1,0:T(8,128)(2,1)}, u32[]{:S(2)}, u32[]{:S(2)}) collective-permute-start(bf16[128,1280]{1,0:T(8,128)(2,1)} %fusion.6.refs_0_), channel_id=1, source_target_pairs={{0,2},{1,3},{2,4},{3,5},{4,6},{5,7},{6,0},{7,1},{8,10},{9,11},{10,... | collective-permute-start | bytes 983048 | tf_op jit(solution)/shard_map/ppermute | solution.py:28
  10.2 14.8 %collective-permute-start.8 = (bf16[128,1280]{1,0:T(8,128)(2,1)}, bf16[128,1280]{1,0:T(8,128)(2,1)S(1)}, u32[]{:S(2)}, u32[]{:S(2)}) collective-permute-start(bf16[128,1280]{1,0:T(8,128)(2,1)} %fusion.6.refs_0_), channel_id=1, source_target_pairs={{0,6},{1,7},{2,0},{3,1},{4,2},{5,3},{6,4},{7,5},{8,14},{9,15},{10,... | collective-permute-start | bytes 983048 | tf_op jit(solution)/shard_map/ppermute | solution.py:28
  11.7 6.1 %collective-permute-start.4 = (f32[1,256]{1,0:T(1,128)S(1)}, f32[1,256]{1,0:T(1,128)S(1)}, u32[]{:S(2)}, u32[]{:S(2)}) collective-permute-start(f32[1,256]{1,0:T(1,128)S(1)} %get-tuple-element.93), channel_id=1, source_target_pairs={{0,8},{8,16},{16,24},{24,32},{32,40},{40,48},{48,56},{56,64},{64,7... | collective-permute-start | bytes 3080 | tf_op jit(solution)/shard_map/ppermute | solution.py:403
  15.7 4.9 %collective-permute-start.5 = (f32[1,256]{1,0:T(1,128)S(1)}, f32[1,256]{1,0:T(1,128)S(1)}, u32[]{:S(2)}, u32[]{:S(2)}) collective-permute-start(f32[1,256]{1,0:T(1,128)S(1)} %get-tuple-element.92), channel_id=1, source_target_pairs={{8,0},{16,8},{24,16},{32,24},{40,32},{48,40},{56,48},{64,56},{72,6... | collective-permute-start | bytes 3080 | tf_op jit(solution)/shard_map/ppermute | solution.py:404
  17.8 20.1 %copy-start.13 = (bf16[768,256]{1,0:T(8,128)(2,1)}, bf16[768,256]{1,0:T(8,128)(2,1)S(1)}, u32[]{:S(2)}) copy-start(bf16[768,256]{1,0:T(8,128)(2,1)S(1)} %multiply_convert_fusion.refs_0_) | copy-start | bytes 1179652
  17.8 19.9 %copy-start.7 = (f32[256]{0:T(256)S(1)}, f32[256]{0:T(256)}, u32[]{:S(2)}) copy-start(f32[256]{0:T(256)} %param.9) | copy-start | bytes 3076
  17.8 19.9 %copy-start.8 = (s32[256]{0:T(256)S(1)}, s32[256]{0:T(256)}, u32[]{:S(2)}) copy-start(s32[256]{0:T(256)} %param.8) | copy-start | bytes 3076
  17.8 21.8 %collective-permute-start = (bf16[768,256]{1,0:T(8,128)(2,1)S(1)}, bf16[768,256]{1,0:T(8,128)(2,1)S(1)}, u32[]{:S(2)}, u32[]{:S(2)}) collective-permute-start(bf16[768,256]{1,0:T(8,128)(2,1)S(1)} %multiply_convert_fusion.refs_0_), channel_id=1, source_target_pairs={{0,16},{1,17},{2,18},{3,19},{4,20},{5,21},{6,22},{7,23},{8,24},{9,... | collective-permute-start | bytes 1179656 | tf_op jit(solution)/shard_map/ppermute | solution.py:28
  20.6 19.0 %collective-permute-start.1 = (bf16[768,256]{1,0:T(8,128)(2,1)S(1)}, bf16[768,256]{1,0:T(8,128)(2,1)S(1)}, u32[]{:S(2)}, u32[]{:S(2)}) collective-permute-start(bf16[768,256]{1,0:T(8,128)(2,1)S(1)} %multiply_convert_fusion.refs_0_), channel_id=1, source_target_pairs={{0,32},{1,33},{2,34},{3,35},{4,36},{5,37},{6,38},{7,39},{8,40},{9,... | collective-permute-start | bytes 1179656 | tf_op jit(solution)/shard_map/ppermute | solution.py:28
  21.9 17.7 %collective-permute-start.2 = (bf16[768,256]{1,0:T(8,128)(2,1)S(1)}, bf16[768,256]{1,0:T(8,128)(2,1)S(1)}, u32[]{:S(2)}, u32[]{:S(2)}) collective-permute-start(bf16[768,256]{1,0:T(8,128)(2,1)S(1)} %multiply_convert_fusion.refs_0_), channel_id=1, source_target_pairs={{0,96},{1,97},{2,98},{3,99},{4,100},{5,101},{6,102},{7,103},{8,104... | collective-permute-start | bytes 1179656 | tf_op jit(solution)/shard_map/ppermute | solution.py:28
  23.4 18.6 %collective-permute-start.3 = (bf16[768,256]{1,0:T(8,128)(2,1)S(1)}, bf16[768,256]{1,0:T(8,128)(2,1)}, u32[]{:S(2)}, u32[]{:S(2)}) collective-permute-start(bf16[768,256]{1,0:T(8,128)(2,1)S(1)} %multiply_convert_fusion.refs_0_), channel_id=1, source_target_pairs={{0,64},{1,65},{2,66},{3,67},{4,68},{5,69},{6,70},{7,71},{8,72},{9,... | collective-permute-start | bytes 1179656 | tf_op jit(solution)/shard_map/ppermute | solution.py:28
  25.0 17.0 %copy-start.14 = (bf16[128,1280]{1,0:T(8,128)(2,1)}, bf16[128,1280]{1,0:T(8,128)(2,1)S(1)}, u32[]{:S(2)}) copy-start(bf16[128,1280]{1,0:T(8,128)(2,1)S(1)} %collective-permute-done.8.refs_6_) | copy-start | bytes 983044
  25.0 9.8 %collective-permute-start.9 = (bf16[128,1280]{1,0:T(8,128)(2,1)}, bf16[128,1280]{1,0:T(8,128)(2,1)S(1)}, u32[]{:S(2)}, u32[]{:S(2)}) collective-permute-start(bf16[128,1280]{1,0:T(8,128)(2,1)} %fusion.6.refs_0_), channel_id=1, source_target_pairs={{0,4},{1,5},{2,6},{3,7},{4,0},{5,1},{6,2},{7,3},{8,12},{9,13},{10,... | collective-permute-start | bytes 983048 | tf_op jit(solution)/shard_map/ppermute | solution.py:28
  35.5 13.4 %collective-permute-start.10 = (bf16[768,256]{1,0:T(8,128)(2,1)S(1)}, bf16[768,256]{1,0:T(8,128)(2,1)}, u32[]{:S(2)}, u32[]{:S(2)}) collective-permute-start(bf16[768,256]{1,0:T(8,128)(2,1)S(1)} %multiply_convert_fusion.refs_0_), channel_id=1, source_target_pairs={{0,8},{1,9},{2,10},{3,11},{4,12},{5,13},{6,14},{7,15},{8,0},{9,1},... | collective-permute-start | bytes 1179656 | tf_op jit(solution)/shard_map/ppermute | solution.py:28
  42.0 44.2 %all-to-all-start = ((bf16[8,304,256]{2,1,0:T(8,128)(2,1)}), bf16[8,304,256]{2,1,0:T(8,128)(2,1)S(1)}, u32[]{:S(2)}, u32[]{:S(2)}) async-start(bf16[8,304,256]{2,1,0:T(8,128)(2,1)} %copy-done.4), calls=%async_computation | async-start | bytes 2490368 | tf_op jit(solution)/shard_map/all_to_all | solution.py:139
  45.7 24.8 %collective-permute-start.11 = (bf16[768,256]{1,0:T(8,128)(2,1)}, bf16[768,256]{1,0:T(8,128)(2,1)S(1)}, u32[]{:S(2)}, u32[]{:S(2)}) collective-permute-start(bf16[768,256]{1,0:T(8,128)(2,1)} %copy-done.17), channel_id=1, source_target_pairs={{0,8},{1,9},{2,10},{3,11},{4,12},{5,13},{6,14},{7,15},{8,0},{9,1},... | collective-permute-start | bytes 1179656 | tf_op jit(solution)/shard_map/ppermute | solution.py:28
  46.8 24.8 %collective-permute-start.12 = (bf16[768,256]{1,0:T(8,128)(2,1)}, bf16[768,256]{1,0:T(8,128)(2,1)S(1)}, u32[]{:S(2)}, u32[]{:S(2)}) collective-permute-start(bf16[768,256]{1,0:T(8,128)(2,1)} %copy-done.18), channel_id=1, source_target_pairs={{0,8},{1,9},{2,10},{3,11},{4,12},{5,13},{6,14},{7,15},{8,0},{9,1},... | collective-permute-start | bytes 1179656 | tf_op jit(solution)/shard_map/ppermute | solution.py:28
  46.9 25.5 %collective-permute-start.13 = (bf16[768,256]{1,0:T(8,128)(2,1)}, bf16[768,256]{1,0:T(8,128)(2,1)S(1)}, u32[]{:S(2)}, u32[]{:S(2)}) collective-permute-start(bf16[768,256]{1,0:T(8,128)(2,1)} %copy-done.19), channel_id=1, source_target_pairs={{0,8},{1,9},{2,10},{3,11},{4,12},{5,13},{6,14},{7,15},{8,0},{9,1},... | collective-permute-start | bytes 1179656 | tf_op jit(solution)/shard_map/ppermute | solution.py:28
  47.3 21.6 %collective-permute-start.18 = (bf16[128,1280]{1,0:T(8,128)(2,1)}, bf16[128,1280]{1,0:T(8,128)(2,1)}, u32[]{:S(2)}, u32[]{:S(2)}) collective-permute-start(bf16[128,1280]{1,0:T(8,128)(2,1)} %collective-permute-done.6.refs_2_), channel_id=1, source_target_pairs={{0,2},{1,3},{2,4},{3,5},{4,6},{5,7},{6,0},{7,1},{8,10},{9,11},{10,... | collective-permute-start | bytes 983048 | tf_op jit(solution)/shard_map/ppermute | solution.py:28
  48.9 26.3 %collective-permute-start.14 = (bf16[768,256]{1,0:T(8,128)(2,1)}, bf16[768,256]{1,0:T(8,128)(2,1)S(1)}, u32[]{:S(2)}, u32[]{:S(2)}) collective-permute-start(bf16[768,256]{1,0:T(8,128)(2,1)} %collective-permute-done.3.refs_8_), channel_id=1, source_target_pairs={{0,8},{1,9},{2,10},{3,11},{4,12},{5,13},{6,14},{7,15},{8,0},{9,1},... | collective-permute-start | bytes 1179656 | tf_op jit(solution)/shard_map/ppermute | solution.py:28
  68.9 15.5 %collective-permute-start.15 = (bf16[768,256]{1,0:T(8,128)(2,1)}, bf16[768,256]{1,0:T(8,128)(2,1)}, u32[]{:S(2)}, u32[]{:S(2)}) collective-permute-start(bf16[768,256]{1,0:T(8,128)(2,1)} %copy-done.17), channel_id=1, source_target_pairs={{0,32},{1,33},{2,34},{3,35},{4,36},{5,37},{6,38},{7,39},{8,40},{9,... | collective-permute-start | bytes 1179656 | tf_op jit(solution)/shard_map/ppermute | solution.py:28
  70.5 13.8 %collective-permute-start.16 = (bf16[768,256]{1,0:T(8,128)(2,1)}, bf16[768,256]{1,0:T(8,128)(2,1)}, u32[]{:S(2)}, u32[]{:S(2)}) collective-permute-start(bf16[768,256]{1,0:T(8,128)(2,1)} %copy-done.17), channel_id=1, source_target_pairs={{0,96},{1,97},{2,98},{3,99},{4,100},{5,101},{6,102},{7,103},{8,104... | collective-permute-start | bytes 1179656 | tf_op jit(solution)/shard_map/ppermute | solution.py:28
  71.6 14.6 %collective-permute-start.17 = (bf16[768,256]{1,0:T(8,128)(2,1)}, bf16[768,256]{1,0:T(8,128)(2,1)}, u32[]{:S(2)}, u32[]{:S(2)}) collective-permute-start(bf16[768,256]{1,0:T(8,128)(2,1)} %copy-done.17), channel_id=1, source_target_pairs={{0,64},{1,65},{2,66},{3,67},{4,68},{5,69},{6,70},{7,71},{8,72},{9,... | collective-permute-start | bytes 1179656 | tf_op jit(solution)/shard_map/ppermute | solution.py:28
  72.4 11.7 %collective-permute-start.19 = (bf16[128,1280]{1,0:T(8,128)(2,1)}, bf16[128,1280]{1,0:T(8,128)(2,1)S(1)}, u32[]{:S(2)}, u32[]{:S(2)}) collective-permute-start(bf16[128,1280]{1,0:T(8,128)(2,1)} %collective-permute-done.6.refs_2_), channel_id=1, source_target_pairs={{0,6},{1,7},{2,0},{3,1},{4,2},{5,3},{6,4},{7,5},{8,14},{9,15},{10,... | collective-permute-start | bytes 983048 | tf_op jit(solution)/shard_map/ppermute | solution.py:28
  75.9 8.4 %collective-permute-start.20 = (bf16[128,1280]{1,0:T(8,128)(2,1)}, bf16[128,1280]{1,0:T(8,128)(2,1)}, u32[]{:S(2)}, u32[]{:S(2)}) collective-permute-start(bf16[128,1280]{1,0:T(8,128)(2,1)} %collective-permute-done.6.refs_2_), channel_id=1, source_target_pairs={{0,4},{1,5},{2,6},{3,7},{4,0},{5,1},{6,2},{7,3},{8,12},{9,13},{10,... | collective-permute-start | bytes 983048 | tf_op jit(solution)/shard_map/ppermute | solution.py:28
  84.1 16.3 %copy-start.16 = (bf16[128,1280]{1,0:T(8,128)(2,1)}, bf16[128,1280]{1,0:T(8,128)(2,1)S(1)}, u32[]{:S(2)}) copy-start(bf16[128,1280]{1,0:T(8,128)(2,1)S(1)} %collective-permute-done.19.refs_12_) | copy-start | bytes 983044
  86.2 6.0 %collective-permute-start.21 = (bf16[768,256]{1,0:T(8,128)(2,1)}, bf16[768,256]{1,0:T(8,128)(2,1)}, u32[]{:S(2)}, u32[]{:S(2)}) collective-permute-start(bf16[768,256]{1,0:T(8,128)(2,1)} %collective-permute-done.15.refs_0_), channel_id=1, source_target_pairs={{0,8},{1,9},{2,10},{3,11},{4,12},{5,13},{6,14},{7,15},{8,0},{9,1},... | collective-permute-start | bytes 1179656 | tf_op jit(solution)/shard_map/ppermute | solution.py:28
  90.5 2.3 collective-permute-start.22
  90.6 2.7 %collective-permute-start.23 = (bf16[768,256]{1,0:T(8,128)(2,1)}, bf16[768,256]{1,0:T(8,128)(2,1)}, u32[]{:S(2)}, u32[]{:S(2)}) collective-permute-start(bf16[768,256]{1,0:T(8,128)(2,1)} %collective-permute-done.17.refs_4_), channel_id=1, source_target_pairs={{0,8},{1,9},{2,10},{3,11},{4,12},{5,13},{6,14},{7,15},{8,0},{9,1},... | collective-permute-start | bytes 1179656 | tf_op jit(solution)/shard_map/ppermute | solution.py:28
  100.4 8.1 %collective-permute-start.24 = (bf16[128,1280]{1,0:T(8,128)(2,1)}, bf16[128,1280]{1,0:T(8,128)(2,1)}, u32[]{:S(2)}, u32[]{:S(2)}) collective-permute-start(bf16[128,1280]{1,0:T(8,128)(2,1)} %fusion.6.refs_0_), channel_id=1, source_target_pairs={{0,8},{1,9},{2,10},{3,11},{4,12},{5,13},{6,14},{7,15},{8,0},{9,1},... | collective-permute-start | bytes 983048 | tf_op jit(solution)/shard_map/ppermute | solution.py:28
  100.8 8.0 %collective-permute-start.25 = (bf16[128,1280]{1,0:T(8,128)(2,1)}, bf16[128,1280]{1,0:T(8,128)(2,1)}, u32[]{:S(2)}, u32[]{:S(2)}) collective-permute-start(bf16[128,1280]{1,0:T(8,128)(2,1)} %collective-permute-done.6.refs_2_), channel_id=1, source_target_pairs={{0,8},{1,9},{2,10},{3,11},{4,12},{5,13},{6,14},{7,15},{8,0},{9,1},... | collective-permute-start | bytes 983048 | tf_op jit(solution)/shard_map/ppermute | solution.py:28
  101.0 8.0 %collective-permute-start.26 = (bf16[128,1280]{1,0:T(8,128)(2,1)}, bf16[128,1280]{1,0:T(8,128)(2,1)}, u32[]{:S(2)}, u32[]{:S(2)}) collective-permute-start(bf16[128,1280]{1,0:T(8,128)(2,1)} %collective-permute-done.7.refs_4_), channel_id=1, source_target_pairs={{0,8},{1,9},{2,10},{3,11},{4,12},{5,13},{6,14},{7,15},{8,0},{9,1},... | collective-permute-start | bytes 983048 | tf_op jit(solution)/shard_map/ppermute | solution.py:28
  101.3 16.1 %all-to-all-start.1 = ((bf16[8,96,256]{2,1,0:T(8,128)(2,1)}), bf16[8,96,256]{2,1,0:T(8,128)(2,1)S(1)}, u32[]{:S(2)}, u32[]{:S(2)}) async-start(bf16[8,96,256]{2,1,0:T(8,128)(2,1)} %bitcast.30), calls=%async_computation.1 | async-start | bytes 786432 | tf_op jit(solution)/shard_map/all_to_all | solution.py:139
  107.9 2.0 collective-permute-start.27
  108.3 2.1 collective-permute-start.28
  108.4 2.4 %collective-permute-start.29 = (bf16[128,1280]{1,0:T(8,128)(2,1)}, bf16[128,1280]{1,0:T(8,128)(2,1)}, u32[]{:S(2)}, u32[]{:S(2)}) collective-permute-start(bf16[128,1280]{1,0:T(8,128)(2,1)} %collective-permute-done.18.refs_10_), channel_id=1, source_target_pairs={{0,8},{1,9},{2,10},{3,11},{4,12},{5,13},{6,14},{7,15},{8,0},{9,1},... | collective-permute-start | bytes 983048 | tf_op jit(solution)/shard_map/ppermute | solution.py:28
  108.8 2.5 %collective-permute-start.30 = (bf16[128,1280]{1,0:T(8,128)(2,1)}, bf16[128,1280]{1,0:T(8,128)(2,1)}, u32[]{:S(2)}, u32[]{:S(2)}) collective-permute-start(bf16[128,1280]{1,0:T(8,128)(2,1)} %copy-done.16), channel_id=1, source_target_pairs={{0,8},{1,9},{2,10},{3,11},{4,12},{5,13},{6,14},{7,15},{8,0},{9,1},... | collective-permute-start | bytes 983048 | tf_op jit(solution)/shard_map/ppermute | solution.py:28
  108.9 2.9 %collective-permute-start.31 = (bf16[128,1280]{1,0:T(8,128)(2,1)}, bf16[128,1280]{1,0:T(8,128)(2,1)}, u32[]{:S(2)}, u32[]{:S(2)}) collective-permute-start(bf16[128,1280]{1,0:T(8,128)(2,1)} %collective-permute-done.20.refs_14_), channel_id=1, source_target_pairs={{0,8},{1,9},{2,10},{3,11},{4,12},{5,13},{6,14},{7,15},{8,0},{9,1},... | collective-permute-start | bytes 983048 | tf_op jit(solution)/shard_map/ppermute | solution.py:28
  167.0 27.7 %copy-start.12 = (bf16[8,96,256]{2,1,0:T(8,128)(2,1)}, bf16[8,96,256]{2,1,0:T(8,128)(2,1)S(1)}, u32[]{:S(2)}) copy-start(bf16[8,96,256]{2,1,0:T(8,128)(2,1)S(1)} %slice.66) | copy-start | bytes 1179652
  167.0 8.7 %collective-permute-start.32 = (bf16[768,256]{1,0:T(8,128)(2,1)S(1)}, bf16[768,256]{1,0:T(8,128)(2,1)}, u32[]{:S(2)}, u32[]{:S(2)}) collective-permute-start(bf16[768,256]{1,0:T(8,128)(2,1)S(1)} %bitcast.55), channel_id=1, source_target_pairs={{0,16},{1,17},{2,18},{3,19},{4,20},{5,21},{6,22},{7,23},{8,24},{9,... | collective-permute-start | bytes 1179656 | tf_op jit(solution)/shard_map/ppermute | solution.py:28
  168.2 10.6 %collective-permute-start.33 = (bf16[768,256]{1,0:T(8,128)(2,1)S(1)}, bf16[768,256]{1,0:T(8,128)(2,1)}, u32[]{:S(2)}, u32[]{:S(2)}) collective-permute-start(bf16[768,256]{1,0:T(8,128)(2,1)S(1)} %bitcast.56), channel_id=1, source_target_pairs={{0,32},{1,33},{2,34},{3,35},{4,36},{5,37},{6,38},{7,39},{8,40},{9,... | collective-permute-start | bytes 1179656 | tf_op jit(solution)/shard_map/ppermute | solution.py:28
  168.7 10.2 %collective-permute-start.34 = (bf16[768,256]{1,0:T(8,128)(2,1)S(1)}, bf16[768,256]{1,0:T(8,128)(2,1)}, u32[]{:S(2)}, u32[]{:S(2)}) collective-permute-start(bf16[768,256]{1,0:T(8,128)(2,1)S(1)} %bitcast.57), channel_id=1, source_target_pairs={{0,96},{1,97},{2,98},{3,99},{4,100},{5,101},{6,102},{7,103},{8,104... | collective-permute-start | bytes 1179656 | tf_op jit(solution)/shard_map/ppermute | solution.py:28
  170.9 15.5 %collective-permute-start.35 = (bf16[768,256]{1,0:T(8,128)(2,1)S(1)}, bf16[768,256]{1,0:T(8,128)(2,1)}, u32[]{:S(2)}, u32[]{:S(2)}) collective-permute-start(bf16[768,256]{1,0:T(8,128)(2,1)S(1)} %bitcast.58), channel_id=1, source_target_pairs={{0,64},{1,65},{2,66},{3,67},{4,68},{5,69},{6,70},{7,71},{8,72},{9,... | collective-permute-start | bytes 1179656 | tf_op jit(solution)/shard_map/ppermute | solution.py:28
  170.9 25.6 %copy-start.11 = (f32[768,1,256]{2,1,0:T(1,128)S(1)}, f32[768,1,256]{2,1,0:T(1,128)}, u32[]{:S(2)}) copy-start(f32[768,1,256]{2,1,0:T(1,128)} %param.6) | copy-start | bytes 2359300
  171.0 23.7 %collective-permute-start.36 = (bf16[768,256]{1,0:T(8,128)(2,1)S(1)}, bf16[768,256]{1,0:T(8,128)(2,1)S(1)}, u32[]{:S(2)}, u32[]{:S(2)}) collective-permute-start(bf16[768,256]{1,0:T(8,128)(2,1)S(1)} %bitcast.59), channel_id=1, source_target_pairs={{0,8},{1,9},{2,10},{3,11},{4,12},{5,13},{6,14},{7,15},{8,0},{9,1},... | collective-permute-start | bytes 1179656 | tf_op jit(solution)/shard_map/ppermute | solution.py:28
  186.4 9.4 %collective-permute-start.37 = (bf16[768,256]{1,0:T(8,128)(2,1)}, bf16[768,256]{1,0:T(8,128)(2,1)S(1)}, u32[]{:S(2)}, u32[]{:S(2)}) collective-permute-start(bf16[768,256]{1,0:T(8,128)(2,1)} %collective-permute-done.32.refs_2_), channel_id=1, source_target_pairs={{0,8},{1,9},{2,10},{3,11},{4,12},{5,13},{6,14},{7,15},{8,0},{9,1},... | collective-permute-start | bytes 1179656 | tf_op jit(solution)/shard_map/ppermute | solution.py:28
  189.5 6.6 %collective-permute-start.38 = (bf16[768,256]{1,0:T(8,128)(2,1)}, bf16[768,256]{1,0:T(8,128)(2,1)S(1)}, u32[]{:S(2)}, u32[]{:S(2)}) collective-permute-start(bf16[768,256]{1,0:T(8,128)(2,1)} %collective-permute-done.33.refs_4_), channel_id=1, source_target_pairs={{0,8},{1,9},{2,10},{3,11},{4,12},{5,13},{6,14},{7,15},{8,0},{9,1},... | collective-permute-start | bytes 1179656 | tf_op jit(solution)/shard_map/ppermute | solution.py:28
  190.2 20.7 %collective-permute-start.41 = (bf16[768,256]{1,0:T(8,128)(2,1)}, bf16[768,256]{1,0:T(8,128)(2,1)S(1)}, u32[]{:S(2)}, u32[]{:S(2)}) collective-permute-start(bf16[768,256]{1,0:T(8,128)(2,1)} %collective-permute-done.32.refs_2_), channel_id=1, source_target_pairs={{0,32},{1,33},{2,34},{3,35},{4,36},{5,37},{6,38},{7,39},{8,40},{9,... | collective-permute-start | bytes 1179656 | tf_op jit(solution)/shard_map/ppermute | solution.py:28
  190.7 20.2 %collective-permute-start.42 = (bf16[768,256]{1,0:T(8,128)(2,1)}, bf16[768,256]{1,0:T(8,128)(2,1)S(1)}, u32[]{:S(2)}, u32[]{:S(2)}) collective-permute-start(bf16[768,256]{1,0:T(8,128)(2,1)} %collective-permute-done.32.refs_2_), channel_id=1, source_target_pairs={{0,96},{1,97},{2,98},{3,99},{4,100},{5,101},{6,102},{7,103},{8,104... | collective-permute-start | bytes 1179656 | tf_op jit(solution)/shard_map/ppermute | solution.py:28
  194.7 5.6 %collective-permute-start.40 = (bf16[768,256]{1,0:T(8,128)(2,1)}, bf16[768,256]{1,0:T(8,128)(2,1)S(1)}, u32[]{:S(2)}, u32[]{:S(2)}) collective-permute-start(bf16[768,256]{1,0:T(8,128)(2,1)} %collective-permute-done.35.refs_8_), channel_id=1, source_target_pairs={{0,8},{1,9},{2,10},{3,11},{4,12},{5,13},{6,14},{7,15},{8,0},{9,1},... | collective-permute-start | bytes 1179656 | tf_op jit(solution)/shard_map/ppermute | solution.py:28
  195.8 15.1 %collective-permute-start.43 = (bf16[768,256]{1,0:T(8,128)(2,1)}, bf16[768,256]{1,0:T(8,128)(2,1)S(1)}, u32[]{:S(2)}, u32[]{:S(2)}) collective-permute-start(bf16[768,256]{1,0:T(8,128)(2,1)} %collective-permute-done.35.refs_8_), channel_id=1, source_target_pairs={{0,16},{1,17},{2,18},{3,19},{4,20},{5,21},{6,22},{7,23},{8,24},{9,... | collective-permute-start | bytes 1179656 | tf_op jit(solution)/shard_map/ppermute | solution.py:28
  196.1 1.9 collective-permute-start.39
  198.1 5.6 %copy-start.28 = (bf16[768,256]{1,0:T(8,128)(2,1)}, bf16[768,256]{1,0:T(8,128)(2,1)S(1)}, u32[]{:S(2)}) copy-start(bf16[768,256]{1,0:T(8,128)(2,1)S(1)} %collective-permute-done.39.refs_7_) | copy-start | bytes 1179652
  198.1 13.6 %collective-permute-start.47 = (f32[1,256]{1,0:T(1,128)S(1)}, f32[1,256]{1,0:T(1,128)S(1)}, u32[]{:S(2)}, u32[]{:S(2)}) collective-permute-start(f32[1,256]{1,0:T(1,128)S(1)} %get-tuple-element.91), channel_id=1, source_target_pairs={{8,0},{16,8},{24,16},{32,24},{40,32},{48,40},{56,48},{64,56},{72,6... | collective-permute-start | bytes 3080 | tf_op jit(solution)/shard_map/ppermute | solution.py:431
  200.4 3.3 %copy-start.27 = (bf16[768,256]{1,0:T(8,128)(2,1)}, bf16[768,256]{1,0:T(8,128)(2,1)S(1)}, u32[]{:S(2)}) copy-start(bf16[768,256]{1,0:T(8,128)(2,1)S(1)} %collective-permute-done.40.refs_9_) | copy-start | bytes 1179652
  200.4 11.3 %collective-permute-start.48 = (f32[1,256]{1,0:T(1,128)S(1)}, f32[1,256]{1,0:T(1,128)S(1)}, u32[]{:S(2)}, u32[]{:S(2)}) collective-permute-start(f32[1,256]{1,0:T(1,128)S(1)} %get-tuple-element.90), channel_id=1, source_target_pairs={{0,8},{8,16},{16,24},{24,32},{32,40},{40,48},{48,56},{56,64},{64,7... | collective-permute-start | bytes 3080 | tf_op jit(solution)/shard_map/ppermute | solution.py:430
  210.9 1.8 collective-permute-start.44
  211.0 2.3 collective-permute-start.45
  211.5 2.3 collective-permute-start.46
  212.2 22.7 %copy-start.3 = (f32[768,1,256]{2,0,1:T(8,128)S(1)}, f32[768,1,256]{2,0,1:T(8,128)}, u32[]{:S(2)}) copy-start(f32[768,1,256]{2,0,1:T(8,128)} %copy-done.2) | copy-start | bytes 2359300
  (22 other events, 26.1 us)

commit v3 on v2

--- a/solution.py
+++ b/solution.py
@@ -35,21 +35,14 @@
 STEPS = [(0, 0), (0, 1), (1, 0), (-1, 0), (2, 0), (1, 1), (-1, 1), (2, 1)]
 
 
-def gather_geno(cells, kernel, *waiting, strip=None):
+def gather_geno(cells, kernel, *waiting, spread=False):
     geno = lax.axis_index("geno")
     y, z, core = geno // 4, geno // 2 % 2, geno % 2
     side, up = hop(cells, z=1), hop(cells, y=1)
     down, across = hop(cells, y=-1), hop(cells, y=2)
-    strips, later = [], []
-    if strip is not None:
-        strips = [hop(strip, **{name: by}) for name, by in (("far", 1), ("x", 1), ("x", -1), ("x", 2))]
-    side, up, down, across, kernel, *rest = together(
-        side, up, down, across, kernel, *waiting, *strips
-    )
-    waiting, strips = rest[: len(waiting)], rest[len(waiting) :]
-    if strip is not None:
+    side, up, down, across, kernel, *waiting = together(side, up, down, across, kernel, *waiting)
+    if spread:
         waiting = [swap(cells) for cells in waiting]
-        later = [hop(strips[0], x=by) for by in (1, -1, 2)] + waiting
         side_across = hop(side, y=2)
     else:
         side_across = hop(across, z=1)
@@ -62,16 +55,13 @@
     order = jnp.stack(order).astype(jnp.int32)
     pieces = [cells, others[0], side, others[1], up, others[2], down, others[3], across, others[4]]
     carry = mix_part(kernel, pieces, order[:10], None, F32)
-    carry, side_up, side_down, side_across, *later = together(
-        carry, side_up, side_down, side_across, *later
-    )
+    carry, side_up, side_down, side_across = together(carry, side_up, side_down, side_across)
     pieces = []
     for piece in (side_up, side_down, side_across):
         pieces += [piece, hop(piece, core=1)]
-    gathered = (kernel, pieces, order[10:], carry)
-    if strip is None:
-        return gathered, waiting
-    return gathered, later[3:], [strip] + strips + later[:3]
+    if spread:
+        pieces[0], *waiting = together(pieces[0], *waiting)
+    return (kernel, pieces, order[10:], carry), waiting
 
 
 STRIP = 5
@@ -235,27 +225,27 @@
 
 def fetch(order_ref, strip_refs, held, sems):
     copies = []
-    for k, strip_ref in enumerate(strip_refs):
-        here = order_ref[8] if k % 2 == 0 else 1 - order_ref[8]
-        target = held.at[k // 2, here]
-        copies.append(pltpu.make_async_copy(strip_ref, target, sems.at[k // 2, k % 2]))
+    for t in range(held.shape[0]):
+        for side, strip_ref in enumerate(strip_refs):
+            here = order_ref[0] if side == 0 else 1 - order_ref[0]
+            target = held.at[t, here]
+            copies.append(pltpu.make_async_copy(strip_ref.at[t], target, sems.at[t, side]))
     for copy in copies:
         copy.start()
     return copies
 
 
-def multiply(order_ref, left_ref, copies, held, total):
+def multiply(left_ref, copies, held, total):
     total[...] = jnp.zeros_like(total)
     count = left_ref.shape[0]
     cols = held.shape[3] // STRIP
-    for slot in range(count):
+    for t in range(count):
         for side in range(2):
-            copies[2 * slot + side].wait()
-        t = order_ref[slot]
+            copies[2 * t + side].wait()
         for r in range(STRIP):
-            other = lax.rem(t + r, count)
+            other = (t + r) % count
             at = slice(r * cols, (r + 1) * cols)
-            block = jnp.concatenate([held[slot, 0, :, at], held[slot, 1, :, at]], axis=0)
+            block = jnp.concatenate([held[t, 0, :, at], held[t, 1, :, at]], axis=0)
             total[other] += jnp.dot(left_ref[t], block, preferred_element_type=F32)
             if 0 < r < STRIP - 1:
                 total[t] += lax.dot_general(
@@ -273,7 +263,7 @@
         scratch_shapes=scratch
         + [
             pltpu.VMEM((count, part, cols), F32),
-            pltpu.VMEM((count, 2) + strips[0].shape, BF16),
+            pltpu.VMEM((count, 2) + strips[0].shape[1:], BF16),
             pltpu.SemaphoreType.DMA((count, 2)),
         ],
         compiler_params=pltpu.CompilerParams(vmem_limit_bytes=14 << 20),
@@ -289,11 +279,11 @@
     count, part, cols = mixed.shape
 
     def body(order_ref, mixed_ref, slab_ref, *refs):
-        image_ref, sums_ref, total, held, sems = refs[16:]
-        multiply(order_ref, mixed_ref, fetch(order_ref, refs[:16], held, sems), held, total)
+        image_ref, sums_ref, total, held, sems = refs[2:]
+        multiply(mixed_ref, fetch(order_ref, refs[:2], held, sems), held, total)
         sums = [jnp.zeros((part, cols), F32) for _ in range(3)]
         line = lax.broadcasted_iota(jnp.int32, (part, cols), 0)
-        first = order_ref[9]
+        first = order_ref[1]
         for t in range(count):
             right = right_of(slab_ref, t, part)
             extra = slab_ref[t, 3 * part :].astype(F32)
@@ -323,8 +313,8 @@
     count, part, cols = image.shape
 
     def body(order_ref, sums_ref, slab_ref, image_ref, *refs):
-        out_ref, factor_ref, left, total, held, sems = refs[16:]
-        copies = fetch(order_ref, refs[:16], held, sems)
+        out_ref, factor_ref, left, total, held, sems = refs[2:]
+        copies = fetch(order_ref, refs[:2], held, sems)
         sums = jnp.sum(sums_ref[...], axis=0)
         rr, ri, ii = sums[:, 0:1], sums[:, 1:2], sums[:, 2:3]
         alpha = rr / ri
@@ -338,7 +328,7 @@
             out_ref[t, part : 2 * part] = high
             out_ref[t, 2 * part :] = low
             left[t] = (seen_of(slab_ref, t, part) * direction).astype(BF16)
-        multiply(order_ref, left, copies, held, total)
+        multiply(left, copies, held, total)
         for t in range(count):
             out_ref[t, :part] = total[t].astype(BF16)
 
@@ -404,16 +394,14 @@
     below = lax.ppermute(right[:1], "geno", previous)
     slabs = pack(count, right, observed, field_coef[None], row_length[None], above, below)
     strip = strip_of(core, trial, kernel_trial)
-    gathered, (slabs,), strips = gather_geno(
-        (seen * right).astype(BF16), kernel_geno, slabs, strip=strip
+    strips = lax.all_gather(strip, "trial", axis=0)
+    gathered, (slabs,) = gather_geno(
+        (seen * right).astype(BF16), kernel_geno, slabs, spread=True
     )
-    mixed = mix_part(*gathered, BF16)
-    mixed, *strips = together(mixed, *strips)
+    mixed, strips = together(mix_part(*gathered, BF16), strips)
     mixed_r = swap(mixed.reshape(count, part, cols))
-    strips = [piece for own in strips for piece in (own, hop(own, core=1))]
-    x, far = trial // PAIR, trial % PAIR
-    order = [((x - a) % RING) * PAIR + (far + b) % PAIR for a, b in STEPS]
-    order = jnp.stack(order + [core, geno * rows + trial * part]).astype(jnp.int32)
+    strips = [strips, hop(strips, core=1)]
+    order = jnp.stack([core, geno * rows + trial * part]).astype(jnp.int32)
 
     image_r, sums = cross_first(order, mixed_r, slabs, strips, total_rows, devices)
     turned, factors = cross_second(order, exchange(sums), slabs, image_r, strips)

time: 237 us -> 224 us (0.945)
  starting transfers between devices: 70.6 us -> 55.3 us
  between operations: 1.19 us -> 14.6 us
  waiting for transfers between devices: 57.1 us -> 48.7 us
  local copies, waits for them, and re-layouts: 11.9 us -> 8.21 us
    ppermute x45 -> x31, waiting for transfers between devices: 50.6 us -> 31.3 us  [hop(): return lax.ppermute(cells, BOTH, pairs)]
    ppermute x45 -> x31, starting transfers between devices: 48.8 us -> 33.5 us  [hop(): return lax.ppermute(cells, BOTH, pairs)]
    all_gather x0 -> x1, waiting for transfers between devices: none -> 4.93 us  [on_device(): strips = lax.all_gather(strip, 'trial', axis=0)]
    all_to_all x2, waiting for transfers between devices: 5.6 us -> 9.08 us  [swap(): lax.all_to_all(slabs, 'trial', split_axis=0, concat_axis=0, tiled=True)]
    unnamed x71 -> x57, local copies, waits for them, and re-layouts: 9.17 us -> 6.53 us
  transfers between devices with their start and end apart: 51 -> 38, of which waited for: 22 -> 17; matrix products, arithmetic and copies ran while one was open for 2% -> 2% of each run, Pallas kernels for 6% -> 9%
where the time goes in v3:
time: 224 us
  starting transfers between devices  55.3 us (25%)
  blocking collectives  53.1 us (24%)
  waiting for transfers between devices  48.7 us (22%)
  Pallas kernels  38.5 us (17%)
  between operations  14.6 us (7%)
  local copies, waits for them, and re-layouts  8.21 us (4%)
  other arithmetic  5.39 us (2%)
    ppermute x31, starting transfers between devices, hop(): return lax.ppermute(cells, BOTH, pairs)  33.5 us
    all_to_all x2, blocking collectives, exchange(): return lax.all_to_all(rows, BOTH, 0, 0, tiled=True)  33 us
    ppermute x31, waiting for transfers between devices, hop(): return lax.ppermute(cells, BOTH, pairs)  31.3 us
    pallas_call x4, Pallas kernels, mix(): pl.pallas_call(body, out_shape=shapes, in_specs=[SMEM] + [HBM] * (1 + cou...  25.5 us
    all_to_all x1, blocking collectives, swap(): lax.all_to_all(slabs, 'trial', split_axis=0, concat_axis=0, tiled=True)  20.1 us
    pallas_call x2, Pallas kernels, cross_call(): pl.pallas_call(body, out_shape=shapes, in_specs=[SMEM if x.ndim == 1 else...  10.8 us
    all_to_all x2, starting transfers between devices, swap(): lax.all_to_all(slabs, 'trial', split_axis=0, concat_axis=0, tiled=True)  10.6 us
    all_to_all x2, waiting for transfers between devices, swap(): lax.all_to_all(slabs, 'trial', split_axis=0, concat_axis=0, tiled=True)  9.08 us
  transfers between devices with their start and end apart: 38, of which 17 were waited for; matrix products, arithmetic and copies ran while one was open for 2% of the time, Pallas kernels for 9%

profile of v3, /device:TPU:1, one launch (start us, length us, event | category | flops | bytes accessed | tf_op | source)
XLA Modules:
  0.0 223.8 jit_solution(17917572763251710212)
XLA Ops:
  7.2 1.2 copy-done
  8.4 0.8 constant_dynamic-slice_fusion.1
  9.3 1.9 fusion.6
  11.4 2.5 %collective-permute-start = (bf16[768,256]{1,0:T(8,128)(2,1)S(1)}, bf16[768,256]{1,0:T(8,128)(2,1)}, u32[]{:S(2)}, u32[]{:S(2)}) collective-permute-start(bf16[768,256]{1,0:T(8,128)(2,1)S(1)} %multiply_convert_fusion.refs_0_), channel_id=1, source_target_pairs={{0,16},{1,17},{2,18},{3,19},{4,20},{5,21},{6,22},{7,23},{8,24},{9,... | collective-permute-start | bytes 1179656 | tf_op jit(solution)/shard_map/ppermute | solution.py:28
  13.9 1.3 collective-permute-start.1
  15.2 1.4 collective-permute-start.2
  16.7 1.6 collective-permute-start.3
  18.3 3.4 %collective-permute-start.4 = (f32[1,256]{1,0:T(1,128)S(1)}, f32[1,256]{1,0:T(1,128)S(1)}, u32[]{:S(2)}, u32[]{:S(2)}) collective-permute-start(f32[1,256]{1,0:T(1,128)S(1)} %get-tuple-element.67), channel_id=1, source_target_pairs={{0,8},{8,16},{16,24},{24,32},{32,40},{40,48},{48,56},{56,64},{64,7... | collective-permute-start | bytes 3080 | tf_op jit(solution)/shard_map/ppermute | solution.py:393
  21.7 0.7 collective-permute-done.4.above_ref
  22.4 1.9 collective-permute-start.5
  24.4 1.2 copy.18
  25.6 2.7 %collective-permute-done.5.below_ref = f32[1,256]{1,0:T(1,128)S(1)} collective-permute-done((f32[1,256]{1,0:T(1,128)S(1)}, f32[1,256]{1,0:T(1,128)S(1)}, u32[]{:S(2)}, u32[]{:S(2)}) %collective-permute-start.5) | collective-permute-done | bytes 1056 | tf_op jit(solution)/shard_map/ppermute | solution.py:394
  28.6 1.0 copy-done.4
  29.7 4.9 %collective-permute-done.3.refs_8_ = bf16[768,256]{1,0:T(8,128)(2,1)} collective-permute-done((bf16[768,256]{1,0:T(8,128)(2,1)S(1)}, bf16[768,256]{1,0:T(8,128)(2,1)}, u32[]{:S(2)}, u32[]{:S(2)}) %collective-permute-start.3) | collective-permute-done | bytes 393248 | tf_op jit(solution)/shard_map/ppermute | solution.py:28
  34.6 1.9 collective-permute-start.7
  36.5 7.0 %all-to-all-start = ((bf16[8,304,256]{2,1,0:T(8,128)(2,1)}), bf16[8,304,256]{2,1,0:T(8,128)(2,1)S(1)}, u32[]{:S(2)}, u32[]{:S(2)}) async-start(bf16[8,304,256]{2,1,0:T(8,128)(2,1)} %copy-done.4), calls=%async_computation | async-start | bytes 2490368 | tf_op jit(solution)/shard_map/all_to_all | solution.py:129
  43.5 0.8 collective-permute-start.8
  44.3 3.2 %collective-permute-start.11 = (bf16[768,256]{1,0:T(8,128)(2,1)}, bf16[768,256]{1,0:T(8,128)(2,1)S(1)}, u32[]{:S(2)}, u32[]{:S(2)}) collective-permute-start(bf16[768,256]{1,0:T(8,128)(2,1)} %collective-permute-done.refs_2_), channel_id=1, source_target_pairs={{0,32},{1,33},{2,34},{3,35},{4,36},{5,37},{6,38},{7,39},{8,40},{9,... | collective-permute-start | bytes 1179656 | tf_op jit(solution)/shard_map/ppermute | solution.py:28
  47.6 1.5 collective-permute-start.12
  49.0 1.2 collective-permute-start.13
  50.3 7.2 %shard_map.78.refs_6_ = f32[768,256]{1,0:T(8,128)S(1)} custom-call(s32[10]{0:T(128)S(1)} %stack.99.order_ref, bf16[768,12288]{1,0:T(8,128)(2,1)} %kernel_ref.3, bf16[768,256]{1,0:T(8,128)(2,1)} %copy-done.13, bf16[768,256]{1,0:T(8,128)(2,1)} %collective-permute-done.6.refs_1_, bf16[768,256]{1,0:T(8,128)(2,1)} %collective-permute-done.refs_2_, ...), custom_call_target="tpu_custom_call" | custom-call | tf_op jit(solution)/shard_map/pallas_call | solution.py:182
  57.5 0.9 copy-done.5
  58.6 9.3 %collective-permute-done.13.refs_4_ = bf16[768,256]{1,0:T(8,128)(2,1)} collective-permute-done((bf16[768,256]{1,0:T(8,128)(2,1)}, bf16[768,256]{1,0:T(8,128)(2,1)}, u32[]{:S(2)}, u32[]{:S(2)}) %collective-permute-start.13) | collective-permute-done | bytes 393248 | tf_op jit(solution)/shard_map/ppermute | solution.py:28
  67.8 1.1 collective-permute-start.14
  69.0 0.5 collective-permute-start.16
  69.6 1.4 collective-permute-done.14.refs_1_
  71.2 0.6 collective-permute-done.16.refs_5_
  71.8 1.1 copy-done.6
  72.9 5.9 %shard_map.79 = bf16[768,256]{1,0:T(8,128)(2,1)} custom-call(s32[6]{0:T(128)S(1)} %stack.85.order_ref, bf16[768,12288]{1,0:T(8,128)(2,1)} %kernel_ref.3, bf16[768,256]{1,0:T(8,128)(2,1)} %copy-done.14, bf16[768,256]{1,0:T(8,128)(2,1)} %collective-permute-done.14.refs_1_, bf16[768,256]{1,0:T(8,128)(2,1)} %collective-permute-done.12.refs_2_, ...), custom_call_target="tpu_custom_call" | custom-call | tf_op jit(solution)/shard_map/pallas_call | solution.py:182
  78.8 4.9 %all-gather.3.cloned.1.call-done = bf16[1024,1280]{1,0:T(8,128)(2,1)} async-done(((bf16[128,1280]{1,0:T(8,128)(2,1)}), bf16[1024,1280]{1,0:T(8,128)(2,1)}) %all-gather.3.cloned.1.call-update) | async-done | bytes 2621456 | tf_op jit(solution)/shard_map/all_gather | solution.py:397
  83.7 0.9 collective-permute-start.17
  84.6 3.6 %all-to-all-start.1 = ((bf16[8,96,256]{2,1,0:T(8,128)(2,1)}), bf16[8,96,256]{2,1,0:T(8,128)(2,1)S(1)}, u32[]{:S(2)}, u32[]{:S(2)}) async-start(bf16[8,96,256]{2,1,0:T(8,128)(2,1)} %bitcast.23), calls=%async_computation.1 | async-start | bytes 786432 | tf_op jit(solution)/shard_map/all_to_all | solution.py:129
  88.3 9.1 %all-to-all-done.1.mixed_ref = bf16[8,96,256]{2,1,0:T(8,128)(2,1)S(1)} async-done(((bf16[8,96,256]{2,1,0:T(8,128)(2,1)}), bf16[8,96,256]{2,1,0:T(8,128)(2,1)S(1)}, u32[]{:S(2)}, u32[]{:S(2)}) %all-to-all-start.1) | async-done | bytes 393248 | tf_op jit(solution)/shard_map/all_to_all | solution.py:129
  97.4 5.8 %shard_map.80 = (f32[8,96,256]{2,1,0:T(8,128)S(1)}, f32[128,1,128]{2,1,0:T(1,128)S(1)}) custom-call(s32[2]{0:T(128)S(1)} %pad_add_fusion.order_ref, bf16[8,96,256]{2,1,0:T(8,128)(2,1)S(1)} %all-to-all-done.1.mixed_ref, bf16[8,304,256]{2,1,0:T(8,128)(2,1)S(1)} %all-to-all-done.slab_ref, bf16[8,128,1280]{2,1,0:T(8,128)(2,1)} %bitcast.49, ...), custom_call_target="tpu_custom_call" | custom-call | flops 805306368 | bytes 8388608 | tf_op jit(solution)/shard_map/pallas_call | solution.py:258
  103.2 18.9 %all_to_all.25.sums_ref = f32[128,1,128]{2,1,0:T(1,128)S(1)} all-to-all(f32[128,1,128]{2,1,0:T(1,128)S(1)} %get-tuple-element.46), channel_id=1, replica_groups=mesh['geno'=16,'trial'=8] {'geno','trial'}, dimensions={0} | all-to-all | bytes 131072 | tf_op jit(solution)/shard_map/all_to_all | solution.py:133
  122.1 5.0 %shard_map.81 = (bf16[8,288,256]{2,1,0:T(8,128)(2,1)S(1)}, f32[1,128]{1,0:T(1,128)S(1)}) custom-call(s32[2]{0:T(128)S(1)} %pad_add_fusion.order_ref, f32[128,1,128]{2,1,0:T(1,128)S(1)} %all_to_all.25.sums_ref, bf16[8,304,256]{2,1,0:T(8,128)(2,1)S(1)} %all-to-all-done.slab_ref, f32[8,96,256]{2,1,0:T(8,128)S(1)} %get-tuple-element.47.image_ref, ...), custom_call_target="tpu_custom_call" | custom-call | flops 805306368 | bytes 8388608 | tf_op jit(solution)/shard_map/pallas_call | solution.py:258
  127.1 20.1 %all_to_all.26 = bf16[8,288,256]{2,1,0:T(8,128)(2,1)S(1)} all-to-all(bf16[8,288,256]{2,1,0:T(8,128)(2,1)S(1)} %get-tuple-element.48), channel_id=1, replica_groups=mesh['geno'=16,'trial'=8] {'trial'}, dimensions={0} | all-to-all | bytes 2359296 | tf_op jit(solution)/shard_map/all_to_all | solution.py:129
  147.5 0.7 collective-permute-start.19
  148.1 2.0 collective-permute-start.20
  150.2 3.0 %collective-permute-start.22 = (bf16[768,256]{1,0:T(8,128)(2,1)S(1)}, bf16[768,256]{1,0:T(8,128)(2,1)S(1)}, u32[]{:S(2)}, u32[]{:S(2)}) collective-permute-start(bf16[768,256]{1,0:T(8,128)(2,1)S(1)} %bitcast.55), channel_id=1, source_target_pairs={{0,8},{1,9},{2,10},{3,11},{4,12},{5,13},{6,14},{7,15},{8,0},{9,1},... | collective-permute-start | bytes 1179656 | tf_op jit(solution)/shard_map/ppermute | solution.py:28
  153.2 2.6 %collective-permute-done.18.refs_2_ = bf16[768,256]{1,0:T(8,128)(2,1)} collective-permute-done((bf16[768,256]{1,0:T(8,128)(2,1)S(1)}, bf16[768,256]{1,0:T(8,128)(2,1)}, u32[]{:S(2)}, u32[]{:S(2)}) %collective-permute-start.18) | collective-permute-done | bytes 393248 | tf_op jit(solution)/shard_map/ppermute | solution.py:28
  155.8 1.2 collective-permute-done.19.refs_4_
  157.1 8.3 %collective-permute-done.21.refs_8_ = bf16[768,256]{1,0:T(8,128)(2,1)} collective-permute-done((bf16[768,256]{1,0:T(8,128)(2,1)S(1)}, bf16[768,256]{1,0:T(8,128)(2,1)}, u32[]{:S(2)}, u32[]{:S(2)}) %collective-permute-start.21) | collective-permute-done | bytes 393248 | tf_op jit(solution)/shard_map/ppermute | solution.py:28
  165.4 3.3 %collective-permute-start.23 = (bf16[768,256]{1,0:T(8,128)(2,1)}, bf16[768,256]{1,0:T(8,128)(2,1)S(1)}, u32[]{:S(2)}, u32[]{:S(2)}) collective-permute-start(bf16[768,256]{1,0:T(8,128)(2,1)} %collective-permute-done.18.refs_2_), channel_id=1, source_target_pairs={{0,8},{1,9},{2,10},{3,11},{4,12},{5,13},{6,14},{7,15},{8,0},{9,1},... | collective-permute-start | bytes 1179656 | tf_op jit(solution)/shard_map/ppermute | solution.py:28
  168.8 0.6 fusion.13
  169.5 0.5 collective-permute-start.27
  170.0 2.2 collective-permute-start.28
  172.1 1.9 add_multiply_fusion
  174.1 1.1 collective-permute-start.26
  175.2 1.3 collective-permute-start.29
  176.9 0.7 bitcast_subtract_fusion
  177.6 0.8 collective-permute-done.25.refs_7_
  178.4 2.3 %collective-permute-start.33 = (f32[1,256]{1,0:T(1,128)S(1)}, f32[1,256]{1,0:T(1,128)S(1)}, u32[]{:S(2)}, u32[]{:S(2)}) collective-permute-start(f32[1,256]{1,0:T(1,128)S(1)} %get-tuple-element.65), channel_id=1, source_target_pairs={{8,0},{16,8},{24,16},{32,24},{40,32},{48,40},{56,48},{64,56},{72,6... | collective-permute-start | bytes 3080 | tf_op jit(solution)/shard_map/ppermute | solution.py:419
  180.7 3.5 %collective-permute-start.34 = (f32[1,256]{1,0:T(1,128)S(1)}, f32[1,256]{1,0:T(1,128)S(1)}, u32[]{:S(2)}, u32[]{:S(2)}) collective-permute-start(f32[1,256]{1,0:T(1,128)S(1)} %get-tuple-element.64), channel_id=1, source_target_pairs={{0,8},{8,16},{16,24},{24,32},{32,40},{40,48},{48,56},{56,64},{64,7... | collective-permute-start | bytes 3080 | tf_op jit(solution)/shard_map/ppermute | solution.py:418
  184.3 7.2 %shard_map.82.refs_6_ = f32[768,256]{1,0:T(8,128)S(1)} custom-call(s32[10]{0:T(128)S(1)} %stack.99.order_ref, bf16[768,12288]{1,0:T(8,128)(2,1)} %kernel_ref.3, bf16[768,256]{1,0:T(8,128)(2,1)} %bitcast.56, bf16[768,256]{1,0:T(8,128)(2,1)} %copy-done.17, bf16[768,256]{1,0:T(8,128)(2,1)} %collective-permute-done.18.refs_2_, bf16[768,256]{1,0:T(8,128)(2,1)} %copy-done.18, ...), custom_call_target="tpu_custom_call" | custom-call | tf_op jit(solution)/shard_map/pallas_call | solution.py:182
  191.6 0.5 collective-permute-start.31
  192.2 0.4 fusion.2
  192.8 0.5 collective-permute-done.30.refs_1_
  193.3 0.6 collective-permute-done.31.refs_3_
  193.9 0.6 collective-permute-done.32.refs_5_
  194.7 0.8 copy-done.27
  195.4 5.4 %shard_map.83 = (f32[768,256]{1,0:T(8,128)S(1)}, f32[128,1,128]{2,1,0:T(1,128)S(1)}) custom-call(s32[6]{0:T(128)S(1)} %stack.85.order_ref, bf16[768,12288]{1,0:T(8,128)(2,1)} %kernel_ref.3, bf16[768,256]{1,0:T(8,128)(2,1)} %copy-done.22, bf16[768,256]{1,0:T(8,128)(2,1)} %copy-done.25, bf16[768,256]{1,0:T(8,128)(2,1)} %copy-done.23, ...), custom_call_target="tpu_custom_call" | custom-call | tf_op jit(solution)/shard_map/pallas_call | solution.py:182
  200.8 14.2 %all_to_all.27.sums_ref = f32[128,1,128]{2,1,0:T(1,128)S(1)} all-to-all(f32[128,1,128]{2,1,0:T(1,128)S(1)} %get-tuple-element.60), channel_id=1, replica_groups=mesh['geno'=16,'trial'=8] {'geno','trial'}, dimensions={0} | all-to-all | bytes 131072 | tf_op jit(solution)/shard_map/all_to_all | solution.py:133
  215.0 1.9 shard_map.84
  (101 shorter events, 2.7 us)
Async XLA Ops:
  7.2 1.2 copy-start
  7.2 76.5 %all-gather.3.cloned.1.call-start = ((), (), s32[]{:S(2)}) async-start(), calls=%async_computation.5 | async-start | bytes 2949120 | tf_op jit(solution)/shard_map/all_gather | solution.py:397
  9.2 2.0 copy-start.1
  9.2 2.0 copy-start.9
  11.4 17.2 %copy-start.13 = (bf16[768,256]{1,0:T(8,128)(2,1)}, bf16[768,256]{1,0:T(8,128)(2,1)S(1)}, u32[]{:S(2)}) copy-start(bf16[768,256]{1,0:T(8,128)(2,1)S(1)} %multiply_convert_fusion.refs_0_) | copy-start | bytes 1179652
  11.4 17.0 %copy-start.7 = (f32[256]{0:T(256)S(1)}, f32[256]{0:T(256)}, u32[]{:S(2)}) copy-start(f32[256]{0:T(256)} %param.9) | copy-start | bytes 3076
  11.4 17.0 %copy-start.8 = (s32[256]{0:T(256)S(1)}, s32[256]{0:T(256)}, u32[]{:S(2)}) copy-start(s32[256]{0:T(256)} %param.8) | copy-start | bytes 3076
  11.4 18.2 %collective-permute-start = (bf16[768,256]{1,0:T(8,128)(2,1)S(1)}, bf16[768,256]{1,0:T(8,128)(2,1)}, u32[]{:S(2)}, u32[]{:S(2)}) collective-permute-start(bf16[768,256]{1,0:T(8,128)(2,1)S(1)} %multiply_convert_fusion.refs_0_), channel_id=1, source_target_pairs={{0,16},{1,17},{2,18},{3,19},{4,20},{5,21},{6,22},{7,23},{8,24},{9,... | collective-permute-start | bytes 1179656 | tf_op jit(solution)/shard_map/ppermute | solution.py:28
  13.9 15.7 %collective-permute-start.1 = (bf16[768,256]{1,0:T(8,128)(2,1)S(1)}, bf16[768,256]{1,0:T(8,128)(2,1)S(1)}, u32[]{:S(2)}, u32[]{:S(2)}) collective-permute-start(bf16[768,256]{1,0:T(8,128)(2,1)S(1)} %multiply_convert_fusion.refs_0_), channel_id=1, source_target_pairs={{0,32},{1,33},{2,34},{3,35},{4,36},{5,37},{6,38},{7,39},{8,40},{9,... | collective-permute-start | bytes 1179656 | tf_op jit(solution)/shard_map/ppermute | solution.py:28
  15.2 14.4 %collective-permute-start.2 = (bf16[768,256]{1,0:T(8,128)(2,1)S(1)}, bf16[768,256]{1,0:T(8,128)(2,1)S(1)}, u32[]{:S(2)}, u32[]{:S(2)}) collective-permute-start(bf16[768,256]{1,0:T(8,128)(2,1)S(1)} %multiply_convert_fusion.refs_0_), channel_id=1, source_target_pairs={{0,96},{1,97},{2,98},{3,99},{4,100},{5,101},{6,102},{7,103},{8,104... | collective-permute-start | bytes 1179656 | tf_op jit(solution)/shard_map/ppermute | solution.py:28
  16.7 17.9 %collective-permute-start.3 = (bf16[768,256]{1,0:T(8,128)(2,1)S(1)}, bf16[768,256]{1,0:T(8,128)(2,1)}, u32[]{:S(2)}, u32[]{:S(2)}) collective-permute-start(bf16[768,256]{1,0:T(8,128)(2,1)S(1)} %multiply_convert_fusion.refs_0_), channel_id=1, source_target_pairs={{0,64},{1,65},{2,66},{3,67},{4,68},{5,69},{6,70},{7,71},{8,72},{9,... | collective-permute-start | bytes 1179656 | tf_op jit(solution)/shard_map/ppermute | solution.py:28
  18.3 4.1 %collective-permute-start.4 = (f32[1,256]{1,0:T(1,128)S(1)}, f32[1,256]{1,0:T(1,128)S(1)}, u32[]{:S(2)}, u32[]{:S(2)}) collective-permute-start(f32[1,256]{1,0:T(1,128)S(1)} %get-tuple-element.67), channel_id=1, source_target_pairs={{0,8},{8,16},{16,24},{24,32},{32,40},{40,48},{48,56},{56,64},{64,7... | collective-permute-start | bytes 3080 | tf_op jit(solution)/shard_map/ppermute | solution.py:393
  22.4 5.9 %collective-permute-start.5 = (f32[1,256]{1,0:T(1,128)S(1)}, f32[1,256]{1,0:T(1,128)S(1)}, u32[]{:S(2)}, u32[]{:S(2)}) collective-permute-start(f32[1,256]{1,0:T(1,128)S(1)} %get-tuple-element.66), channel_id=1, source_target_pairs={{8,0},{16,8},{24,16},{32,24},{40,32},{48,40},{56,48},{64,56},{72,6... | collective-permute-start | bytes 3080 | tf_op jit(solution)/shard_map/ppermute | solution.py:394
  25.6 3.0 %copy-start.2 = (f32[768,1,256]{2,0,1:T(8,128)}, f32[768,1,256]{2,0,1:T(8,128)S(1)}, u32[]{:S(2)}) copy-start(f32[768,1,256]{2,0,1:T(8,128)S(1)} %copy.18) | copy-start | bytes 2359300
  28.3 16.0 %collective-permute-start.6 = (bf16[768,256]{1,0:T(8,128)(2,1)S(1)}, bf16[768,256]{1,0:T(8,128)(2,1)}, u32[]{:S(2)}, u32[]{:S(2)}) collective-permute-start(bf16[768,256]{1,0:T(8,128)(2,1)S(1)} %multiply_convert_fusion.refs_0_), channel_id=1, source_target_pairs={{0,8},{1,9},{2,10},{3,11},{4,12},{5,13},{6,14},{7,15},{8,0},{9,1},... | collective-permute-start | bytes 1179656 | tf_op jit(solution)/shard_map/ppermute | solution.py:28
  28.6 1.1 copy-start.4
  29.6 6.8 %copy-start.15 = (bf16[768,256]{1,0:T(8,128)(2,1)}, bf16[768,256]{1,0:T(8,128)(2,1)S(1)}, u32[]{:S(2)}) copy-start(bf16[768,256]{1,0:T(8,128)(2,1)S(1)} %collective-permute-done.1.refs_4_) | copy-start | bytes 1179652
  29.6 5.0 %copy-start.16 = (bf16[768,256]{1,0:T(8,128)(2,1)}, bf16[768,256]{1,0:T(8,128)(2,1)S(1)}, u32[]{:S(2)}) copy-start(bf16[768,256]{1,0:T(8,128)(2,1)S(1)} %collective-permute-done.2.refs_6_) | copy-start | bytes 1179652
  34.6 13.0 %collective-permute-start.7 = (bf16[768,256]{1,0:T(8,128)(2,1)}, bf16[768,256]{1,0:T(8,128)(2,1)}, u32[]{:S(2)}, u32[]{:S(2)}) collective-permute-start(bf16[768,256]{1,0:T(8,128)(2,1)} %collective-permute-done.refs_2_), channel_id=1, source_target_pairs={{0,8},{1,9},{2,10},{3,11},{4,12},{5,13},{6,14},{7,15},{8,0},{9,1},... | collective-permute-start | bytes 1179656 | tf_op jit(solution)/shard_map/ppermute | solution.py:28
  36.5 12.6 %collective-permute-start.10 = (bf16[768,256]{1,0:T(8,128)(2,1)}, bf16[768,256]{1,0:T(8,128)(2,1)}, u32[]{:S(2)}, u32[]{:S(2)}) collective-permute-start(bf16[768,256]{1,0:T(8,128)(2,1)} %collective-permute-done.3.refs_8_), channel_id=1, source_target_pairs={{0,8},{1,9},{2,10},{3,11},{4,12},{5,13},{6,14},{7,15},{8,0},{9,1},... | collective-permute-start | bytes 1179656 | tf_op jit(solution)/shard_map/ppermute | solution.py:28
  36.5 33.1 %all-to-all-start = ((bf16[8,304,256]{2,1,0:T(8,128)(2,1)}), bf16[8,304,256]{2,1,0:T(8,128)(2,1)S(1)}, u32[]{:S(2)}, u32[]{:S(2)}) async-start(bf16[8,304,256]{2,1,0:T(8,128)(2,1)} %copy-done.4), calls=%async_computation | async-start | bytes 2490368 | tf_op jit(solution)/shard_map/all_to_all | solution.py:129
  43.5 6.9 %collective-permute-start.8 = (bf16[768,256]{1,0:T(8,128)(2,1)}, bf16[768,256]{1,0:T(8,128)(2,1)}, u32[]{:S(2)}, u32[]{:S(2)}) collective-permute-start(bf16[768,256]{1,0:T(8,128)(2,1)} %copy-done.15), channel_id=1, source_target_pairs={{0,8},{1,9},{2,10},{3,11},{4,12},{5,13},{6,14},{7,15},{8,0},{9,1},... | collective-permute-start | bytes 1179656 | tf_op jit(solution)/shard_map/ppermute | solution.py:28
  44.3 6.1 %collective-permute-start.9 = (bf16[768,256]{1,0:T(8,128)(2,1)}, bf16[768,256]{1,0:T(8,128)(2,1)}, u32[]{:S(2)}, u32[]{:S(2)}) collective-permute-start(bf16[768,256]{1,0:T(8,128)(2,1)} %copy-done.16), channel_id=1, source_target_pairs={{0,8},{1,9},{2,10},{3,11},{4,12},{5,13},{6,14},{7,15},{8,0},{9,1},... | collective-permute-start | bytes 1179656 | tf_op jit(solution)/shard_map/ppermute | solution.py:28
  44.3 14.2 %collective-permute-start.11 = (bf16[768,256]{1,0:T(8,128)(2,1)}, bf16[768,256]{1,0:T(8,128)(2,1)S(1)}, u32[]{:S(2)}, u32[]{:S(2)}) collective-permute-start(bf16[768,256]{1,0:T(8,128)(2,1)} %collective-permute-done.refs_2_), channel_id=1, source_target_pairs={{0,32},{1,33},{2,34},{3,35},{4,36},{5,37},{6,38},{7,39},{8,40},{9,... | collective-permute-start | bytes 1179656 | tf_op jit(solution)/shard_map/ppermute | solution.py:28
  47.6 11.0 %collective-permute-start.12 = (bf16[768,256]{1,0:T(8,128)(2,1)}, bf16[768,256]{1,0:T(8,128)(2,1)}, u32[]{:S(2)}, u32[]{:S(2)}) collective-permute-start(bf16[768,256]{1,0:T(8,128)(2,1)} %collective-permute-done.refs_2_), channel_id=1, source_target_pairs={{0,96},{1,97},{2,98},{3,99},{4,100},{5,101},{6,102},{7,103},{8,104... | collective-permute-start | bytes 1179656 | tf_op jit(solution)/shard_map/ppermute | solution.py:28
  49.0 18.8 %collective-permute-start.13 = (bf16[768,256]{1,0:T(8,128)(2,1)}, bf16[768,256]{1,0:T(8,128)(2,1)}, u32[]{:S(2)}, u32[]{:S(2)}) collective-permute-start(bf16[768,256]{1,0:T(8,128)(2,1)} %collective-permute-done.refs_2_), channel_id=1, source_target_pairs={{0,64},{1,65},{2,66},{3,67},{4,68},{5,69},{6,70},{7,71},{8,72},{9,... | collective-permute-start | bytes 1179656 | tf_op jit(solution)/shard_map/ppermute | solution.py:28
  57.5 0.9 copy-start.5
  58.6 13.2 %copy-start.14 = (bf16[768,256]{1,0:T(8,128)(2,1)}, bf16[768,256]{1,0:T(8,128)(2,1)S(1)}, u32[]{:S(2)}) copy-start(bf16[768,256]{1,0:T(8,128)(2,1)S(1)} %collective-permute-done.11.refs_0_) | copy-start | bytes 1179652
  67.8 3.1 %collective-permute-start.14 = (bf16[768,256]{1,0:T(8,128)(2,1)S(1)}, bf16[768,256]{1,0:T(8,128)(2,1)}, u32[]{:S(2)}, u32[]{:S(2)}) collective-permute-start(bf16[768,256]{1,0:T(8,128)(2,1)S(1)} %collective-permute-done.11.refs_0_), channel_id=1, source_target_pairs={{0,8},{1,9},{2,10},{3,11},{4,12},{5,13},{6,14},{7,15},{8,0},{9,1},... | collective-permute-start | bytes 1179656 | tf_op jit(solution)/shard_map/ppermute | solution.py:28
  69.0 2.3 %collective-permute-start.15 = (bf16[768,256]{1,0:T(8,128)(2,1)}, bf16[768,256]{1,0:T(8,128)(2,1)}, u32[]{:S(2)}, u32[]{:S(2)}) collective-permute-start(bf16[768,256]{1,0:T(8,128)(2,1)} %collective-permute-done.12.refs_2_), channel_id=1, source_target_pairs={{0,8},{1,9},{2,10},{3,11},{4,12},{5,13},{6,14},{7,15},{8,0},{9,1},... | collective-permute-start | bytes 1179656 | tf_op jit(solution)/shard_map/ppermute | solution.py:28
  69.0 2.8 %collective-permute-start.16 = (bf16[768,256]{1,0:T(8,128)(2,1)}, bf16[768,256]{1,0:T(8,128)(2,1)}, u32[]{:S(2)}, u32[]{:S(2)}) collective-permute-start(bf16[768,256]{1,0:T(8,128)(2,1)} %collective-permute-done.13.refs_4_), channel_id=1, source_target_pairs={{0,8},{1,9},{2,10},{3,11},{4,12},{5,13},{6,14},{7,15},{8,0},{9,1},... | collective-permute-start | bytes 1179656 | tf_op jit(solution)/shard_map/ppermute | solution.py:28
  71.8 1.1 copy-start.6
  83.7 13.7 %collective-permute-start.17 = (bf16[8,128,1280]{2,1,0:T(8,128)(2,1)}, bf16[8,128,1280]{2,1,0:T(8,128)(2,1)}, u32[]{:S(2)}, u32[]{:S(2)}) collective-permute-start(bf16[8,128,1280]{2,1,0:T(8,128)(2,1)} %bitcast.48), channel_id=1, source_target_pairs={{0,8},{1,9},{2,10},{3,11},{4,12},{5,13},{6,14},{7,15},{8,0},{9,1},... | collective-permute-start | bytes 7864328 | tf_op jit(solution)/shard_map/ppermute | solution.py:28
  84.6 12.8 %all-to-all-start.1 = ((bf16[8,96,256]{2,1,0:T(8,128)(2,1)}), bf16[8,96,256]{2,1,0:T(8,128)(2,1)S(1)}, u32[]{:S(2)}, u32[]{:S(2)}) async-start(bf16[8,96,256]{2,1,0:T(8,128)(2,1)} %bitcast.23), calls=%async_computation.1 | async-start | bytes 786432 | tf_op jit(solution)/shard_map/all_to_all | solution.py:129
  147.2 3.0 %copy-start.11 = (bf16[8,288,256]{2,1,0:T(8,128)(2,1)}, bf16[8,288,256]{2,1,0:T(8,128)(2,1)S(1)}, u32[]{:S(2)}) copy-start(bf16[8,288,256]{2,1,0:T(8,128)(2,1)S(1)} %all_to_all.26) | copy-start | bytes 3538948
  147.2 26.8 %copy-start.12 = (bf16[8,96,256]{2,1,0:T(8,128)(2,1)}, bf16[8,96,256]{2,1,0:T(8,128)(2,1)S(1)}, u32[]{:S(2)}) copy-start(bf16[8,96,256]{2,1,0:T(8,128)(2,1)S(1)} %slice.66) | copy-start | bytes 1179652
  147.2 8.6 %collective-permute-start.18 = (bf16[768,256]{1,0:T(8,128)(2,1)S(1)}, bf16[768,256]{1,0:T(8,128)(2,1)}, u32[]{:S(2)}, u32[]{:S(2)}) collective-permute-start(bf16[768,256]{1,0:T(8,128)(2,1)S(1)} %bitcast.51), channel_id=1, source_target_pairs={{0,16},{1,17},{2,18},{3,19},{4,20},{5,21},{6,22},{7,23},{8,24},{9,... | collective-permute-start | bytes 1179656 | tf_op jit(solution)/shard_map/ppermute | solution.py:28
  147.5 9.6 %collective-permute-start.19 = (bf16[768,256]{1,0:T(8,128)(2,1)S(1)}, bf16[768,256]{1,0:T(8,128)(2,1)}, u32[]{:S(2)}, u32[]{:S(2)}) collective-permute-start(bf16[768,256]{1,0:T(8,128)(2,1)S(1)} %bitcast.52), channel_id=1, source_target_pairs={{0,32},{1,33},{2,34},{3,35},{4,36},{5,37},{6,38},{7,39},{8,40},{9,... | collective-permute-start | bytes 1179656 | tf_op jit(solution)/shard_map/ppermute | solution.py:28
  148.1 9.0 %collective-permute-start.20 = (bf16[768,256]{1,0:T(8,128)(2,1)S(1)}, bf16[768,256]{1,0:T(8,128)(2,1)}, u32[]{:S(2)}, u32[]{:S(2)}) collective-permute-start(bf16[768,256]{1,0:T(8,128)(2,1)S(1)} %bitcast.53), channel_id=1, source_target_pairs={{0,96},{1,97},{2,98},{3,99},{4,100},{5,101},{6,102},{7,103},{8,104... | collective-permute-start | bytes 1179656 | tf_op jit(solution)/shard_map/ppermute | solution.py:28
  150.1 15.3 %collective-permute-start.21 = (bf16[768,256]{1,0:T(8,128)(2,1)S(1)}, bf16[768,256]{1,0:T(8,128)(2,1)}, u32[]{:S(2)}, u32[]{:S(2)}) collective-permute-start(bf16[768,256]{1,0:T(8,128)(2,1)S(1)} %bitcast.54), channel_id=1, source_target_pairs={{0,64},{1,65},{2,66},{3,67},{4,68},{5,69},{6,70},{7,71},{8,72},{9,... | collective-permute-start | bytes 1179656 | tf_op jit(solution)/shard_map/ppermute | solution.py:28
  150.2 26.7 %copy-start.10 = (f32[768,1,256]{2,1,0:T(1,128)S(1)}, f32[768,1,256]{2,1,0:T(1,128)}, u32[]{:S(2)}) copy-start(f32[768,1,256]{2,1,0:T(1,128)} %param.6) | copy-start | bytes 2359300
  150.2 23.8 %collective-permute-start.22 = (bf16[768,256]{1,0:T(8,128)(2,1)S(1)}, bf16[768,256]{1,0:T(8,128)(2,1)S(1)}, u32[]{:S(2)}, u32[]{:S(2)}) collective-permute-start(bf16[768,256]{1,0:T(8,128)(2,1)S(1)} %bitcast.55), channel_id=1, source_target_pairs={{0,8},{1,9},{2,10},{3,11},{4,12},{5,13},{6,14},{7,15},{8,0},{9,1},... | collective-permute-start | bytes 1179656 | tf_op jit(solution)/shard_map/ppermute | solution.py:28
  165.4 9.7 %collective-permute-start.23 = (bf16[768,256]{1,0:T(8,128)(2,1)}, bf16[768,256]{1,0:T(8,128)(2,1)S(1)}, u32[]{:S(2)}, u32[]{:S(2)}) collective-permute-start(bf16[768,256]{1,0:T(8,128)(2,1)} %collective-permute-done.18.refs_2_), channel_id=1, source_target_pairs={{0,8},{1,9},{2,10},{3,11},{4,12},{5,13},{6,14},{7,15},{8,0},{9,1},... | collective-permute-start | bytes 1179656 | tf_op jit(solution)/shard_map/ppermute | solution.py:28
  168.7 7.8 %collective-permute-start.24 = (bf16[768,256]{1,0:T(8,128)(2,1)}, bf16[768,256]{1,0:T(8,128)(2,1)S(1)}, u32[]{:S(2)}, u32[]{:S(2)}) collective-permute-start(bf16[768,256]{1,0:T(8,128)(2,1)} %collective-permute-done.19.refs_4_), channel_id=1, source_target_pairs={{0,8},{1,9},{2,10},{3,11},{4,12},{5,13},{6,14},{7,15},{8,0},{9,1},... | collective-permute-start | bytes 1179656 | tf_op jit(solution)/shard_map/ppermute | solution.py:28
  169.5 22.0 %collective-permute-start.27 = (bf16[768,256]{1,0:T(8,128)(2,1)}, bf16[768,256]{1,0:T(8,128)(2,1)S(1)}, u32[]{:S(2)}, u32[]{:S(2)}) collective-permute-start(bf16[768,256]{1,0:T(8,128)(2,1)} %collective-permute-done.18.refs_2_), channel_id=1, source_target_pairs={{0,32},{1,33},{2,34},{3,35},{4,36},{5,37},{6,38},{7,39},{8,40},{9,... | collective-permute-start | bytes 1179656 | tf_op jit(solution)/shard_map/ppermute | solution.py:28
  170.0 21.5 %collective-permute-start.28 = (bf16[768,256]{1,0:T(8,128)(2,1)}, bf16[768,256]{1,0:T(8,128)(2,1)S(1)}, u32[]{:S(2)}, u32[]{:S(2)}) collective-permute-start(bf16[768,256]{1,0:T(8,128)(2,1)} %collective-permute-done.18.refs_2_), channel_id=1, source_target_pairs={{0,96},{1,97},{2,98},{3,99},{4,100},{5,101},{6,102},{7,103},{8,104... | collective-permute-start | bytes 1179656 | tf_op jit(solution)/shard_map/ppermute | solution.py:28
  174.1 3.5 %copy-start.17 = (bf16[768,256]{1,0:T(8,128)(2,1)}, bf16[768,256]{1,0:T(8,128)(2,1)S(1)}, u32[]{:S(2)}) copy-start(bf16[768,256]{1,0:T(8,128)(2,1)S(1)} %collective-permute-done.22.refs_1_) | copy-start | bytes 1179652
  174.1 6.6 %collective-permute-start.26 = (bf16[768,256]{1,0:T(8,128)(2,1)}, bf16[768,256]{1,0:T(8,128)(2,1)S(1)}, u32[]{:S(2)}, u32[]{:S(2)}) collective-permute-start(bf16[768,256]{1,0:T(8,128)(2,1)} %collective-permute-done.21.refs_8_), channel_id=1, source_target_pairs={{0,8},{1,9},{2,10},{3,11},{4,12},{5,13},{6,14},{7,15},{8,0},{9,1},... | collective-permute-start | bytes 1179656 | tf_op jit(solution)/shard_map/ppermute | solution.py:28
  175.2 2.5 %copy-start.18 = (bf16[768,256]{1,0:T(8,128)(2,1)}, bf16[768,256]{1,0:T(8,128)(2,1)S(1)}, u32[]{:S(2)}) copy-start(bf16[768,256]{1,0:T(8,128)(2,1)S(1)} %collective-permute-done.23.refs_3_) | copy-start | bytes 1179652
  175.2 16.3 %collective-permute-start.29 = (bf16[768,256]{1,0:T(8,128)(2,1)}, bf16[768,256]{1,0:T(8,128)(2,1)S(1)}, u32[]{:S(2)}, u32[]{:S(2)}) collective-permute-start(bf16[768,256]{1,0:T(8,128)(2,1)} %collective-permute-done.21.refs_8_), channel_id=1, source_target_pairs={{0,16},{1,17},{2,18},{3,19},{4,20},{5,21},{6,22},{7,23},{8,24},{9,... | collective-permute-start | bytes 1179656 | tf_op jit(solution)/shard_map/ppermute | solution.py:28
  176.5 1.1 copy-start.19
  176.5 1.9 collective-permute-start.25
  178.4 5.8 %copy-start.21 = (bf16[768,256]{1,0:T(8,128)(2,1)}, bf16[768,256]{1,0:T(8,128)(2,1)S(1)}, u32[]{:S(2)}) copy-start(bf16[768,256]{1,0:T(8,128)(2,1)S(1)} %collective-permute-done.25.refs_7_) | copy-start | bytes 1179652
  178.4 13.8 %collective-permute-start.33 = (f32[1,256]{1,0:T(1,128)S(1)}, f32[1,256]{1,0:T(1,128)S(1)}, u32[]{:S(2)}, u32[]{:S(2)}) collective-permute-start(f32[1,256]{1,0:T(1,128)S(1)} %get-tuple-element.65), channel_id=1, source_target_pairs={{8,0},{16,8},{24,16},{32,24},{40,32},{48,40},{56,48},{64,56},{72,6... | collective-permute-start | bytes 3080 | tf_op jit(solution)/shard_map/ppermute | solution.py:419
  180.7 3.6 %copy-start.20 = (bf16[768,256]{1,0:T(8,128)(2,1)}, bf16[768,256]{1,0:T(8,128)(2,1)S(1)}, u32[]{:S(2)}) copy-start(bf16[768,256]{1,0:T(8,128)(2,1)S(1)} %collective-permute-done.26.refs_9_) | copy-start | bytes 1179652
  180.7 11.5 %collective-permute-start.34 = (f32[1,256]{1,0:T(1,128)S(1)}, f32[1,256]{1,0:T(1,128)S(1)}, u32[]{:S(2)}, u32[]{:S(2)}) collective-permute-start(f32[1,256]{1,0:T(1,128)S(1)} %get-tuple-element.64), channel_id=1, source_target_pairs={{0,8},{8,16},{16,24},{24,32},{32,40},{40,48},{48,56},{56,64},{64,7... | collective-permute-start | bytes 3080 | tf_op jit(solution)/shard_map/ppermute | solution.py:418
  191.5 1.3 copy-start.22
  191.5 1.3 copy-start.23
  191.5 1.3 copy-start.24
  191.5 1.8 collective-permute-start.30
  191.6 2.3 %collective-permute-start.31 = (bf16[768,256]{1,0:T(8,128)(2,1)S(1)}, bf16[768,256]{1,0:T(8,128)(2,1)S(1)}, u32[]{:S(2)}, u32[]{:S(2)}) collective-permute-start(bf16[768,256]{1,0:T(8,128)(2,1)S(1)} %collective-permute-done.28.refs_2_), channel_id=1, source_target_pairs={{0,8},{1,9},{2,10},{3,11},{4,12},{5,13},{6,14},{7,15},{8,0},{9,1},... | collective-permute-start | bytes 1179656 | tf_op jit(solution)/shard_map/ppermute | solution.py:28
  192.1 2.3 %collective-permute-start.32 = (bf16[768,256]{1,0:T(8,128)(2,1)S(1)}, bf16[768,256]{1,0:T(8,128)(2,1)S(1)}, u32[]{:S(2)}, u32[]{:S(2)}) collective-permute-start(bf16[768,256]{1,0:T(8,128)(2,1)S(1)} %collective-permute-done.29.refs_4_), channel_id=1, source_target_pairs={{0,8},{1,9},{2,10},{3,11},{4,12},{5,13},{6,14},{7,15},{8,0},{9,1},... | collective-permute-start | bytes 1179656 | tf_op jit(solution)/shard_map/ppermute | solution.py:28
  192.8 22.2 %copy-start.3 = (f32[768,1,256]{2,0,1:T(8,128)S(1)}, f32[768,1,256]{2,0,1:T(8,128)}, u32[]{:S(2)}) copy-start(f32[768,1,256]{2,0,1:T(8,128)} %copy-done.2) | copy-start | bytes 2359300
  193.3 1.1 copy-start.25
  (2 other events, 1.6 us)
Sparse Core Ops, SparseCore 0:
  11.3 72.3 all-gather.2

commit v4 on v3

--- a/solution.py
+++ b/solution.py
@@ -55,6 +55,8 @@
     order = jnp.stack(order).astype(jnp.int32)
     pieces = [cells, others[0], side, others[1], up, others[2], down, others[3], across, others[4]]
     carry = mix_part(kernel, pieces, order[:10], None, F32)
+    if not spread:
+        carry, *waiting = together(carry, *waiting)
     carry, side_up, side_down, side_across = together(carry, side_up, side_down, side_across)
     pieces = []
     for piece in (side_up, side_down, side_across):
@@ -324,16 +326,13 @@
         for t in range(count):
             right = right_of(slab_ref, t, part)
             direction = right - alpha * image_ref[t] + beta * right
-            high, low = split(image_ref[t], 2)
-            out_ref[t, part : 2 * part] = high
-            out_ref[t, 2 * part :] = low
             left[t] = (seen_of(slab_ref, t, part) * direction).astype(BF16)
         multiply(left, copies, held, total)
         for t in range(count):
-            out_ref[t, :part] = total[t].astype(BF16)
+            out_ref[t] = total[t].astype(BF16)
 
     shapes = [
-        jax.ShapeDtypeStruct((count, 3 * part, cols), BF16),
+        jax.ShapeDtypeStruct(image.shape, BF16),
         jax.ShapeDtypeStruct((1, 128), F32),
     ]
     scratch = [pltpu.VMEM(image.shape, BF16)]
@@ -405,13 +404,10 @@
 
     image_r, sums = cross_first(order, mixed_r, slabs, strips, total_rows, devices)
     turned, factors = cross_second(order, exchange(sums), slabs, image_r, strips)
-    turned = swap(turned)
-    gathered, (turned,) = gather_geno(
-        turned[:, :part].reshape(rows, cols), kernel_geno, turned
-    )
+    turned, image_r = together(swap(turned), image_r)
+    gathered, (image,) = gather_geno(turned.reshape(rows, cols), kernel_geno, swap(image_r))
 
     alpha, beta, new = factors[:, 0:1], factors[:, 1:2], factors[:, 2:3]
-    image = turned[:, part : 2 * part].astype(F32) + turned[:, 2 * part :].astype(F32)
     image = image.reshape(rows, cols)
     residual = right - alpha * image
     direction = residual + beta * right

time: 224 us -> 222 us (level)
  blocking collectives: 53.1 us -> 49 us
  starting transfers between devices: 55.3 us -> 58.4 us
    all_to_all x1, blocking collectives: 20.1 us -> 11.6 us  [swap(): lax.all_to_all(slabs, 'trial', split_axis=0, concat_axis=0, tiled=True)]
    all_to_all x2, blocking collectives: 33 us -> 37.4 us  [exchange(): return lax.all_to_all(rows, BOTH, 0, 0, tiled=True)]
    all_to_all x2 -> x3, starting transfers between devices: 10.6 us -> 14.2 us  [swap(): lax.all_to_all(slabs, 'trial', split_axis=0, concat_axis=0, tiled=True)]
    unnamed x57 -> x55, local copies, waits for them, and re-layouts: 6.53 us -> 7.93 us
    all_to_all x2 -> x3, waiting for transfers between devices: 9.08 us -> 9.11 us  [swap(): lax.all_to_all(slabs, 'trial', split_axis=0, concat_axis=0, tiled=True)]
  transfers between devices with their start and end apart: 38 -> 39, of which waited for: 17 -> 14; matrix products, arithmetic and copies ran while one was open for 2% -> 2% of each run, Pallas kernels for 9% -> 9%
where the time goes in v4:
time: 222 us
  starting transfers between devices  58.4 us (26%)
  blocking collectives  49 us (22%)
  waiting for transfers between devices  47.7 us (21%)
  Pallas kernels  38.4 us (17%)
  between operations  14.5 us (7%)
  local copies, waits for them, and re-layouts  9.6 us (4%)
  other arithmetic  4.1 us (2%)
    all_to_all x2, blocking collectives, exchange(): return lax.all_to_all(rows, BOTH, 0, 0, tiled=True)  37.4 us
    ppermute x31, starting transfers between devices, hop(): return lax.ppermute(cells, BOTH, pairs)  33.3 us
    ppermute x31, waiting for transfers between devices, hop(): return lax.ppermute(cells, BOTH, pairs)  29.8 us
    pallas_call x4, Pallas kernels, mix(): pl.pallas_call(body, out_shape=shapes, in_specs=[SMEM] + [HBM] * (1 + cou...  25.5 us
    all_to_all x3, starting transfers between devices, swap(): lax.all_to_all(slabs, 'trial', split_axis=0, concat_axis=0, tiled=True)  14.2 us
    all_to_all x1, blocking collectives, swap(): lax.all_to_all(slabs, 'trial', split_axis=0, concat_axis=0, tiled=True)  11.6 us
    pallas_call x2, Pallas kernels, cross_call(): pl.pallas_call(body, out_shape=shapes, in_specs=[SMEM if x.ndim == 1 else...  10.7 us
    all_to_all x3, waiting for transfers between devices, swap(): lax.all_to_all(slabs, 'trial', split_axis=0, concat_axis=0, tiled=True)  9.11 us
  transfers between devices with their start and end apart: 39, of which 14 were waited for; matrix products, arithmetic and copies ran while one was open for 2% of the time, Pallas kernels for 9%

profile of v4, /device:TPU:1, one launch (start us, length us, event | category | flops | bytes accessed | tf_op | source)
XLA Modules:
  0.0 221.7 jit_solution(1405174542788439634)
XLA Ops:
  7.3 1.1 copy-done
  8.4 0.8 constant_dynamic-slice_fusion.1
  9.3 1.8 fusion.6
  11.3 2.5 %collective-permute-start = (bf16[768,256]{1,0:T(8,128)(2,1)S(1)}, bf16[768,256]{1,0:T(8,128)(2,1)}, u32[]{:S(2)}, u32[]{:S(2)}) collective-permute-start(bf16[768,256]{1,0:T(8,128)(2,1)S(1)} %multiply_convert_fusion.refs_0_), channel_id=1, source_target_pairs={{0,16},{1,17},{2,18},{3,19},{4,20},{5,21},{6,22},{7,23},{8,24},{9,... | collective-permute-start | bytes 1179656 | tf_op jit(solution)/shard_map/ppermute | solution.py:28
  13.8 1.3 collective-permute-start.1
  15.1 1.4 collective-permute-start.2
  16.6 1.6 collective-permute-start.3
  18.2 3.4 %collective-permute-start.4 = (f32[1,256]{1,0:T(1,128)S(1)}, f32[1,256]{1,0:T(1,128)S(1)}, u32[]{:S(2)}, u32[]{:S(2)}) collective-permute-start(f32[1,256]{1,0:T(1,128)S(1)} %get-tuple-element.75), channel_id=1, source_target_pairs={{0,8},{8,16},{16,24},{24,32},{32,40},{40,48},{48,56},{56,64},{64,7... | collective-permute-start | bytes 3080 | tf_op jit(solution)/shard_map/ppermute | solution.py:392
  21.6 0.7 collective-permute-done.4.above_ref
  22.3 1.9 collective-permute-start.5
  24.3 1.2 copy.18
  25.5 2.7 %collective-permute-done.5.below_ref = f32[1,256]{1,0:T(1,128)S(1)} collective-permute-done((f32[1,256]{1,0:T(1,128)S(1)}, f32[1,256]{1,0:T(1,128)S(1)}, u32[]{:S(2)}, u32[]{:S(2)}) %collective-permute-start.5) | collective-permute-done | bytes 1056 | tf_op jit(solution)/shard_map/ppermute | solution.py:393
  28.5 1.0 copy-done.4
  29.5 5.0 %collective-permute-done.3.refs_8_ = bf16[768,256]{1,0:T(8,128)(2,1)} collective-permute-done((bf16[768,256]{1,0:T(8,128)(2,1)S(1)}, bf16[768,256]{1,0:T(8,128)(2,1)}, u32[]{:S(2)}, u32[]{:S(2)}) %collective-permute-start.3) | collective-permute-done | bytes 393248 | tf_op jit(solution)/shard_map/ppermute | solution.py:28
  34.5 1.9 collective-permute-start.7
  36.4 7.0 %all-to-all-start = ((bf16[8,304,256]{2,1,0:T(8,128)(2,1)}), bf16[8,304,256]{2,1,0:T(8,128)(2,1)S(1)}, u32[]{:S(2)}, u32[]{:S(2)}) async-start(bf16[8,304,256]{2,1,0:T(8,128)(2,1)} %copy-done.4), calls=%async_computation | async-start | bytes 2490368 | tf_op jit(solution)/shard_map/all_to_all | solution.py:131
  43.4 0.8 collective-permute-start.8
  44.3 3.0 %collective-permute-start.11 = (bf16[768,256]{1,0:T(8,128)(2,1)}, bf16[768,256]{1,0:T(8,128)(2,1)S(1)}, u32[]{:S(2)}, u32[]{:S(2)}) collective-permute-start(bf16[768,256]{1,0:T(8,128)(2,1)} %collective-permute-done.refs_2_), channel_id=1, source_target_pairs={{0,32},{1,33},{2,34},{3,35},{4,36},{5,37},{6,38},{7,39},{8,40},{9,... | collective-permute-start | bytes 1179656 | tf_op jit(solution)/shard_map/ppermute | solution.py:28
  47.3 1.5 collective-permute-start.12
  48.7 1.2 collective-permute-start.13
  50.0 7.2 %shard_map.78.refs_6_ = f32[768,256]{1,0:T(8,128)S(1)} custom-call(s32[10]{0:T(128)S(1)} %stack.99.order_ref, bf16[768,12288]{1,0:T(8,128)(2,1)} %kernel_ref.3, bf16[768,256]{1,0:T(8,128)(2,1)} %copy-done.13, bf16[768,256]{1,0:T(8,128)(2,1)} %collective-permute-done.6.refs_1_, bf16[768,256]{1,0:T(8,128)(2,1)} %collective-permute-done.refs_2_, ...), custom_call_target="tpu_custom_call" | custom-call | tf_op jit(solution)/shard_map/pallas_call | solution.py:184
  57.2 0.9 copy-done.5
  58.1 9.3 %collective-permute-done.13.refs_4_ = bf16[768,256]{1,0:T(8,128)(2,1)} collective-permute-done((bf16[768,256]{1,0:T(8,128)(2,1)}, bf16[768,256]{1,0:T(8,128)(2,1)}, u32[]{:S(2)}, u32[]{:S(2)}) %collective-permute-start.13) | collective-permute-done | bytes 393248 | tf_op jit(solution)/shard_map/ppermute | solution.py:28
  67.4 1.3 collective-permute-start.14
  68.6 0.5 collective-permute-start.16
  69.2 1.4 collective-permute-done.14.refs_1_
  70.9 0.6 collective-permute-done.16.refs_5_
  71.5 1.1 copy-done.6
  72.6 5.9 %shard_map.79 = bf16[768,256]{1,0:T(8,128)(2,1)} custom-call(s32[6]{0:T(128)S(1)} %stack.85.order_ref, bf16[768,12288]{1,0:T(8,128)(2,1)} %kernel_ref.3, bf16[768,256]{1,0:T(8,128)(2,1)} %copy-done.14, bf16[768,256]{1,0:T(8,128)(2,1)} %collective-permute-done.14.refs_1_, bf16[768,256]{1,0:T(8,128)(2,1)} %collective-permute-done.12.refs_2_, ...), custom_call_target="tpu_custom_call" | custom-call | tf_op jit(solution)/shard_map/pallas_call | solution.py:184
  78.5 5.3 %all-gather.3.cloned.1.call-done = bf16[1024,1280]{1,0:T(8,128)(2,1)} async-done(((bf16[128,1280]{1,0:T(8,128)(2,1)}), bf16[1024,1280]{1,0:T(8,128)(2,1)}) %all-gather.3.cloned.1.call-update) | async-done | bytes 2621456 | tf_op jit(solution)/shard_map/all_gather | solution.py:396
  83.7 0.8 collective-permute-start.17
  84.5 3.6 %all-to-all-start.1 = ((bf16[8,96,256]{2,1,0:T(8,128)(2,1)}), bf16[8,96,256]{2,1,0:T(8,128)(2,1)S(1)}, u32[]{:S(2)}, u32[]{:S(2)}) async-start(bf16[8,96,256]{2,1,0:T(8,128)(2,1)} %bitcast.23), calls=%async_computation.1 | async-start | bytes 786432 | tf_op jit(solution)/shard_map/all_to_all | solution.py:131
  88.3 9.1 %all-to-all-done.1.mixed_ref = bf16[8,96,256]{2,1,0:T(8,128)(2,1)S(1)} async-done(((bf16[8,96,256]{2,1,0:T(8,128)(2,1)}), bf16[8,96,256]{2,1,0:T(8,128)(2,1)S(1)}, u32[]{:S(2)}, u32[]{:S(2)}) %all-to-all-start.1) | async-done | bytes 393248 | tf_op jit(solution)/shard_map/all_to_all | solution.py:131
  97.4 5.8 %shard_map.80 = (f32[8,96,256]{2,1,0:T(8,128)S(1)}, f32[128,1,128]{2,1,0:T(1,128)S(1)}) custom-call(s32[2]{0:T(128)S(1)} %pad_add_fusion.order_ref, bf16[8,96,256]{2,1,0:T(8,128)(2,1)S(1)} %all-to-all-done.1.mixed_ref, bf16[8,304,256]{2,1,0:T(8,128)(2,1)S(1)} %all-to-all-done.slab_ref, bf16[8,128,1280]{2,1,0:T(8,128)(2,1)} %bitcast.49, ...), custom_call_target="tpu_custom_call" | custom-call | flops 805306368 | bytes 8388608 | tf_op jit(solution)/shard_map/pallas_call | solution.py:260
  103.2 18.8 %all_to_all.30.sums_ref = f32[128,1,128]{2,1,0:T(1,128)S(1)} all-to-all(f32[128,1,128]{2,1,0:T(1,128)S(1)} %get-tuple-element.50), channel_id=1, replica_groups=mesh['geno'=16,'trial'=8] {'geno','trial'}, dimensions={0} | all-to-all | bytes 131072 | tf_op jit(solution)/shard_map/all_to_all | solution.py:135
  122.0 4.9 %shard_map.81 = (bf16[8,96,256]{2,1,0:T(8,128)(2,1)S(1)}, f32[1,128]{1,0:T(1,128)S(1)}) custom-call(s32[2]{0:T(128)S(1)} %pad_add_fusion.order_ref, f32[128,1,128]{2,1,0:T(1,128)S(1)} %all_to_all.30.sums_ref, bf16[8,304,256]{2,1,0:T(8,128)(2,1)S(1)} %all-to-all-done.slab_ref, f32[8,96,256]{2,1,0:T(8,128)S(1)} %get-tuple-element.54.image_ref, ...), custom_call_target="tpu_custom_call" | custom-call | flops 805306368 | bytes 8388608 | tf_op jit(solution)/shard_map/pallas_call | solution.py:260
  126.9 11.6 %all_to_all.31 = bf16[8,96,256]{2,1,0:T(8,128)(2,1)S(1)} all-to-all(bf16[8,96,256]{2,1,0:T(8,128)(2,1)S(1)} %get-tuple-element.52), channel_id=1, replica_groups=mesh['geno'=16,'trial'=8] {'trial'}, dimensions={0} | all-to-all | bytes 786432 | tf_op jit(solution)/shard_map/all_to_all | solution.py:131
  138.5 3.5 %all-to-all-start.4 = ((f32[8,96,256]{2,1,0:T(8,128)}), f32[8,96,256]{2,1,0:T(8,128)S(1)}, u32[]{:S(2)}, u32[]{:S(2)}) async-start(f32[8,96,256]{2,1,0:T(8,128)} %copy-done.7), calls=%async_computation.4 | async-start | bytes 1572864 | tf_op jit(solution)/shard_map/all_to_all | solution.py:131
  142.3 0.4 collective-permute-start.19
  142.7 2.3 %collective-permute-start.20 = (bf16[768,256]{1,0:T(8,128)(2,1)S(1)}, bf16[768,256]{1,0:T(8,128)(2,1)}, u32[]{:S(2)}, u32[]{:S(2)}) collective-permute-start(bf16[768,256]{1,0:T(8,128)(2,1)S(1)} %bitcast.53), channel_id=1, source_target_pairs={{0,96},{1,97},{2,98},{3,99},{4,100},{5,101},{6,102},{7,103},{8,104... | collective-permute-start | bytes 1179656 | tf_op jit(solution)/shard_map/ppermute | solution.py:28
  145.0 3.0 %collective-permute-start.22 = (bf16[768,256]{1,0:T(8,128)(2,1)S(1)}, bf16[768,256]{1,0:T(8,128)(2,1)}, u32[]{:S(2)}, u32[]{:S(2)}) collective-permute-start(bf16[768,256]{1,0:T(8,128)(2,1)S(1)} %bitcast.55), channel_id=1, source_target_pairs={{0,8},{1,9},{2,10},{3,11},{4,12},{5,13},{6,14},{7,15},{8,0},{9,1},... | collective-permute-start | bytes 1179656 | tf_op jit(solution)/shard_map/ppermute | solution.py:28
  148.1 11.5 %collective-permute-done.18.refs_2_ = bf16[768,256]{1,0:T(8,128)(2,1)} collective-permute-done((bf16[768,256]{1,0:T(8,128)(2,1)S(1)}, bf16[768,256]{1,0:T(8,128)(2,1)}, u32[]{:S(2)}, u32[]{:S(2)}) %collective-permute-start.18) | collective-permute-done | bytes 393248 | tf_op jit(solution)/shard_map/ppermute | solution.py:28
  159.7 4.0 %collective-permute-start.23 = (bf16[768,256]{1,0:T(8,128)(2,1)}, bf16[768,256]{1,0:T(8,128)(2,1)S(1)}, u32[]{:S(2)}, u32[]{:S(2)}) collective-permute-start(bf16[768,256]{1,0:T(8,128)(2,1)} %collective-permute-done.18.refs_2_), channel_id=1, source_target_pairs={{0,8},{1,9},{2,10},{3,11},{4,12},{5,13},{6,14},{7,15},{8,0},{9,1},... | collective-permute-start | bytes 1179656 | tf_op jit(solution)/shard_map/ppermute | solution.py:28
  163.8 0.4 collective-permute-start.25
  164.4 0.6 fusion.13
  165.0 0.4 collective-permute-start.27
  165.4 2.4 %collective-permute-start.28 = (bf16[768,256]{1,0:T(8,128)(2,1)}, bf16[768,256]{1,0:T(8,128)(2,1)S(1)}, u32[]{:S(2)}, u32[]{:S(2)}) collective-permute-start(bf16[768,256]{1,0:T(8,128)(2,1)} %collective-permute-done.18.refs_2_), channel_id=1, source_target_pairs={{0,96},{1,97},{2,98},{3,99},{4,100},{5,101},{6,102},{7,103},{8,104... | collective-permute-start | bytes 1179656 | tf_op jit(solution)/shard_map/ppermute | solution.py:28
  167.9 1.3 collective-permute-start.29
  169.2 0.7 copy-done.19
  169.9 0.8 copy-done.20
  170.7 7.2 %shard_map.82.refs_6_ = f32[768,256]{1,0:T(8,128)S(1)} custom-call(s32[10]{0:T(128)S(1)} %stack.99.order_ref, bf16[768,12288]{1,0:T(8,128)(2,1)} %kernel_ref.3, bf16[768,256]{1,0:T(8,128)(2,1)} %bitcast.56, bf16[768,256]{1,0:T(8,128)(2,1)} %collective-permute-done.22.refs_1_, bf16[768,256]{1,0:T(8,128)(2,1)} %collective-permute-done.18.refs_2_, ...), custom_call_target="tpu_custom_call" | custom-call | tf_op jit(solution)/shard_map/pallas_call | solution.py:184
  177.8 0.7 broadcast_multiply_fusion
  178.6 0.8 bitcast_subtract_fusion
  179.3 3.0 %collective-permute-start.33 = (f32[1,256]{1,0:T(1,128)S(1)}, f32[1,256]{1,0:T(1,128)S(1)}, u32[]{:S(2)}, u32[]{:S(2)}) collective-permute-start(f32[1,256]{1,0:T(1,128)S(1)} %get-tuple-element.73), channel_id=1, source_target_pairs={{8,0},{16,8},{24,16},{32,24},{40,32},{48,40},{56,48},{64,56},{72,6... | collective-permute-start | bytes 3080 | tf_op jit(solution)/shard_map/ppermute | solution.py:415
  182.4 2.5 %collective-permute-start.34 = (f32[1,256]{1,0:T(1,128)S(1)}, f32[1,256]{1,0:T(1,128)S(1)}, u32[]{:S(2)}, u32[]{:S(2)}) collective-permute-start(f32[1,256]{1,0:T(1,128)S(1)} %get-tuple-element.72), channel_id=1, source_target_pairs={{0,8},{8,16},{16,24},{24,32},{32,40},{40,48},{48,56},{56,64},{64,7... | collective-permute-start | bytes 3080 | tf_op jit(solution)/shard_map/ppermute | solution.py:414
  185.1 0.5 collective-permute-start.31
  185.7 0.4 fusion.2
  186.2 0.6 collective-permute-done.30.refs_1_
  186.8 0.6 collective-permute-done.31.refs_3_
  187.4 0.6 collective-permute-done.32.refs_5_
  188.1 0.8 copy-done.26
  188.9 5.4 %shard_map.83 = (f32[768,256]{1,0:T(8,128)S(1)}, f32[128,1,128]{2,1,0:T(1,128)S(1)}) custom-call(s32[6]{0:T(128)S(1)} %stack.85.order_ref, bf16[768,12288]{1,0:T(8,128)(2,1)} %kernel_ref.3, bf16[768,256]{1,0:T(8,128)(2,1)} %copy-done.21, bf16[768,256]{1,0:T(8,128)(2,1)} %copy-done.24, bf16[768,256]{1,0:T(8,128)(2,1)} %copy-done.22, ...), custom_call_target="tpu_custom_call" | custom-call | tf_op jit(solution)/shard_map/pallas_call | solution.py:184
  194.3 18.6 %all_to_all.32.sums_ref = f32[128,1,128]{2,1,0:T(1,128)S(1)} all-to-all(f32[128,1,128]{2,1,0:T(1,128)S(1)} %get-tuple-element.68), channel_id=1, replica_groups=mesh['geno'=16,'trial'=8] {'geno','trial'}, dimensions={0} | all-to-all | bytes 131072 | tf_op jit(solution)/shard_map/all_to_all | solution.py:135
  212.9 1.9 shard_map.84
  (100 shorter events, 2.4 us)
Async XLA Ops:
  7.2 1.2 copy-start
  7.2 3.9 %copy-start.10 = (f32[768,1,256]{2,1,0:T(1,128)S(1)}, f32[768,1,256]{2,1,0:T(1,128)}, u32[]{:S(2)}) copy-start(f32[768,1,256]{2,1,0:T(1,128)} %param.6) | copy-start | bytes 2359300
  7.2 3.9 %copy-start.1 = (s32[768,256]{1,0:T(8,128)S(1)}, s32[768,256]{1,0:T(8,128)}, u32[]{:S(2)}) copy-start(s32[768,256]{1,0:T(8,128)} %seen_ref.1) | copy-start | bytes 2359300
  7.2 76.5 %all-gather.3.cloned.1.call-start = ((), (), s32[]{:S(2)}) async-start(), calls=%async_computation.6 | async-start | bytes 2949120 | tf_op jit(solution)/shard_map/all_gather | solution.py:396
  9.2 19.0 %copy-start.8 = (f32[256]{0:T(256)S(1)}, f32[256]{0:T(256)}, u32[]{:S(2)}) copy-start(f32[256]{0:T(256)} %param.9) | copy-start | bytes 3076
  9.3 19.0 %copy-start.9 = (s32[256]{0:T(256)S(1)}, s32[256]{0:T(256)}, u32[]{:S(2)}) copy-start(s32[256]{0:T(256)} %param.8) | copy-start | bytes 3076
  11.3 25.1 %copy-start.13 = (bf16[768,256]{1,0:T(8,128)(2,1)}, bf16[768,256]{1,0:T(8,128)(2,1)S(1)}, u32[]{:S(2)}) copy-start(bf16[768,256]{1,0:T(8,128)(2,1)S(1)} %multiply_convert_fusion.refs_0_) | copy-start | bytes 1179652
  11.3 18.2 %collective-permute-start = (bf16[768,256]{1,0:T(8,128)(2,1)S(1)}, bf16[768,256]{1,0:T(8,128)(2,1)}, u32[]{:S(2)}, u32[]{:S(2)}) collective-permute-start(bf16[768,256]{1,0:T(8,128)(2,1)S(1)} %multiply_convert_fusion.refs_0_), channel_id=1, source_target_pairs={{0,16},{1,17},{2,18},{3,19},{4,20},{5,21},{6,22},{7,23},{8,24},{9,... | collective-permute-start | bytes 1179656 | tf_op jit(solution)/shard_map/ppermute | solution.py:28
  13.8 15.7 %collective-permute-start.1 = (bf16[768,256]{1,0:T(8,128)(2,1)S(1)}, bf16[768,256]{1,0:T(8,128)(2,1)S(1)}, u32[]{:S(2)}, u32[]{:S(2)}) collective-permute-start(bf16[768,256]{1,0:T(8,128)(2,1)S(1)} %multiply_convert_fusion.refs_0_), channel_id=1, source_target_pairs={{0,32},{1,33},{2,34},{3,35},{4,36},{5,37},{6,38},{7,39},{8,40},{9,... | collective-permute-start | bytes 1179656 | tf_op jit(solution)/shard_map/ppermute | solution.py:28
  15.1 14.4 %collective-permute-start.2 = (bf16[768,256]{1,0:T(8,128)(2,1)S(1)}, bf16[768,256]{1,0:T(8,128)(2,1)S(1)}, u32[]{:S(2)}, u32[]{:S(2)}) collective-permute-start(bf16[768,256]{1,0:T(8,128)(2,1)S(1)} %multiply_convert_fusion.refs_0_), channel_id=1, source_target_pairs={{0,96},{1,97},{2,98},{3,99},{4,100},{5,101},{6,102},{7,103},{8,104... | collective-permute-start | bytes 1179656 | tf_op jit(solution)/shard_map/ppermute | solution.py:28
  16.6 17.9 %collective-permute-start.3 = (bf16[768,256]{1,0:T(8,128)(2,1)S(1)}, bf16[768,256]{1,0:T(8,128)(2,1)}, u32[]{:S(2)}, u32[]{:S(2)}) collective-permute-start(bf16[768,256]{1,0:T(8,128)(2,1)S(1)} %multiply_convert_fusion.refs_0_), channel_id=1, source_target_pairs={{0,64},{1,65},{2,66},{3,67},{4,68},{5,69},{6,70},{7,71},{8,72},{9,... | collective-permute-start | bytes 1179656 | tf_op jit(solution)/shard_map/ppermute | solution.py:28
  18.2 4.1 %collective-permute-start.4 = (f32[1,256]{1,0:T(1,128)S(1)}, f32[1,256]{1,0:T(1,128)S(1)}, u32[]{:S(2)}, u32[]{:S(2)}) collective-permute-start(f32[1,256]{1,0:T(1,128)S(1)} %get-tuple-element.75), channel_id=1, source_target_pairs={{0,8},{8,16},{16,24},{24,32},{32,40},{40,48},{48,56},{56,64},{64,7... | collective-permute-start | bytes 3080 | tf_op jit(solution)/shard_map/ppermute | solution.py:392
  22.3 5.9 %collective-permute-start.5 = (f32[1,256]{1,0:T(1,128)S(1)}, f32[1,256]{1,0:T(1,128)S(1)}, u32[]{:S(2)}, u32[]{:S(2)}) collective-permute-start(f32[1,256]{1,0:T(1,128)S(1)} %get-tuple-element.74), channel_id=1, source_target_pairs={{8,0},{16,8},{24,16},{32,24},{40,32},{48,40},{56,48},{64,56},{72,6... | collective-permute-start | bytes 3080 | tf_op jit(solution)/shard_map/ppermute | solution.py:393
  25.5 10.9 %copy-start.2 = (f32[768,1,256]{2,0,1:T(8,128)}, f32[768,1,256]{2,0,1:T(8,128)S(1)}, u32[]{:S(2)}) copy-start(f32[768,1,256]{2,0,1:T(8,128)S(1)} %copy.18) | copy-start | bytes 2359300
  28.2 16.0 %collective-permute-start.6 = (bf16[768,256]{1,0:T(8,128)(2,1)S(1)}, bf16[768,256]{1,0:T(8,128)(2,1)}, u32[]{:S(2)}, u32[]{:S(2)}) collective-permute-start(bf16[768,256]{1,0:T(8,128)(2,1)S(1)} %multiply_convert_fusion.refs_0_), channel_id=1, source_target_pairs={{0,8},{1,9},{2,10},{3,11},{4,12},{5,13},{6,14},{7,15},{8,0},{9,1},... | collective-permute-start | bytes 1179656 | tf_op jit(solution)/shard_map/ppermute | solution.py:28
  28.4 1.1 copy-start.4
  29.5 6.9 %copy-start.15 = (bf16[768,256]{1,0:T(8,128)(2,1)}, bf16[768,256]{1,0:T(8,128)(2,1)S(1)}, u32[]{:S(2)}) copy-start(bf16[768,256]{1,0:T(8,128)(2,1)S(1)} %collective-permute-done.1.refs_4_) | copy-start | bytes 1179652
  29.5 5.0 %copy-start.16 = (bf16[768,256]{1,0:T(8,128)(2,1)}, bf16[768,256]{1,0:T(8,128)(2,1)S(1)}, u32[]{:S(2)}) copy-start(bf16[768,256]{1,0:T(8,128)(2,1)S(1)} %collective-permute-done.2.refs_6_) | copy-start | bytes 1179652
  34.5 12.8 %collective-permute-start.7 = (bf16[768,256]{1,0:T(8,128)(2,1)}, bf16[768,256]{1,0:T(8,128)(2,1)}, u32[]{:S(2)}, u32[]{:S(2)}) collective-permute-start(bf16[768,256]{1,0:T(8,128)(2,1)} %collective-permute-done.refs_2_), channel_id=1, source_target_pairs={{0,8},{1,9},{2,10},{3,11},{4,12},{5,13},{6,14},{7,15},{8,0},{9,1},... | collective-permute-start | bytes 1179656 | tf_op jit(solution)/shard_map/ppermute | solution.py:28
  36.4 12.4 %collective-permute-start.10 = (bf16[768,256]{1,0:T(8,128)(2,1)}, bf16[768,256]{1,0:T(8,128)(2,1)}, u32[]{:S(2)}, u32[]{:S(2)}) collective-permute-start(bf16[768,256]{1,0:T(8,128)(2,1)} %collective-permute-done.3.refs_8_), channel_id=1, source_target_pairs={{0,8},{1,9},{2,10},{3,11},{4,12},{5,13},{6,14},{7,15},{8,0},{9,1},... | collective-permute-start | bytes 1179656 | tf_op jit(solution)/shard_map/ppermute | solution.py:28
  36.4 32.8 %all-to-all-start = ((bf16[8,304,256]{2,1,0:T(8,128)(2,1)}), bf16[8,304,256]{2,1,0:T(8,128)(2,1)S(1)}, u32[]{:S(2)}, u32[]{:S(2)}) async-start(bf16[8,304,256]{2,1,0:T(8,128)(2,1)} %copy-done.4), calls=%async_computation | async-start | bytes 2490368 | tf_op jit(solution)/shard_map/all_to_all | solution.py:131
  43.4 6.6 %collective-permute-start.8 = (bf16[768,256]{1,0:T(8,128)(2,1)}, bf16[768,256]{1,0:T(8,128)(2,1)}, u32[]{:S(2)}, u32[]{:S(2)}) collective-permute-start(bf16[768,256]{1,0:T(8,128)(2,1)} %copy-done.15), channel_id=1, source_target_pairs={{0,8},{1,9},{2,10},{3,11},{4,12},{5,13},{6,14},{7,15},{8,0},{9,1},... | collective-permute-start | bytes 1179656 | tf_op jit(solution)/shard_map/ppermute | solution.py:28
  44.2 5.8 %collective-permute-start.9 = (bf16[768,256]{1,0:T(8,128)(2,1)}, bf16[768,256]{1,0:T(8,128)(2,1)}, u32[]{:S(2)}, u32[]{:S(2)}) collective-permute-start(bf16[768,256]{1,0:T(8,128)(2,1)} %copy-done.16), channel_id=1, source_target_pairs={{0,8},{1,9},{2,10},{3,11},{4,12},{5,13},{6,14},{7,15},{8,0},{9,1},... | collective-permute-start | bytes 1179656 | tf_op jit(solution)/shard_map/ppermute | solution.py:28
  44.3 13.8 %collective-permute-start.11 = (bf16[768,256]{1,0:T(8,128)(2,1)}, bf16[768,256]{1,0:T(8,128)(2,1)S(1)}, u32[]{:S(2)}, u32[]{:S(2)}) collective-permute-start(bf16[768,256]{1,0:T(8,128)(2,1)} %collective-permute-done.refs_2_), channel_id=1, source_target_pairs={{0,32},{1,33},{2,34},{3,35},{4,36},{5,37},{6,38},{7,39},{8,40},{9,... | collective-permute-start | bytes 1179656 | tf_op jit(solution)/shard_map/ppermute | solution.py:28
  47.3 10.8 %collective-permute-start.12 = (bf16[768,256]{1,0:T(8,128)(2,1)}, bf16[768,256]{1,0:T(8,128)(2,1)}, u32[]{:S(2)}, u32[]{:S(2)}) collective-permute-start(bf16[768,256]{1,0:T(8,128)(2,1)} %collective-permute-done.refs_2_), channel_id=1, source_target_pairs={{0,96},{1,97},{2,98},{3,99},{4,100},{5,101},{6,102},{7,103},{8,104... | collective-permute-start | bytes 1179656 | tf_op jit(solution)/shard_map/ppermute | solution.py:28
  48.7 18.6 %collective-permute-start.13 = (bf16[768,256]{1,0:T(8,128)(2,1)}, bf16[768,256]{1,0:T(8,128)(2,1)}, u32[]{:S(2)}, u32[]{:S(2)}) collective-permute-start(bf16[768,256]{1,0:T(8,128)(2,1)} %collective-permute-done.refs_2_), channel_id=1, source_target_pairs={{0,64},{1,65},{2,66},{3,67},{4,68},{5,69},{6,70},{7,71},{8,72},{9,... | collective-permute-start | bytes 1179656 | tf_op jit(solution)/shard_map/ppermute | solution.py:28
  57.2 0.9 copy-start.5
  58.1 13.4 %copy-start.14 = (bf16[768,256]{1,0:T(8,128)(2,1)}, bf16[768,256]{1,0:T(8,128)(2,1)S(1)}, u32[]{:S(2)}) copy-start(bf16[768,256]{1,0:T(8,128)(2,1)S(1)} %collective-permute-done.11.refs_0_) | copy-start | bytes 1179652
  67.4 3.3 %collective-permute-start.14 = (bf16[768,256]{1,0:T(8,128)(2,1)S(1)}, bf16[768,256]{1,0:T(8,128)(2,1)}, u32[]{:S(2)}, u32[]{:S(2)}) collective-permute-start(bf16[768,256]{1,0:T(8,128)(2,1)S(1)} %collective-permute-done.11.refs_0_), channel_id=1, source_target_pairs={{0,8},{1,9},{2,10},{3,11},{4,12},{5,13},{6,14},{7,15},{8,0},{9,1},... | collective-permute-start | bytes 1179656 | tf_op jit(solution)/shard_map/ppermute | solution.py:28
  68.6 2.3 %collective-permute-start.15 = (bf16[768,256]{1,0:T(8,128)(2,1)}, bf16[768,256]{1,0:T(8,128)(2,1)}, u32[]{:S(2)}, u32[]{:S(2)}) collective-permute-start(bf16[768,256]{1,0:T(8,128)(2,1)} %collective-permute-done.12.refs_2_), channel_id=1, source_target_pairs={{0,8},{1,9},{2,10},{3,11},{4,12},{5,13},{6,14},{7,15},{8,0},{9,1},... | collective-permute-start | bytes 1179656 | tf_op jit(solution)/shard_map/ppermute | solution.py:28
  68.6 2.8 %collective-permute-start.16 = (bf16[768,256]{1,0:T(8,128)(2,1)}, bf16[768,256]{1,0:T(8,128)(2,1)}, u32[]{:S(2)}, u32[]{:S(2)}) collective-permute-start(bf16[768,256]{1,0:T(8,128)(2,1)} %collective-permute-done.13.refs_4_), channel_id=1, source_target_pairs={{0,8},{1,9},{2,10},{3,11},{4,12},{5,13},{6,14},{7,15},{8,0},{9,1},... | collective-permute-start | bytes 1179656 | tf_op jit(solution)/shard_map/ppermute | solution.py:28
  71.5 1.1 copy-start.6
  83.7 13.7 %collective-permute-start.17 = (bf16[8,128,1280]{2,1,0:T(8,128)(2,1)}, bf16[8,128,1280]{2,1,0:T(8,128)(2,1)}, u32[]{:S(2)}, u32[]{:S(2)}) collective-permute-start(bf16[8,128,1280]{2,1,0:T(8,128)(2,1)} %bitcast.48), channel_id=1, source_target_pairs={{0,8},{1,9},{2,10},{3,11},{4,12},{5,13},{6,14},{7,15},{8,0},{9,1},... | collective-permute-start | bytes 7864328 | tf_op jit(solution)/shard_map/ppermute | solution.py:28
  84.5 12.8 %all-to-all-start.1 = ((bf16[8,96,256]{2,1,0:T(8,128)(2,1)}), bf16[8,96,256]{2,1,0:T(8,128)(2,1)S(1)}, u32[]{:S(2)}, u32[]{:S(2)}) async-start(bf16[8,96,256]{2,1,0:T(8,128)(2,1)} %bitcast.23), calls=%async_computation.1 | async-start | bytes 786432 | tf_op jit(solution)/shard_map/all_to_all | solution.py:131
  103.2 23.7 %copy-start.7 = (f32[8,96,256]{2,1,0:T(8,128)}, f32[8,96,256]{2,1,0:T(8,128)S(1)}, u32[]{:S(2)}) copy-start(f32[8,96,256]{2,1,0:T(8,128)S(1)} %get-tuple-element.54.image_ref) | copy-start | bytes 2359300
  138.5 30.6 %copy-start.12 = (bf16[8,96,256]{2,1,0:T(8,128)(2,1)}, bf16[8,96,256]{2,1,0:T(8,128)(2,1)S(1)}, u32[]{:S(2)}) copy-start(bf16[8,96,256]{2,1,0:T(8,128)(2,1)S(1)} %all_to_all.31) | copy-start | bytes 1179652
  138.5 21.1 %all-to-all-start.4 = ((f32[8,96,256]{2,1,0:T(8,128)}), f32[8,96,256]{2,1,0:T(8,128)S(1)}, u32[]{:S(2)}, u32[]{:S(2)}) async-start(f32[8,96,256]{2,1,0:T(8,128)} %copy-done.7), calls=%async_computation.4 | async-start | bytes 1572864 | tf_op jit(solution)/shard_map/all_to_all | solution.py:131
  142.1 17.4 %collective-permute-start.18 = (bf16[768,256]{1,0:T(8,128)(2,1)S(1)}, bf16[768,256]{1,0:T(8,128)(2,1)}, u32[]{:S(2)}, u32[]{:S(2)}) collective-permute-start(bf16[768,256]{1,0:T(8,128)(2,1)S(1)} %bitcast.51), channel_id=1, source_target_pairs={{0,16},{1,17},{2,18},{3,19},{4,20},{5,21},{6,22},{7,23},{8,24},{9,... | collective-permute-start | bytes 1179656 | tf_op jit(solution)/shard_map/ppermute | solution.py:28
  142.3 17.2 %collective-permute-start.19 = (bf16[768,256]{1,0:T(8,128)(2,1)S(1)}, bf16[768,256]{1,0:T(8,128)(2,1)}, u32[]{:S(2)}, u32[]{:S(2)}) collective-permute-start(bf16[768,256]{1,0:T(8,128)(2,1)S(1)} %bitcast.52), channel_id=1, source_target_pairs={{0,32},{1,33},{2,34},{3,35},{4,36},{5,37},{6,38},{7,39},{8,40},{9,... | collective-permute-start | bytes 1179656 | tf_op jit(solution)/shard_map/ppermute | solution.py:28
  142.7 16.8 %collective-permute-start.20 = (bf16[768,256]{1,0:T(8,128)(2,1)S(1)}, bf16[768,256]{1,0:T(8,128)(2,1)}, u32[]{:S(2)}, u32[]{:S(2)}) collective-permute-start(bf16[768,256]{1,0:T(8,128)(2,1)S(1)} %bitcast.53), channel_id=1, source_target_pairs={{0,96},{1,97},{2,98},{3,99},{4,100},{5,101},{6,102},{7,103},{8,104... | collective-permute-start | bytes 1179656 | tf_op jit(solution)/shard_map/ppermute | solution.py:28
  145.0 14.7 %collective-permute-start.21 = (bf16[768,256]{1,0:T(8,128)(2,1)S(1)}, bf16[768,256]{1,0:T(8,128)(2,1)}, u32[]{:S(2)}, u32[]{:S(2)}) collective-permute-start(bf16[768,256]{1,0:T(8,128)(2,1)S(1)} %bitcast.54), channel_id=1, source_target_pairs={{0,64},{1,65},{2,66},{3,67},{4,68},{5,69},{6,70},{7,71},{8,72},{9,... | collective-permute-start | bytes 1179656 | tf_op jit(solution)/shard_map/ppermute | solution.py:28
  145.0 20.0 %collective-permute-start.22 = (bf16[768,256]{1,0:T(8,128)(2,1)S(1)}, bf16[768,256]{1,0:T(8,128)(2,1)}, u32[]{:S(2)}, u32[]{:S(2)}) collective-permute-start(bf16[768,256]{1,0:T(8,128)(2,1)S(1)} %bitcast.55), channel_id=1, source_target_pairs={{0,8},{1,9},{2,10},{3,11},{4,12},{5,13},{6,14},{7,15},{8,0},{9,1},... | collective-permute-start | bytes 1179656 | tf_op jit(solution)/shard_map/ppermute | solution.py:28
  159.7 5.8 %collective-permute-start.23 = (bf16[768,256]{1,0:T(8,128)(2,1)}, bf16[768,256]{1,0:T(8,128)(2,1)S(1)}, u32[]{:S(2)}, u32[]{:S(2)}) collective-permute-start(bf16[768,256]{1,0:T(8,128)(2,1)} %collective-permute-done.18.refs_2_), channel_id=1, source_target_pairs={{0,8},{1,9},{2,10},{3,11},{4,12},{5,13},{6,14},{7,15},{8,0},{9,1},... | collective-permute-start | bytes 1179656 | tf_op jit(solution)/shard_map/ppermute | solution.py:28
  163.7 4.2 %collective-permute-start.24 = (bf16[768,256]{1,0:T(8,128)(2,1)}, bf16[768,256]{1,0:T(8,128)(2,1)S(1)}, u32[]{:S(2)}, u32[]{:S(2)}) collective-permute-start(bf16[768,256]{1,0:T(8,128)(2,1)} %collective-permute-done.19.refs_4_), channel_id=1, source_target_pairs={{0,8},{1,9},{2,10},{3,11},{4,12},{5,13},{6,14},{7,15},{8,0},{9,1},... | collective-permute-start | bytes 1179656 | tf_op jit(solution)/shard_map/ppermute | solution.py:28
  163.8 5.4 %collective-permute-start.25 = (bf16[768,256]{1,0:T(8,128)(2,1)}, bf16[768,256]{1,0:T(8,128)(2,1)S(1)}, u32[]{:S(2)}, u32[]{:S(2)}) collective-permute-start(bf16[768,256]{1,0:T(8,128)(2,1)} %collective-permute-done.20.refs_6_), channel_id=1, source_target_pairs={{0,8},{1,9},{2,10},{3,11},{4,12},{5,13},{6,14},{7,15},{8,0},{9,1},... | collective-permute-start | bytes 1179656 | tf_op jit(solution)/shard_map/ppermute | solution.py:28
  164.2 5.0 %collective-permute-start.26 = (bf16[768,256]{1,0:T(8,128)(2,1)}, bf16[768,256]{1,0:T(8,128)(2,1)S(1)}, u32[]{:S(2)}, u32[]{:S(2)}) collective-permute-start(bf16[768,256]{1,0:T(8,128)(2,1)} %collective-permute-done.21.refs_8_), channel_id=1, source_target_pairs={{0,8},{1,9},{2,10},{3,11},{4,12},{5,13},{6,14},{7,15},{8,0},{9,1},... | collective-permute-start | bytes 1179656 | tf_op jit(solution)/shard_map/ppermute | solution.py:28
  165.0 13.5 %copy-start.11 = (f32[768,1,256]{2,1,0:T(1,128)S(1)}, f32[768,1,256]{2,1,0:T(1,128)}, u32[]{:S(2)}) copy-start(f32[768,1,256]{2,1,0:T(1,128)} %param.6) | copy-start | bytes 2359300
  165.0 19.9 %collective-permute-start.27 = (bf16[768,256]{1,0:T(8,128)(2,1)}, bf16[768,256]{1,0:T(8,128)(2,1)S(1)}, u32[]{:S(2)}, u32[]{:S(2)}) collective-permute-start(bf16[768,256]{1,0:T(8,128)(2,1)} %collective-permute-done.18.refs_2_), channel_id=1, source_target_pairs={{0,32},{1,33},{2,34},{3,35},{4,36},{5,37},{6,38},{7,39},{8,40},{9,... | collective-permute-start | bytes 1179656 | tf_op jit(solution)/shard_map/ppermute | solution.py:28
  165.4 3.7 %copy-start.17 = (bf16[768,256]{1,0:T(8,128)(2,1)}, bf16[768,256]{1,0:T(8,128)(2,1)S(1)}, u32[]{:S(2)}) copy-start(bf16[768,256]{1,0:T(8,128)(2,1)S(1)} %collective-permute-done.23.refs_3_) | copy-start | bytes 1179652
  165.4 19.5 %collective-permute-start.28 = (bf16[768,256]{1,0:T(8,128)(2,1)}, bf16[768,256]{1,0:T(8,128)(2,1)S(1)}, u32[]{:S(2)}, u32[]{:S(2)}) collective-permute-start(bf16[768,256]{1,0:T(8,128)(2,1)} %collective-permute-done.18.refs_2_), channel_id=1, source_target_pairs={{0,96},{1,97},{2,98},{3,99},{4,100},{5,101},{6,102},{7,103},{8,104... | collective-permute-start | bytes 1179656 | tf_op jit(solution)/shard_map/ppermute | solution.py:28
  167.9 1.3 copy-start.18
  167.9 17.1 %collective-permute-start.29 = (bf16[768,256]{1,0:T(8,128)(2,1)}, bf16[768,256]{1,0:T(8,128)(2,1)S(1)}, u32[]{:S(2)}, u32[]{:S(2)}) collective-permute-start(bf16[768,256]{1,0:T(8,128)(2,1)} %collective-permute-done.21.refs_8_), channel_id=1, source_target_pairs={{0,16},{1,17},{2,18},{3,19},{4,20},{5,21},{6,22},{7,23},{8,24},{9,... | collective-permute-start | bytes 1179656 | tf_op jit(solution)/shard_map/ppermute | solution.py:28
  169.9 0.8 copy-start.20
  179.3 6.4 %collective-permute-start.33 = (f32[1,256]{1,0:T(1,128)S(1)}, f32[1,256]{1,0:T(1,128)S(1)}, u32[]{:S(2)}, u32[]{:S(2)}) collective-permute-start(f32[1,256]{1,0:T(1,128)S(1)} %get-tuple-element.73), channel_id=1, source_target_pairs={{8,0},{16,8},{24,16},{32,24},{40,32},{48,40},{56,48},{64,56},{72,6... | collective-permute-start | bytes 3080 | tf_op jit(solution)/shard_map/ppermute | solution.py:415
  182.4 3.3 %collective-permute-start.34 = (f32[1,256]{1,0:T(1,128)S(1)}, f32[1,256]{1,0:T(1,128)S(1)}, u32[]{:S(2)}, u32[]{:S(2)}) collective-permute-start(f32[1,256]{1,0:T(1,128)S(1)} %get-tuple-element.72), channel_id=1, source_target_pairs={{0,8},{8,16},{16,24},{24,32},{32,40},{40,48},{48,56},{56,64},{64,7... | collective-permute-start | bytes 3080 | tf_op jit(solution)/shard_map/ppermute | solution.py:414
  184.9 3.0 %copy-start.21 = (bf16[768,256]{1,0:T(8,128)(2,1)}, bf16[768,256]{1,0:T(8,128)(2,1)S(1)}, u32[]{:S(2)}) copy-start(bf16[768,256]{1,0:T(8,128)(2,1)S(1)} %collective-permute-done.27.refs_0_) | copy-start | bytes 1179652
  185.0 3.0 %copy-start.22 = (bf16[768,256]{1,0:T(8,128)(2,1)}, bf16[768,256]{1,0:T(8,128)(2,1)S(1)}, u32[]{:S(2)}) copy-start(bf16[768,256]{1,0:T(8,128)(2,1)S(1)} %collective-permute-done.28.refs_2_) | copy-start | bytes 1179652
  185.0 2.9 %copy-start.23 = (bf16[768,256]{1,0:T(8,128)(2,1)}, bf16[768,256]{1,0:T(8,128)(2,1)S(1)}, u32[]{:S(2)}) copy-start(bf16[768,256]{1,0:T(8,128)(2,1)S(1)} %collective-permute-done.29.refs_4_) | copy-start | bytes 1179652
  185.0 1.8 collective-permute-start.30
  185.1 2.3 %collective-permute-start.31 = (bf16[768,256]{1,0:T(8,128)(2,1)S(1)}, bf16[768,256]{1,0:T(8,128)(2,1)S(1)}, u32[]{:S(2)}, u32[]{:S(2)}) collective-permute-start(bf16[768,256]{1,0:T(8,128)(2,1)S(1)} %collective-permute-done.28.refs_2_), channel_id=1, source_target_pairs={{0,8},{1,9},{2,10},{3,11},{4,12},{5,13},{6,14},{7,15},{8,0},{9,1},... | collective-permute-start | bytes 1179656 | tf_op jit(solution)/shard_map/ppermute | solution.py:28
  185.6 2.3 %collective-permute-start.32 = (bf16[768,256]{1,0:T(8,128)(2,1)S(1)}, bf16[768,256]{1,0:T(8,128)(2,1)S(1)}, u32[]{:S(2)}, u32[]{:S(2)}) collective-permute-start(bf16[768,256]{1,0:T(8,128)(2,1)S(1)} %collective-permute-done.29.refs_4_), channel_id=1, source_target_pairs={{0,8},{1,9},{2,10},{3,11},{4,12},{5,13},{6,14},{7,15},{8,0},{9,1},... | collective-permute-start | bytes 1179656 | tf_op jit(solution)/shard_map/ppermute | solution.py:28
  186.2 26.7 %copy-start.3 = (f32[768,1,256]{2,0,1:T(8,128)S(1)}, f32[768,1,256]{2,0,1:T(8,128)}, u32[]{:S(2)}) copy-start(f32[768,1,256]{2,0,1:T(8,128)} %copy-done.2) | copy-start | bytes 2359300
  186.8 1.1 copy-start.24
  187.4 0.8 copy-start.25
  (2 other events, 1.5 us)
Sparse Core Ops, SparseCore 0:
  11.2 72.4 all-gather.2

commit v5 on v4

--- a/solution.py
+++ b/solution.py
@@ -56,8 +56,19 @@
     pieces = [cells, others[0], side, others[1], up, others[2], down, others[3], across, others[4]]
     carry = mix_part(kernel, pieces, order[:10], None, F32)
     if not spread:
-        carry, *waiting = together(carry, *waiting)
-    carry, side_up, side_down, side_across = together(carry, side_up, side_down, side_across)
+        image, edges = waiting[0], waiting[1:]
+        carry, image = together(carry, image)
+        following = [(i, i + 1) for i in range(RING * PAIR * CORES - 1)]
+        previous = [(i + 1, i) for i in range(RING * PAIR * CORES - 1)]
+        waiting = [
+            lax.ppermute(edges[0], "geno", following),
+            lax.ppermute(edges[1], "geno", previous),
+        ]
+    carry, side_up, side_down, side_across, *waiting = together(
+        carry, side_up, side_down, side_across, *waiting
+    )
+    if not spread:
+        waiting = [image, *waiting]
     pieces = []
     for piece in (side_up, side_down, side_across):
         pieces += [piece, hop(piece, core=1)]
@@ -405,14 +416,18 @@
     image_r, sums = cross_first(order, mixed_r, slabs, strips, total_rows, devices)
     turned, factors = cross_second(order, exchange(sums), slabs, image_r, strips)
     turned, image_r = together(swap(turned), image_r)
-    gathered, (image,) = gather_geno(turned.reshape(rows, cols), kernel_geno, swap(image_r))
-
     alpha, beta, new = factors[:, 0:1], factors[:, 1:2], factors[:, 2:3]
+    image = swap(image_r)
+    last, first = image[-1, -1:], image[0, :1]
+    last = right[-1:] - alpha * last + beta * right[-1:]
+    first = right[:1] - alpha * first + beta * right[:1]
+    gathered, (image, above, below) = gather_geno(
+        turned.reshape(rows, cols), kernel_geno, image, last, first
+    )
+
     image = image.reshape(rows, cols)
     residual = right - alpha * image
     direction = residual + beta * right
-    above = lax.ppermute(direction[-1:], "geno", following)
-    below = lax.ppermute(direction[:1], "geno", previous)
     position = (geno * rows - 1 + lax.iota(jnp.int32, rows + 1))[:, None]
     links = linked(position, row_length[None].astype(F32), total_rows)
     field = field_of(direction, above, below, links, field_coef[None])

time: 222 us -> 220 us (level)
  waiting for transfers between devices: 47.7 us -> 40.7 us
    ppermute x31, waiting for transfers between devices: 29.8 us -> 21.3 us  [hop(): return lax.ppermute(cells, BOTH, pairs)]
    all_to_all x3, waiting for transfers between devices: 9.11 us -> 14.5 us  [swap(): lax.all_to_all(slabs, 'trial', split_axis=0, concat_axis=0, tiled=True)]
    all_gather x1, waiting for transfers between devices: 5.25 us -> 1.42 us  [on_device(): strips = lax.all_gather(strip, 'trial', axis=0)]
    unnamed x55 -> x59, local copies, waits for them, and re-layouts: 7.93 us -> 8.71 us
  transfers between devices with their start and end apart: 39 -> 39, of which waited for: 14 -> 18; matrix products, arithmetic and copies ran while one was open for 2% -> 3% of each run, Pallas kernels for 9% -> 9%
where the time goes in v5:
time: 220 us
  starting transfers between devices  60.1 us (27%)
  blocking collectives  49.2 us (22%)
  waiting for transfers between devices  40.7 us (19%)
  Pallas kernels  38.4 us (17%)
  between operations  14.6 us (7%)
  local copies, waits for them, and re-layouts  10.4 us (5%)
  other arithmetic  6.28 us (3%)
    all_to_all x2, blocking collectives, exchange(): return lax.all_to_all(rows, BOTH, 0, 0, tiled=True)  37.6 us
    ppermute x31, starting transfers between devices, hop(): return lax.ppermute(cells, BOTH, pairs)  34.2 us
    pallas_call x4, Pallas kernels, mix(): pl.pallas_call(body, out_shape=shapes, in_specs=[SMEM] + [HBM] * (1 + cou...  25.6 us
    ppermute x31, waiting for transfers between devices, hop(): return lax.ppermute(cells, BOTH, pairs)  21.3 us
    all_to_all x3, starting transfers between devices, swap(): lax.all_to_all(slabs, 'trial', split_axis=0, concat_axis=0, tiled=True)  15.5 us
    all_to_all x3, waiting for transfers between devices, swap(): lax.all_to_all(slabs, 'trial', split_axis=0, concat_axis=0, tiled=True)  14.5 us
    all_to_all x1, blocking collectives, swap(): lax.all_to_all(slabs, 'trial', split_axis=0, concat_axis=0, tiled=True)  11.6 us
    pallas_call x2, Pallas kernels, cross_call(): pl.pallas_call(body, out_shape=shapes, in_specs=[SMEM if x.ndim == 1 else...  10.7 us
  transfers between devices with their start and end apart: 39, of which 18 were waited for; matrix products, arithmetic and copies ran while one was open for 3% of the time, Pallas kernels for 9%

profile of v5, /device:TPU:1, one launch (start us, length us, event | category | flops | bytes accessed | tf_op | source)
XLA Modules:
  0.0 219.7 jit_solution(14910405315181739545)
XLA Ops:
  7.3 1.1 copy-done
  8.4 0.8 constant_dynamic-slice_fusion.1
  9.3 1.8 fusion.6
  11.3 2.5 %collective-permute-start = (bf16[768,256]{1,0:T(8,128)(2,1)S(1)}, bf16[768,256]{1,0:T(8,128)(2,1)S(1)}, u32[]{:S(2)}, u32[]{:S(2)}) collective-permute-start(bf16[768,256]{1,0:T(8,128)(2,1)S(1)} %multiply_convert_fusion.refs_0_), channel_id=1, source_target_pairs={{0,16},{1,17},{2,18},{3,19},{4,20},{5,21},{6,22},{7,23},{8,24},{9,... | collective-permute-start | bytes 1179656 | tf_op jit(solution)/shard_map/ppermute | solution.py:28
  13.8 1.3 collective-permute-start.1
  15.1 1.4 collective-permute-start.2
  16.6 1.6 collective-permute-start.3
  18.2 3.4 %collective-permute-start.4 = (f32[1,256]{1,0:T(1,128)S(1)}, f32[1,256]{1,0:T(1,128)S(1)}, u32[]{:S(2)}, u32[]{:S(2)}) collective-permute-start(f32[1,256]{1,0:T(1,128)S(1)} %get-tuple-element.85), channel_id=1, source_target_pairs={{0,8},{8,16},{16,24},{24,32},{32,40},{40,48},{48,56},{56,64},{64,7... | collective-permute-start | bytes 3080 | tf_op jit(solution)/shard_map/ppermute | solution.py:403
  21.6 0.7 collective-permute-done.4.above_ref
  22.3 1.9 collective-permute-start.5
  24.3 1.2 copy.18
  25.5 2.7 %collective-permute-done.5.below_ref = f32[1,256]{1,0:T(1,128)S(1)} collective-permute-done((f32[1,256]{1,0:T(1,128)S(1)}, f32[1,256]{1,0:T(1,128)S(1)}, u32[]{:S(2)}, u32[]{:S(2)}) %collective-permute-start.5) | collective-permute-done | bytes 1056 | tf_op jit(solution)/shard_map/ppermute | solution.py:404
  28.4 1.0 copy-done.4
  29.5 0.7 copy-done.16
  30.3 0.8 copy-done.17
  31.0 3.4 %collective-permute-done.3.refs_8_ = bf16[768,256]{1,0:T(8,128)(2,1)} collective-permute-done((bf16[768,256]{1,0:T(8,128)(2,1)S(1)}, bf16[768,256]{1,0:T(8,128)(2,1)}, u32[]{:S(2)}, u32[]{:S(2)}) %collective-permute-start.3) | collective-permute-done | bytes 393248 | tf_op jit(solution)/shard_map/ppermute | solution.py:28
  34.5 7.0 %all-to-all-start = ((bf16[8,304,256]{2,1,0:T(8,128)(2,1)}), bf16[8,304,256]{2,1,0:T(8,128)(2,1)S(1)}, u32[]{:S(2)}, u32[]{:S(2)}) async-start(bf16[8,304,256]{2,1,0:T(8,128)(2,1)} %copy-done.4), calls=%async_computation | async-start | bytes 2490368 | tf_op jit(solution)/shard_map/all_to_all | solution.py:142
  41.5 2.2 %collective-permute-start.6 = (bf16[768,256]{1,0:T(8,128)(2,1)S(1)}, bf16[768,256]{1,0:T(8,128)(2,1)S(1)}, u32[]{:S(2)}, u32[]{:S(2)}) collective-permute-start(bf16[768,256]{1,0:T(8,128)(2,1)S(1)} %multiply_convert_fusion.refs_0_), channel_id=1, source_target_pairs={{0,8},{1,9},{2,10},{3,11},{4,12},{5,13},{6,14},{7,15},{8,0},{9,1},... | collective-permute-start | bytes 1179656 | tf_op jit(solution)/shard_map/ppermute | solution.py:28
  45.1 0.8 copy-done.18
  45.8 3.2 %collective-permute-start.11 = (bf16[768,256]{1,0:T(8,128)(2,1)}, bf16[768,256]{1,0:T(8,128)(2,1)S(1)}, u32[]{:S(2)}, u32[]{:S(2)}) collective-permute-start(bf16[768,256]{1,0:T(8,128)(2,1)} %copy-done.14), channel_id=1, source_target_pairs={{0,32},{1,33},{2,34},{3,35},{4,36},{5,37},{6,38},{7,39},{8,40},{9,... | collective-permute-start | bytes 1179656 | tf_op jit(solution)/shard_map/ppermute | solution.py:28
  49.1 1.5 collective-permute-start.12
  50.6 1.1 collective-permute-start.13
  51.8 7.2 %shard_map.78.refs_6_ = f32[768,256]{1,0:T(8,128)S(1)} custom-call(s32[10]{0:T(128)S(1)} %stack.99.order_ref, bf16[768,12288]{1,0:T(8,128)(2,1)} %kernel_ref.3, bf16[768,256]{1,0:T(8,128)(2,1)} %copy-done.13, bf16[768,256]{1,0:T(8,128)(2,1)} %copy-done.18, bf16[768,256]{1,0:T(8,128)(2,1)} %copy-done.14, bf16[768,256]{1,0:T(8,128)(2,1)} %collective-permute-done.7.refs_3_, ...), custom_call_target="tpu_custom_call" | custom-call | tf_op jit(solution)/shard_map/pallas_call | solution.py:195
  59.0 0.9 copy-done.5
  60.0 9.3 %collective-permute-done.13.refs_4_ = bf16[768,256]{1,0:T(8,128)(2,1)} collective-permute-done((bf16[768,256]{1,0:T(8,128)(2,1)}, bf16[768,256]{1,0:T(8,128)(2,1)}, u32[]{:S(2)}, u32[]{:S(2)}) %collective-permute-start.13) | collective-permute-done | bytes 393248 | tf_op jit(solution)/shard_map/ppermute | solution.py:28
  69.3 1.2 collective-permute-start.14
  70.5 0.5 collective-permute-start.16
  71.0 1.4 collective-permute-done.14.refs_1_
  72.7 0.6 collective-permute-done.16.refs_5_
  73.3 1.1 copy-done.6
  74.4 5.9 %shard_map.79 = bf16[768,256]{1,0:T(8,128)(2,1)} custom-call(s32[6]{0:T(128)S(1)} %stack.85.order_ref, bf16[768,12288]{1,0:T(8,128)(2,1)} %kernel_ref.3, bf16[768,256]{1,0:T(8,128)(2,1)} %copy-done.15, bf16[768,256]{1,0:T(8,128)(2,1)} %collective-permute-done.14.refs_1_, bf16[768,256]{1,0:T(8,128)(2,1)} %collective-permute-done.12.refs_2_, ...), custom_call_target="tpu_custom_call" | custom-call | tf_op jit(solution)/shard_map/pallas_call | solution.py:195
  80.3 1.4 all-gather.3.cloned.1.call-done
  81.7 0.9 collective-permute-start.17
  82.6 4.9 %all-to-all-start.1 = ((bf16[8,96,256]{2,1,0:T(8,128)(2,1)}), bf16[8,96,256]{2,1,0:T(8,128)(2,1)S(1)}, u32[]{:S(2)}, u32[]{:S(2)}) async-start(bf16[8,96,256]{2,1,0:T(8,128)(2,1)} %bitcast.23), calls=%async_computation.1 | async-start | bytes 786432 | tf_op jit(solution)/shard_map/all_to_all | solution.py:142
  87.6 9.4 %all-to-all-done.1.mixed_ref = bf16[8,96,256]{2,1,0:T(8,128)(2,1)S(1)} async-done(((bf16[8,96,256]{2,1,0:T(8,128)(2,1)}), bf16[8,96,256]{2,1,0:T(8,128)(2,1)S(1)}, u32[]{:S(2)}, u32[]{:S(2)}) %all-to-all-start.1) | async-done | bytes 393248 | tf_op jit(solution)/shard_map/all_to_all | solution.py:142
  97.1 5.8 %shard_map.80 = (f32[8,96,256]{2,1,0:T(8,128)S(1)}, f32[128,1,128]{2,1,0:T(1,128)S(1)}) custom-call(s32[2]{0:T(128)S(1)} %pad_add_fusion.order_ref, bf16[8,96,256]{2,1,0:T(8,128)(2,1)S(1)} %all-to-all-done.1.mixed_ref, bf16[8,304,256]{2,1,0:T(8,128)(2,1)S(1)} %all-to-all-done.slab_ref, bf16[8,128,1280]{2,1,0:T(8,128)(2,1)} %bitcast.65, ...), custom_call_target="tpu_custom_call" | custom-call | flops 805306368 | bytes 8388608 | tf_op jit(solution)/shard_map/pallas_call | solution.py:271
  102.9 18.2 %all_to_all.30.sums_ref = f32[128,1,128]{2,1,0:T(1,128)S(1)} all-to-all(f32[128,1,128]{2,1,0:T(1,128)S(1)} %get-tuple-element.56), channel_id=1, replica_groups=mesh['geno'=16,'trial'=8] {'geno','trial'}, dimensions={0} | all-to-all | bytes 131072 | tf_op jit(solution)/shard_map/all_to_all | solution.py:146
  121.1 4.9 %shard_map.81 = (bf16[8,96,256]{2,1,0:T(8,128)(2,1)S(1)}, f32[1,128]{1,0:T(1,128)S(1)}) custom-call(s32[2]{0:T(128)S(1)} %pad_add_fusion.order_ref, f32[128,1,128]{2,1,0:T(1,128)S(1)} %all_to_all.30.sums_ref, bf16[8,304,256]{2,1,0:T(8,128)(2,1)S(1)} %all-to-all-done.slab_ref, f32[8,96,256]{2,1,0:T(8,128)S(1)} %get-tuple-element.60.image_ref, ...), custom_call_target="tpu_custom_call" | custom-call | flops 805306368 | bytes 8388608 | tf_op jit(solution)/shard_map/pallas_call | solution.py:271
  126.1 11.6 %all_to_all.31 = bf16[8,96,256]{2,1,0:T(8,128)(2,1)S(1)} all-to-all(bf16[8,96,256]{2,1,0:T(8,128)(2,1)S(1)} %get-tuple-element.58), channel_id=1, replica_groups=mesh['geno'=16,'trial'=8] {'trial'}, dimensions={0} | all-to-all | bytes 786432 | tf_op jit(solution)/shard_map/all_to_all | solution.py:142
  137.7 3.5 %all-to-all-start.4 = ((f32[8,96,256]{2,1,0:T(8,128)}), f32[8,96,256]{2,1,0:T(8,128)S(1)}, u32[]{:S(2)}, u32[]{:S(2)}) async-start(f32[8,96,256]{2,1,0:T(8,128)} %copy-done.7), calls=%async_computation.4 | async-start | bytes 1572864 | tf_op jit(solution)/shard_map/all_to_all | solution.py:142
  141.9 2.3 %collective-permute-start.20 = (bf16[768,256]{1,0:T(8,128)(2,1)S(1)}, bf16[768,256]{1,0:T(8,128)(2,1)}, u32[]{:S(2)}, u32[]{:S(2)}) collective-permute-start(bf16[768,256]{1,0:T(8,128)(2,1)S(1)} %bitcast.69), channel_id=1, source_target_pairs={{0,96},{1,97},{2,98},{3,99},{4,100},{5,101},{6,102},{7,103},{8,104... | collective-permute-start | bytes 1179656 | tf_op jit(solution)/shard_map/ppermute | solution.py:28
  144.2 0.7 fusion.18
  144.9 3.0 %collective-permute-start.22 = (bf16[768,256]{1,0:T(8,128)(2,1)S(1)}, bf16[768,256]{1,0:T(8,128)(2,1)}, u32[]{:S(2)}, u32[]{:S(2)}) collective-permute-start(bf16[768,256]{1,0:T(8,128)(2,1)S(1)} %bitcast.71), channel_id=1, source_target_pairs={{0,8},{1,9},{2,10},{3,11},{4,12},{5,13},{6,14},{7,15},{8,0},{9,1},... | collective-permute-start | bytes 1179656 | tf_op jit(solution)/shard_map/ppermute | solution.py:28
  147.8 5.0 %all-to-all-done.4 = f32[8,96,256]{2,1,0:T(8,128)S(1)} async-done(((f32[8,96,256]{2,1,0:T(8,128)}), f32[8,96,256]{2,1,0:T(8,128)S(1)}, u32[]{:S(2)}, u32[]{:S(2)}) %all-to-all-start.4) | async-done | bytes 786464 | tf_op jit(solution)/shard_map/all_to_all | solution.py:142
  152.8 2.1 fusion.14
  154.9 3.8 %collective-permute-done.18.refs_2_ = bf16[768,256]{1,0:T(8,128)(2,1)} collective-permute-done((bf16[768,256]{1,0:T(8,128)(2,1)S(1)}, bf16[768,256]{1,0:T(8,128)(2,1)}, u32[]{:S(2)}, u32[]{:S(2)}) %collective-permute-start.18) | collective-permute-done | bytes 393248 | tf_op jit(solution)/shard_map/ppermute | solution.py:28
  158.8 3.9 %collective-permute-start.23 = (bf16[768,256]{1,0:T(8,128)(2,1)}, bf16[768,256]{1,0:T(8,128)(2,1)S(1)}, u32[]{:S(2)}, u32[]{:S(2)}) collective-permute-start(bf16[768,256]{1,0:T(8,128)(2,1)} %collective-permute-done.18.refs_2_), channel_id=1, source_target_pairs={{0,8},{1,9},{2,10},{3,11},{4,12},{5,13},{6,14},{7,15},{8,0},{9,1},... | collective-permute-start | bytes 1179656 | tf_op jit(solution)/shard_map/ppermute | solution.py:28
  162.9 0.4 collective-permute-start.25
  163.5 0.6 collective-permute-start.27
  164.3 2.7 %collective-permute-start.28 = (bf16[768,256]{1,0:T(8,128)(2,1)}, bf16[768,256]{1,0:T(8,128)(2,1)S(1)}, u32[]{:S(2)}, u32[]{:S(2)}) collective-permute-start(bf16[768,256]{1,0:T(8,128)(2,1)} %collective-permute-done.18.refs_2_), channel_id=1, source_target_pairs={{0,96},{1,97},{2,98},{3,99},{4,100},{5,101},{6,102},{7,103},{8,104... | collective-permute-start | bytes 1179656 | tf_op jit(solution)/shard_map/ppermute | solution.py:28
  167.0 1.3 collective-permute-start.29
  168.3 2.9 %collective-permute-start.30 = (f32[1,256]{1,0:T(1,128)S(1)}, f32[1,256]{1,0:T(1,128)S(1)}, u32[]{:S(2)}, u32[]{:S(2)}) collective-permute-start(f32[1,256]{1,0:T(1,128)S(1)} %get-tuple-element.69), channel_id=1, source_target_pairs={{0,8},{8,16},{16,24},{24,32},{32,40},{40,48},{48,56},{56,64},{64,7... | collective-permute-start | bytes 3080 | tf_op jit(solution)/shard_map/ppermute | solution.py:64
  171.2 2.1 collective-permute-start.31
  173.4 7.2 %shard_map.82.refs_6_ = f32[768,256]{1,0:T(8,128)S(1)} custom-call(s32[10]{0:T(128)S(1)} %stack.99.order_ref, bf16[768,12288]{1,0:T(8,128)(2,1)} %kernel_ref.3, bf16[768,256]{1,0:T(8,128)(2,1)} %bitcast.72, bf16[768,256]{1,0:T(8,128)(2,1)} %collective-permute-done.22.refs_1_, bf16[768,256]{1,0:T(8,128)(2,1)} %collective-permute-done.18.refs_2_, ...), custom_call_target="tpu_custom_call" | custom-call | tf_op jit(solution)/shard_map/pallas_call | solution.py:195
  180.6 0.7 broadcast_multiply_fusion
  181.4 0.8 bitcast_subtract_fusion
  182.3 0.5 collective-permute-start.33
  183.5 0.5 collective-permute-done.32.refs_1_
  184.1 0.6 collective-permute-done.33.refs_3_
  184.6 0.6 collective-permute-done.34.refs_5_
  185.4 0.8 copy-done.28
  186.1 5.3 %shard_map.83 = (f32[768,256]{1,0:T(8,128)S(1)}, f32[128,1,128]{2,1,0:T(1,128)S(1)}) custom-call(s32[6]{0:T(128)S(1)} %stack.85.order_ref, bf16[768,12288]{1,0:T(8,128)(2,1)} %kernel_ref.3, bf16[768,256]{1,0:T(8,128)(2,1)} %copy-done.23, bf16[768,256]{1,0:T(8,128)(2,1)} %copy-done.26, bf16[768,256]{1,0:T(8,128)(2,1)} %copy-done.24, ...), custom_call_target="tpu_custom_call" | custom-call | tf_op jit(solution)/shard_map/pallas_call | solution.py:195
  191.5 19.4 %all_to_all.32.sums_ref = f32[128,1,128]{2,1,0:T(1,128)S(1)} all-to-all(f32[128,1,128]{2,1,0:T(1,128)S(1)} %get-tuple-element.78), channel_id=1, replica_groups=mesh['geno'=16,'trial'=8] {'geno','trial'}, dimensions={0} | all-to-all | bytes 131072 | tf_op jit(solution)/shard_map/all_to_all | solution.py:146
  210.8 2.0 shard_map.84
  (104 shorter events, 4.8 us)
Async XLA Ops:
  7.2 1.2 copy-start
  7.2 3.9 %copy-start.10 = (f32[768,1,256]{2,1,0:T(1,128)S(1)}, f32[768,1,256]{2,1,0:T(1,128)}, u32[]{:S(2)}) copy-start(f32[768,1,256]{2,1,0:T(1,128)} %param.6) | copy-start | bytes 2359300
  7.2 3.9 %copy-start.1 = (s32[768,256]{1,0:T(8,128)S(1)}, s32[768,256]{1,0:T(8,128)}, u32[]{:S(2)}) copy-start(s32[768,256]{1,0:T(8,128)} %seen_ref.1) | copy-start | bytes 2359300
  7.2 74.5 %all-gather.3.cloned.1.call-start = ((), (), s32[]{:S(2)}) async-start(), calls=%async_computation.6 | async-start | bytes 2949120 | tf_op jit(solution)/shard_map/all_gather | solution.py:407
  9.2 19.0 %copy-start.8 = (f32[256]{0:T(256)S(1)}, f32[256]{0:T(256)}, u32[]{:S(2)}) copy-start(f32[256]{0:T(256)} %param.9) | copy-start | bytes 3076
  9.3 19.0 %copy-start.9 = (s32[256]{0:T(256)S(1)}, s32[256]{0:T(256)}, u32[]{:S(2)}) copy-start(s32[256]{0:T(256)} %param.8) | copy-start | bytes 3076
  11.3 30.2 %copy-start.13 = (bf16[768,256]{1,0:T(8,128)(2,1)}, bf16[768,256]{1,0:T(8,128)(2,1)S(1)}, u32[]{:S(2)}) copy-start(bf16[768,256]{1,0:T(8,128)(2,1)S(1)} %multiply_convert_fusion.refs_0_) | copy-start | bytes 1179652
  11.3 18.2 %collective-permute-start = (bf16[768,256]{1,0:T(8,128)(2,1)S(1)}, bf16[768,256]{1,0:T(8,128)(2,1)S(1)}, u32[]{:S(2)}, u32[]{:S(2)}) collective-permute-start(bf16[768,256]{1,0:T(8,128)(2,1)S(1)} %multiply_convert_fusion.refs_0_), channel_id=1, source_target_pairs={{0,16},{1,17},{2,18},{3,19},{4,20},{5,21},{6,22},{7,23},{8,24},{9,... | collective-permute-start | bytes 1179656 | tf_op jit(solution)/shard_map/ppermute | solution.py:28
  13.8 15.7 %collective-permute-start.1 = (bf16[768,256]{1,0:T(8,128)(2,1)S(1)}, bf16[768,256]{1,0:T(8,128)(2,1)S(1)}, u32[]{:S(2)}, u32[]{:S(2)}) collective-permute-start(bf16[768,256]{1,0:T(8,128)(2,1)S(1)} %multiply_convert_fusion.refs_0_), channel_id=1, source_target_pairs={{0,32},{1,33},{2,34},{3,35},{4,36},{5,37},{6,38},{7,39},{8,40},{9,... | collective-permute-start | bytes 1179656 | tf_op jit(solution)/shard_map/ppermute | solution.py:28
  15.1 14.4 %collective-permute-start.2 = (bf16[768,256]{1,0:T(8,128)(2,1)S(1)}, bf16[768,256]{1,0:T(8,128)(2,1)S(1)}, u32[]{:S(2)}, u32[]{:S(2)}) collective-permute-start(bf16[768,256]{1,0:T(8,128)(2,1)S(1)} %multiply_convert_fusion.refs_0_), channel_id=1, source_target_pairs={{0,96},{1,97},{2,98},{3,99},{4,100},{5,101},{6,102},{7,103},{8,104... | collective-permute-start | bytes 1179656 | tf_op jit(solution)/shard_map/ppermute | solution.py:28
  16.6 17.9 %collective-permute-start.3 = (bf16[768,256]{1,0:T(8,128)(2,1)S(1)}, bf16[768,256]{1,0:T(8,128)(2,1)}, u32[]{:S(2)}, u32[]{:S(2)}) collective-permute-start(bf16[768,256]{1,0:T(8,128)(2,1)S(1)} %multiply_convert_fusion.refs_0_), channel_id=1, source_target_pairs={{0,64},{1,65},{2,66},{3,67},{4,68},{5,69},{6,70},{7,71},{8,72},{9,... | collective-permute-start | bytes 1179656 | tf_op jit(solution)/shard_map/ppermute | solution.py:28
  18.2 4.1 %collective-permute-start.4 = (f32[1,256]{1,0:T(1,128)S(1)}, f32[1,256]{1,0:T(1,128)S(1)}, u32[]{:S(2)}, u32[]{:S(2)}) collective-permute-start(f32[1,256]{1,0:T(1,128)S(1)} %get-tuple-element.85), channel_id=1, source_target_pairs={{0,8},{8,16},{16,24},{24,32},{32,40},{40,48},{48,56},{56,64},{64,7... | collective-permute-start | bytes 3080 | tf_op jit(solution)/shard_map/ppermute | solution.py:403
  22.3 5.9 %collective-permute-start.5 = (f32[1,256]{1,0:T(1,128)S(1)}, f32[1,256]{1,0:T(1,128)S(1)}, u32[]{:S(2)}, u32[]{:S(2)}) collective-permute-start(f32[1,256]{1,0:T(1,128)S(1)} %get-tuple-element.84), channel_id=1, source_target_pairs={{8,0},{16,8},{24,16},{32,24},{40,32},{48,40},{56,48},{64,56},{72,6... | collective-permute-start | bytes 3080 | tf_op jit(solution)/shard_map/ppermute | solution.py:404
  25.5 9.0 %copy-start.2 = (f32[768,1,256]{2,0,1:T(8,128)}, f32[768,1,256]{2,0,1:T(8,128)S(1)}, u32[]{:S(2)}) copy-start(f32[768,1,256]{2,0,1:T(8,128)S(1)} %copy.18) | copy-start | bytes 2359300
  28.4 1.1 copy-start.4
  29.5 5.0 %copy-start.14 = (bf16[768,256]{1,0:T(8,128)(2,1)}, bf16[768,256]{1,0:T(8,128)(2,1)S(1)}, u32[]{:S(2)}) copy-start(bf16[768,256]{1,0:T(8,128)(2,1)S(1)} %collective-permute-done.refs_2_) | copy-start | bytes 1179652
  30.3 0.8 copy-start.17
  34.5 34.8 %all-to-all-start = ((bf16[8,304,256]{2,1,0:T(8,128)(2,1)}), bf16[8,304,256]{2,1,0:T(8,128)(2,1)S(1)}, u32[]{:S(2)}, u32[]{:S(2)}) async-start(bf16[8,304,256]{2,1,0:T(8,128)(2,1)} %copy-done.4), calls=%async_computation | async-start | bytes 2490368 | tf_op jit(solution)/shard_map/all_to_all | solution.py:142
  41.5 3.6 %collective-permute-start.6 = (bf16[768,256]{1,0:T(8,128)(2,1)S(1)}, bf16[768,256]{1,0:T(8,128)(2,1)S(1)}, u32[]{:S(2)}, u32[]{:S(2)}) collective-permute-start(bf16[768,256]{1,0:T(8,128)(2,1)S(1)} %multiply_convert_fusion.refs_0_), channel_id=1, source_target_pairs={{0,8},{1,9},{2,10},{3,11},{4,12},{5,13},{6,14},{7,15},{8,0},{9,1},... | collective-permute-start | bytes 1179656 | tf_op jit(solution)/shard_map/ppermute | solution.py:28
  43.7 5.3 %collective-permute-start.7 = (bf16[768,256]{1,0:T(8,128)(2,1)}, bf16[768,256]{1,0:T(8,128)(2,1)}, u32[]{:S(2)}, u32[]{:S(2)}) collective-permute-start(bf16[768,256]{1,0:T(8,128)(2,1)} %copy-done.14), channel_id=1, source_target_pairs={{0,8},{1,9},{2,10},{3,11},{4,12},{5,13},{6,14},{7,15},{8,0},{9,1},... | collective-permute-start | bytes 1179656 | tf_op jit(solution)/shard_map/ppermute | solution.py:28
  43.8 6.8 %collective-permute-start.10 = (bf16[768,256]{1,0:T(8,128)(2,1)}, bf16[768,256]{1,0:T(8,128)(2,1)}, u32[]{:S(2)}, u32[]{:S(2)}) collective-permute-start(bf16[768,256]{1,0:T(8,128)(2,1)} %collective-permute-done.3.refs_8_), channel_id=1, source_target_pairs={{0,8},{1,9},{2,10},{3,11},{4,12},{5,13},{6,14},{7,15},{8,0},{9,1},... | collective-permute-start | bytes 1179656 | tf_op jit(solution)/shard_map/ppermute | solution.py:28
  44.2 7.6 %collective-permute-start.8 = (bf16[768,256]{1,0:T(8,128)(2,1)}, bf16[768,256]{1,0:T(8,128)(2,1)}, u32[]{:S(2)}, u32[]{:S(2)}) collective-permute-start(bf16[768,256]{1,0:T(8,128)(2,1)} %copy-done.16), channel_id=1, source_target_pairs={{0,8},{1,9},{2,10},{3,11},{4,12},{5,13},{6,14},{7,15},{8,0},{9,1},... | collective-permute-start | bytes 1179656 | tf_op jit(solution)/shard_map/ppermute | solution.py:28
  44.3 7.5 %collective-permute-start.9 = (bf16[768,256]{1,0:T(8,128)(2,1)}, bf16[768,256]{1,0:T(8,128)(2,1)}, u32[]{:S(2)}, u32[]{:S(2)}) collective-permute-start(bf16[768,256]{1,0:T(8,128)(2,1)} %copy-done.17), channel_id=1, source_target_pairs={{0,8},{1,9},{2,10},{3,11},{4,12},{5,13},{6,14},{7,15},{8,0},{9,1},... | collective-permute-start | bytes 1179656 | tf_op jit(solution)/shard_map/ppermute | solution.py:28
  45.8 14.2 %collective-permute-start.11 = (bf16[768,256]{1,0:T(8,128)(2,1)}, bf16[768,256]{1,0:T(8,128)(2,1)S(1)}, u32[]{:S(2)}, u32[]{:S(2)}) collective-permute-start(bf16[768,256]{1,0:T(8,128)(2,1)} %copy-done.14), channel_id=1, source_target_pairs={{0,32},{1,33},{2,34},{3,35},{4,36},{5,37},{6,38},{7,39},{8,40},{9,... | collective-permute-start | bytes 1179656 | tf_op jit(solution)/shard_map/ppermute | solution.py:28
  49.1 10.9 %collective-permute-start.12 = (bf16[768,256]{1,0:T(8,128)(2,1)}, bf16[768,256]{1,0:T(8,128)(2,1)}, u32[]{:S(2)}, u32[]{:S(2)}) collective-permute-start(bf16[768,256]{1,0:T(8,128)(2,1)} %copy-done.14), channel_id=1, source_target_pairs={{0,96},{1,97},{2,98},{3,99},{4,100},{5,101},{6,102},{7,103},{8,104... | collective-permute-start | bytes 1179656 | tf_op jit(solution)/shard_map/ppermute | solution.py:28
  50.6 18.7 %collective-permute-start.13 = (bf16[768,256]{1,0:T(8,128)(2,1)}, bf16[768,256]{1,0:T(8,128)(2,1)}, u32[]{:S(2)}, u32[]{:S(2)}) collective-permute-start(bf16[768,256]{1,0:T(8,128)(2,1)} %copy-done.14), channel_id=1, source_target_pairs={{0,64},{1,65},{2,66},{3,67},{4,68},{5,69},{6,70},{7,71},{8,72},{9,... | collective-permute-start | bytes 1179656 | tf_op jit(solution)/shard_map/ppermute | solution.py:28
  59.0 0.9 copy-start.5
  60.0 13.3 %copy-start.15 = (bf16[768,256]{1,0:T(8,128)(2,1)}, bf16[768,256]{1,0:T(8,128)(2,1)S(1)}, u32[]{:S(2)}) copy-start(bf16[768,256]{1,0:T(8,128)(2,1)S(1)} %collective-permute-done.11.refs_0_) | copy-start | bytes 1179652
  69.3 3.2 %collective-permute-start.14 = (bf16[768,256]{1,0:T(8,128)(2,1)S(1)}, bf16[768,256]{1,0:T(8,128)(2,1)}, u32[]{:S(2)}, u32[]{:S(2)}) collective-permute-start(bf16[768,256]{1,0:T(8,128)(2,1)S(1)} %collective-permute-done.11.refs_0_), channel_id=1, source_target_pairs={{0,8},{1,9},{2,10},{3,11},{4,12},{5,13},{6,14},{7,15},{8,0},{9,1},... | collective-permute-start | bytes 1179656 | tf_op jit(solution)/shard_map/ppermute | solution.py:28
  70.4 2.3 %collective-permute-start.15 = (bf16[768,256]{1,0:T(8,128)(2,1)}, bf16[768,256]{1,0:T(8,128)(2,1)}, u32[]{:S(2)}, u32[]{:S(2)}) collective-permute-start(bf16[768,256]{1,0:T(8,128)(2,1)} %collective-permute-done.12.refs_2_), channel_id=1, source_target_pairs={{0,8},{1,9},{2,10},{3,11},{4,12},{5,13},{6,14},{7,15},{8,0},{9,1},... | collective-permute-start | bytes 1179656 | tf_op jit(solution)/shard_map/ppermute | solution.py:28
  70.5 2.8 %collective-permute-start.16 = (bf16[768,256]{1,0:T(8,128)(2,1)}, bf16[768,256]{1,0:T(8,128)(2,1)}, u32[]{:S(2)}, u32[]{:S(2)}) collective-permute-start(bf16[768,256]{1,0:T(8,128)(2,1)} %collective-permute-done.13.refs_4_), channel_id=1, source_target_pairs={{0,8},{1,9},{2,10},{3,11},{4,12},{5,13},{6,14},{7,15},{8,0},{9,1},... | collective-permute-start | bytes 1179656 | tf_op jit(solution)/shard_map/ppermute | solution.py:28
  73.3 1.1 copy-start.6
  81.7 15.3 %collective-permute-start.17 = (bf16[8,128,1280]{2,1,0:T(8,128)(2,1)}, bf16[8,128,1280]{2,1,0:T(8,128)(2,1)}, u32[]{:S(2)}, u32[]{:S(2)}) collective-permute-start(bf16[8,128,1280]{2,1,0:T(8,128)(2,1)} %bitcast.64), channel_id=1, source_target_pairs={{0,8},{1,9},{2,10},{3,11},{4,12},{5,13},{6,14},{7,15},{8,0},{9,1},... | collective-permute-start | bytes 7864328 | tf_op jit(solution)/shard_map/ppermute | solution.py:28
  82.6 14.5 %all-to-all-start.1 = ((bf16[8,96,256]{2,1,0:T(8,128)(2,1)}), bf16[8,96,256]{2,1,0:T(8,128)(2,1)S(1)}, u32[]{:S(2)}, u32[]{:S(2)}) async-start(bf16[8,96,256]{2,1,0:T(8,128)(2,1)} %bitcast.23), calls=%async_computation.1 | async-start | bytes 786432 | tf_op jit(solution)/shard_map/all_to_all | solution.py:142
  102.9 23.2 %copy-start.7 = (f32[8,96,256]{2,1,0:T(8,128)}, f32[8,96,256]{2,1,0:T(8,128)S(1)}, u32[]{:S(2)}) copy-start(f32[8,96,256]{2,1,0:T(8,128)S(1)} %get-tuple-element.60.image_ref) | copy-start | bytes 2359300
  137.7 35.7 %copy-start.12 = (bf16[8,96,256]{2,1,0:T(8,128)(2,1)}, bf16[8,96,256]{2,1,0:T(8,128)(2,1)S(1)}, u32[]{:S(2)}) copy-start(bf16[8,96,256]{2,1,0:T(8,128)(2,1)S(1)} %all_to_all.31) | copy-start | bytes 1179652
  137.7 15.1 %all-to-all-start.4 = ((f32[8,96,256]{2,1,0:T(8,128)}), f32[8,96,256]{2,1,0:T(8,128)S(1)}, u32[]{:S(2)}, u32[]{:S(2)}) async-start(f32[8,96,256]{2,1,0:T(8,128)} %copy-done.7), calls=%async_computation.4 | async-start | bytes 1572864 | tf_op jit(solution)/shard_map/all_to_all | solution.py:142
  141.3 17.4 %collective-permute-start.18 = (bf16[768,256]{1,0:T(8,128)(2,1)S(1)}, bf16[768,256]{1,0:T(8,128)(2,1)}, u32[]{:S(2)}, u32[]{:S(2)}) collective-permute-start(bf16[768,256]{1,0:T(8,128)(2,1)S(1)} %bitcast.67), channel_id=1, source_target_pairs={{0,16},{1,17},{2,18},{3,19},{4,20},{5,21},{6,22},{7,23},{8,24},{9,... | collective-permute-start | bytes 1179656 | tf_op jit(solution)/shard_map/ppermute | solution.py:28
  141.5 17.2 %collective-permute-start.19 = (bf16[768,256]{1,0:T(8,128)(2,1)S(1)}, bf16[768,256]{1,0:T(8,128)(2,1)}, u32[]{:S(2)}, u32[]{:S(2)}) collective-permute-start(bf16[768,256]{1,0:T(8,128)(2,1)S(1)} %bitcast.68), channel_id=1, source_target_pairs={{0,32},{1,33},{2,34},{3,35},{4,36},{5,37},{6,38},{7,39},{8,40},{9,... | collective-permute-start | bytes 1179656 | tf_op jit(solution)/shard_map/ppermute | solution.py:28
  141.9 16.8 %collective-permute-start.20 = (bf16[768,256]{1,0:T(8,128)(2,1)S(1)}, bf16[768,256]{1,0:T(8,128)(2,1)}, u32[]{:S(2)}, u32[]{:S(2)}) collective-permute-start(bf16[768,256]{1,0:T(8,128)(2,1)S(1)} %bitcast.69), channel_id=1, source_target_pairs={{0,96},{1,97},{2,98},{3,99},{4,100},{5,101},{6,102},{7,103},{8,104... | collective-permute-start | bytes 1179656 | tf_op jit(solution)/shard_map/ppermute | solution.py:28
  144.2 14.7 %collective-permute-start.21 = (bf16[768,256]{1,0:T(8,128)(2,1)S(1)}, bf16[768,256]{1,0:T(8,128)(2,1)}, u32[]{:S(2)}, u32[]{:S(2)}) collective-permute-start(bf16[768,256]{1,0:T(8,128)(2,1)S(1)} %bitcast.70), channel_id=1, source_target_pairs={{0,64},{1,65},{2,66},{3,67},{4,68},{5,69},{6,70},{7,71},{8,72},{9,... | collective-permute-start | bytes 1179656 | tf_op jit(solution)/shard_map/ppermute | solution.py:28
  144.9 18.6 %collective-permute-start.22 = (bf16[768,256]{1,0:T(8,128)(2,1)S(1)}, bf16[768,256]{1,0:T(8,128)(2,1)}, u32[]{:S(2)}, u32[]{:S(2)}) collective-permute-start(bf16[768,256]{1,0:T(8,128)(2,1)S(1)} %bitcast.71), channel_id=1, source_target_pairs={{0,8},{1,9},{2,10},{3,11},{4,12},{5,13},{6,14},{7,15},{8,0},{9,1},... | collective-permute-start | bytes 1179656 | tf_op jit(solution)/shard_map/ppermute | solution.py:28
  158.8 5.5 %collective-permute-start.23 = (bf16[768,256]{1,0:T(8,128)(2,1)}, bf16[768,256]{1,0:T(8,128)(2,1)S(1)}, u32[]{:S(2)}, u32[]{:S(2)}) collective-permute-start(bf16[768,256]{1,0:T(8,128)(2,1)} %collective-permute-done.18.refs_2_), channel_id=1, source_target_pairs={{0,8},{1,9},{2,10},{3,11},{4,12},{5,13},{6,14},{7,15},{8,0},{9,1},... | collective-permute-start | bytes 1179656 | tf_op jit(solution)/shard_map/ppermute | solution.py:28
  162.8 4.2 %collective-permute-start.24 = (bf16[768,256]{1,0:T(8,128)(2,1)}, bf16[768,256]{1,0:T(8,128)(2,1)S(1)}, u32[]{:S(2)}, u32[]{:S(2)}) collective-permute-start(bf16[768,256]{1,0:T(8,128)(2,1)} %collective-permute-done.19.refs_4_), channel_id=1, source_target_pairs={{0,8},{1,9},{2,10},{3,11},{4,12},{5,13},{6,14},{7,15},{8,0},{9,1},... | collective-permute-start | bytes 1179656 | tf_op jit(solution)/shard_map/ppermute | solution.py:28
  162.9 5.5 %collective-permute-start.25 = (bf16[768,256]{1,0:T(8,128)(2,1)}, bf16[768,256]{1,0:T(8,128)(2,1)S(1)}, u32[]{:S(2)}, u32[]{:S(2)}) collective-permute-start(bf16[768,256]{1,0:T(8,128)(2,1)} %collective-permute-done.20.refs_6_), channel_id=1, source_target_pairs={{0,8},{1,9},{2,10},{3,11},{4,12},{5,13},{6,14},{7,15},{8,0},{9,1},... | collective-permute-start | bytes 1179656 | tf_op jit(solution)/shard_map/ppermute | solution.py:28
  163.3 7.9 %collective-permute-start.26 = (bf16[768,256]{1,0:T(8,128)(2,1)}, bf16[768,256]{1,0:T(8,128)(2,1)S(1)}, u32[]{:S(2)}, u32[]{:S(2)}) collective-permute-start(bf16[768,256]{1,0:T(8,128)(2,1)} %collective-permute-done.21.refs_8_), channel_id=1, source_target_pairs={{0,8},{1,9},{2,10},{3,11},{4,12},{5,13},{6,14},{7,15},{8,0},{9,1},... | collective-permute-start | bytes 1179656 | tf_op jit(solution)/shard_map/ppermute | solution.py:28
  163.5 17.9 %copy-start.11 = (f32[768,1,256]{2,1,0:T(1,128)S(1)}, f32[768,1,256]{2,1,0:T(1,128)}, u32[]{:S(2)}) copy-start(f32[768,1,256]{2,1,0:T(1,128)} %param.6) | copy-start | bytes 2359300
  163.5 18.7 %collective-permute-start.27 = (bf16[768,256]{1,0:T(8,128)(2,1)}, bf16[768,256]{1,0:T(8,128)(2,1)S(1)}, u32[]{:S(2)}, u32[]{:S(2)}) collective-permute-start(bf16[768,256]{1,0:T(8,128)(2,1)} %collective-permute-done.18.refs_2_), channel_id=1, source_target_pairs={{0,32},{1,33},{2,34},{3,35},{4,36},{5,37},{6,38},{7,39},{8,40},{9,... | collective-permute-start | bytes 1179656 | tf_op jit(solution)/shard_map/ppermute | solution.py:28
  164.3 9.1 %copy-start.19 = (bf16[768,256]{1,0:T(8,128)(2,1)}, bf16[768,256]{1,0:T(8,128)(2,1)S(1)}, u32[]{:S(2)}) copy-start(bf16[768,256]{1,0:T(8,128)(2,1)S(1)} %collective-permute-done.23.refs_3_) | copy-start | bytes 1179652
  164.3 17.9 %collective-permute-start.28 = (bf16[768,256]{1,0:T(8,128)(2,1)}, bf16[768,256]{1,0:T(8,128)(2,1)S(1)}, u32[]{:S(2)}, u32[]{:S(2)}) collective-permute-start(bf16[768,256]{1,0:T(8,128)(2,1)} %collective-permute-done.18.refs_2_), channel_id=1, source_target_pairs={{0,96},{1,97},{2,98},{3,99},{4,100},{5,101},{6,102},{7,103},{8,104... | collective-permute-start | bytes 1179656 | tf_op jit(solution)/shard_map/ppermute | solution.py:28
  167.0 6.4 %copy-start.20 = (bf16[768,256]{1,0:T(8,128)(2,1)}, bf16[768,256]{1,0:T(8,128)(2,1)S(1)}, u32[]{:S(2)}) copy-start(bf16[768,256]{1,0:T(8,128)(2,1)S(1)} %collective-permute-done.24.refs_5_) | copy-start | bytes 1179652
  167.0 15.2 %collective-permute-start.29 = (bf16[768,256]{1,0:T(8,128)(2,1)}, bf16[768,256]{1,0:T(8,128)(2,1)S(1)}, u32[]{:S(2)}, u32[]{:S(2)}) collective-permute-start(bf16[768,256]{1,0:T(8,128)(2,1)} %collective-permute-done.21.refs_8_), channel_id=1, source_target_pairs={{0,16},{1,17},{2,18},{3,19},{4,20},{5,21},{6,22},{7,23},{8,24},{9,... | collective-permute-start | bytes 1179656 | tf_op jit(solution)/shard_map/ppermute | solution.py:28
  168.3 5.1 %copy-start.21 = (bf16[768,256]{1,0:T(8,128)(2,1)}, bf16[768,256]{1,0:T(8,128)(2,1)S(1)}, u32[]{:S(2)}) copy-start(bf16[768,256]{1,0:T(8,128)(2,1)S(1)} %collective-permute-done.25.refs_7_) | copy-start | bytes 1179652
  168.3 13.8 %collective-permute-start.30 = (f32[1,256]{1,0:T(1,128)S(1)}, f32[1,256]{1,0:T(1,128)S(1)}, u32[]{:S(2)}, u32[]{:S(2)}) collective-permute-start(f32[1,256]{1,0:T(1,128)S(1)} %get-tuple-element.69), channel_id=1, source_target_pairs={{0,8},{8,16},{16,24},{24,32},{32,40},{40,48},{48,56},{56,64},{64,7... | collective-permute-start | bytes 3080 | tf_op jit(solution)/shard_map/ppermute | solution.py:64
  171.2 2.2 %copy-start.22 = (bf16[768,256]{1,0:T(8,128)(2,1)}, bf16[768,256]{1,0:T(8,128)(2,1)S(1)}, u32[]{:S(2)}) copy-start(bf16[768,256]{1,0:T(8,128)(2,1)S(1)} %collective-permute-done.26.refs_9_) | copy-start | bytes 1179652
  171.2 10.9 %collective-permute-start.31 = (f32[1,256]{1,0:T(1,128)S(1)}, f32[1,256]{1,0:T(1,128)S(1)}, u32[]{:S(2)}, u32[]{:S(2)}) collective-permute-start(f32[1,256]{1,0:T(1,128)S(1)} %get-tuple-element.70), channel_id=1, source_target_pairs={{8,0},{16,8},{24,16},{32,24},{40,32},{48,40},{56,48},{64,56},{72,6... | collective-permute-start | bytes 3080 | tf_op jit(solution)/shard_map/ppermute | solution.py:65
  182.2 3.0 %copy-start.23 = (bf16[768,256]{1,0:T(8,128)(2,1)}, bf16[768,256]{1,0:T(8,128)(2,1)S(1)}, u32[]{:S(2)}) copy-start(bf16[768,256]{1,0:T(8,128)(2,1)S(1)} %collective-permute-done.27.refs_0_) | copy-start | bytes 1179652
  182.2 3.0 %copy-start.24 = (bf16[768,256]{1,0:T(8,128)(2,1)}, bf16[768,256]{1,0:T(8,128)(2,1)S(1)}, u32[]{:S(2)}) copy-start(bf16[768,256]{1,0:T(8,128)(2,1)S(1)} %collective-permute-done.28.refs_2_) | copy-start | bytes 1179652
  182.2 2.9 %copy-start.25 = (bf16[768,256]{1,0:T(8,128)(2,1)}, bf16[768,256]{1,0:T(8,128)(2,1)S(1)}, u32[]{:S(2)}) copy-start(bf16[768,256]{1,0:T(8,128)(2,1)S(1)} %collective-permute-done.29.refs_4_) | copy-start | bytes 1179652
  182.2 1.8 collective-permute-start.32
  182.3 2.3 %collective-permute-start.33 = (bf16[768,256]{1,0:T(8,128)(2,1)S(1)}, bf16[768,256]{1,0:T(8,128)(2,1)S(1)}, u32[]{:S(2)}, u32[]{:S(2)}) collective-permute-start(bf16[768,256]{1,0:T(8,128)(2,1)S(1)} %collective-permute-done.28.refs_2_), channel_id=1, source_target_pairs={{0,8},{1,9},{2,10},{3,11},{4,12},{5,13},{6,14},{7,15},{8,0},{9,1},... | collective-permute-start | bytes 1179656 | tf_op jit(solution)/shard_map/ppermute | solution.py:28
  182.8 2.3 %collective-permute-start.34 = (bf16[768,256]{1,0:T(8,128)(2,1)S(1)}, bf16[768,256]{1,0:T(8,128)(2,1)S(1)}, u32[]{:S(2)}, u32[]{:S(2)}) collective-permute-start(bf16[768,256]{1,0:T(8,128)(2,1)S(1)} %collective-permute-done.29.refs_4_), channel_id=1, source_target_pairs={{0,8},{1,9},{2,10},{3,11},{4,12},{5,13},{6,14},{7,15},{8,0},{9,1},... | collective-permute-start | bytes 1179656 | tf_op jit(solution)/shard_map/ppermute | solution.py:28
  183.5 27.3 %copy-start.3 = (f32[768,1,256]{2,0,1:T(8,128)S(1)}, f32[768,1,256]{2,0,1:T(8,128)}, u32[]{:S(2)}) copy-start(f32[768,1,256]{2,0,1:T(8,128)} %copy-done.2) | copy-start | bytes 2359300
  184.1 1.1 copy-start.26
  (4 other events, 3.0 us)
Sparse Core Ops, SparseCore 0:
  11.2 70.4 all-gather.2

commit v6 on v5

--- a/solution.py
+++ b/solution.py
@@ -169,10 +169,11 @@
         copies = []
         for k in range(count):
             at = pl.ds(pl.multiple_of(order_ref[k] * rows, rows), rows)
+            here = slice(k * rows, (k + 1) * rows)
             copies.append(
                 (
-                    pltpu.make_async_copy(kernel_ref.at[:, at], blocks.at[k], sems.at[k, 0]),
-                    pltpu.make_async_copy(piece_refs[k], cells.at[k], sems.at[k, 1]),
+                    pltpu.make_async_copy(kernel_ref.at[:, at], blocks.at[:, here], sems.at[k, 0]),
+                    pltpu.make_async_copy(piece_refs[k], cells.at[here], sems.at[k, 1]),
                 )
             )
         for pair in copies:
@@ -181,11 +182,12 @@
         if carry is not None:
             total[...] = rest[0][...]
             rest = rest[1:]
-        for k in range(count):
-            for copy in copies[k]:
+        for k in range(0, count, 2):
+            for copy in copies[k] + copies[k + 1]:
                 copy.wait()
+            two = slice(k * rows, (k + 2) * rows)
             for m in range(0, rows, 256):
-                term = jnp.dot(blocks[k, m : m + 256], cells[k], preferred_element_type=F32)
+                term = jnp.dot(blocks[m : m + 256, two], cells[two], preferred_element_type=F32)
                 if carry is None and k == 0:
                     total[m : m + 256] = term
                 else:
@@ -198,8 +200,8 @@
         in_specs=[SMEM] + [HBM] * (1 + count) + [VMEM] * len(others),
         out_specs=[VMEM] * len(shapes),
         scratch_shapes=[
-            pltpu.VMEM((count, rows, rows), BF16),
-            pltpu.VMEM((count, rows, cols), BF16),
+            pltpu.VMEM((rows, count * rows), BF16),
+            pltpu.VMEM((count * rows, cols), BF16),
             pltpu.VMEM((rows, cols), F32),
             pltpu.SemaphoreType.DMA((count, 2)),
         ],

time: 220 us -> 221 us (level)
  transfers between devices with their start and end apart: 39 -> 39, of which waited for: 18 -> 17; matrix products, arithmetic and copies ran while one was open for 3% -> 3% of each run, Pallas kernels for 9% -> 10%
where the time goes in v6:
time: 221 us; the launch traced here: 220 us
  starting transfers between devices  60.5 us (27%)
  blocking collectives  48.9 us (22%)
  waiting for transfers between devices  40.2 us (18%)
  Pallas kernels  39.4 us (18%)
  between operations  14.6 us (7%)
  local copies, waits for them, and re-layouts  10.4 us (5%)
  other arithmetic  6.28 us (3%)
    all_to_all x2, blocking collectives, exchange(): return lax.all_to_all(rows, BOTH, 0, 0, tiled=True)  37.2 us
    ppermute x31, starting transfers between devices, hop(): return lax.ppermute(cells, BOTH, pairs)  34.2 us
    pallas_call x4, Pallas kernels, mix(): pl.pallas_call(body, out_shape=shapes, in_specs=[SMEM] + [HBM] * (1 + cou...  26.5 us
    ppermute x31, waiting for transfers between devices, hop(): return lax.ppermute(cells, BOTH, pairs)  21.2 us
    all_to_all x3, starting transfers between devices, swap(): lax.all_to_all(slabs, 'trial', split_axis=0, concat_axis=0, tiled=True)  15.9 us
    all_to_all x3, waiting for transfers between devices, swap(): lax.all_to_all(slabs, 'trial', split_axis=0, concat_axis=0, tiled=True)  14.5 us
    all_to_all x1, blocking collectives, swap(): lax.all_to_all(slabs, 'trial', split_axis=0, concat_axis=0, tiled=True)  11.6 us
    pallas_call x2, Pallas kernels, cross_call(): pl.pallas_call(body, out_shape=shapes, in_specs=[SMEM if x.ndim == 1 else...  10.7 us
  transfers between devices with their start and end apart: 39, of which 17 were waited for; matrix products, arithmetic and copies ran while one was open for 3% of the time, Pallas kernels for 10%

profile of v6, /device:TPU:1, one launch (start us, length us, event | category | flops | bytes accessed | tf_op | source)
XLA Modules:
  0.0 220.1 jit_solution(10666866086225314940)
XLA Ops:
  7.3 1.1 copy-done
  8.4 0.8 constant_dynamic-slice_fusion.1
  9.3 1.8 fusion.6
  11.3 2.5 %collective-permute-start = (bf16[768,256]{1,0:T(8,128)(2,1)S(1)}, bf16[768,256]{1,0:T(8,128)(2,1)S(1)}, u32[]{:S(2)}, u32[]{:S(2)}) collective-permute-start(bf16[768,256]{1,0:T(8,128)(2,1)S(1)} %multiply_convert_fusion.refs_0_), channel_id=1, source_target_pairs={{0,16},{1,17},{2,18},{3,19},{4,20},{5,21},{6,22},{7,23},{8,24},{9,... | collective-permute-start | bytes 1179656 | tf_op jit(solution)/shard_map/ppermute | solution.py:28
  13.8 1.3 collective-permute-start.1
  15.1 1.4 collective-permute-start.2
  16.6 1.6 collective-permute-start.3
  18.2 3.4 %collective-permute-start.4 = (f32[1,256]{1,0:T(1,128)S(1)}, f32[1,256]{1,0:T(1,128)S(1)}, u32[]{:S(2)}, u32[]{:S(2)}) collective-permute-start(f32[1,256]{1,0:T(1,128)S(1)} %get-tuple-element.85), channel_id=1, source_target_pairs={{0,8},{8,16},{16,24},{24,32},{32,40},{40,48},{48,56},{56,64},{64,7... | collective-permute-start | bytes 3080 | tf_op jit(solution)/shard_map/ppermute | solution.py:405
  21.6 0.7 collective-permute-done.4.above_ref
  22.3 1.9 collective-permute-start.5
  24.3 1.2 copy.18
  25.5 2.7 %collective-permute-done.5.below_ref = f32[1,256]{1,0:T(1,128)S(1)} collective-permute-done((f32[1,256]{1,0:T(1,128)S(1)}, f32[1,256]{1,0:T(1,128)S(1)}, u32[]{:S(2)}, u32[]{:S(2)}) %collective-permute-start.5) | collective-permute-done | bytes 1056 | tf_op jit(solution)/shard_map/ppermute | solution.py:406
  28.4 1.0 copy-done.4
  29.5 0.7 copy-done.16
  30.3 0.8 copy-done.17
  31.0 3.4 %collective-permute-done.3.refs_8_ = bf16[768,256]{1,0:T(8,128)(2,1)} collective-permute-done((bf16[768,256]{1,0:T(8,128)(2,1)S(1)}, bf16[768,256]{1,0:T(8,128)(2,1)}, u32[]{:S(2)}, u32[]{:S(2)}) %collective-permute-start.3) | collective-permute-done | bytes 393248 | tf_op jit(solution)/shard_map/ppermute | solution.py:28
  34.5 7.0 %all-to-all-start = ((bf16[8,304,256]{2,1,0:T(8,128)(2,1)}), bf16[8,304,256]{2,1,0:T(8,128)(2,1)S(1)}, u32[]{:S(2)}, u32[]{:S(2)}) async-start(bf16[8,304,256]{2,1,0:T(8,128)(2,1)} %copy-done.4), calls=%async_computation | async-start | bytes 2490368 | tf_op jit(solution)/shard_map/all_to_all | solution.py:142
  41.5 2.2 %collective-permute-start.6 = (bf16[768,256]{1,0:T(8,128)(2,1)S(1)}, bf16[768,256]{1,0:T(8,128)(2,1)S(1)}, u32[]{:S(2)}, u32[]{:S(2)}) collective-permute-start(bf16[768,256]{1,0:T(8,128)(2,1)S(1)} %multiply_convert_fusion.refs_0_), channel_id=1, source_target_pairs={{0,8},{1,9},{2,10},{3,11},{4,12},{5,13},{6,14},{7,15},{8,0},{9,1},... | collective-permute-start | bytes 1179656 | tf_op jit(solution)/shard_map/ppermute | solution.py:28
  45.1 0.8 copy-done.18
  45.8 3.2 %collective-permute-start.11 = (bf16[768,256]{1,0:T(8,128)(2,1)}, bf16[768,256]{1,0:T(8,128)(2,1)S(1)}, u32[]{:S(2)}, u32[]{:S(2)}) collective-permute-start(bf16[768,256]{1,0:T(8,128)(2,1)} %copy-done.14), channel_id=1, source_target_pairs={{0,32},{1,33},{2,34},{3,35},{4,36},{5,37},{6,38},{7,39},{8,40},{9,... | collective-permute-start | bytes 1179656 | tf_op jit(solution)/shard_map/ppermute | solution.py:28
  49.1 1.5 collective-permute-start.12
  50.6 1.1 collective-permute-start.13
  51.8 7.3 %shard_map.78.refs_6_ = f32[768,256]{1,0:T(8,128)S(1)} custom-call(s32[10]{0:T(128)S(1)} %stack.99.order_ref, bf16[768,12288]{1,0:T(8,128)(2,1)} %kernel_ref.3, bf16[768,256]{1,0:T(8,128)(2,1)} %copy-done.13, bf16[768,256]{1,0:T(8,128)(2,1)} %copy-done.18, bf16[768,256]{1,0:T(8,128)(2,1)} %copy-done.14, bf16[768,256]{1,0:T(8,128)(2,1)} %collective-permute-done.7.refs_3_, ...), custom_call_target="tpu_custom_call" | custom-call | tf_op jit(solution)/shard_map/pallas_call | solution.py:197
  59.1 0.9 copy-done.5
  60.0 9.3 %collective-permute-done.13.refs_4_ = bf16[768,256]{1,0:T(8,128)(2,1)} collective-permute-done((bf16[768,256]{1,0:T(8,128)(2,1)}, bf16[768,256]{1,0:T(8,128)(2,1)}, u32[]{:S(2)}, u32[]{:S(2)}) %collective-permute-start.13) | collective-permute-done | bytes 393248 | tf_op jit(solution)/shard_map/ppermute | solution.py:28
  69.3 1.2 collective-permute-start.14
  70.5 0.5 collective-permute-start.16
  71.0 1.4 collective-permute-done.14.refs_1_
  72.7 0.6 collective-permute-done.16.refs_5_
  73.3 1.1 copy-done.6
  74.4 6.3 %shard_map.79 = bf16[768,256]{1,0:T(8,128)(2,1)} custom-call(s32[6]{0:T(128)S(1)} %stack.85.order_ref, bf16[768,12288]{1,0:T(8,128)(2,1)} %kernel_ref.3, bf16[768,256]{1,0:T(8,128)(2,1)} %copy-done.15, bf16[768,256]{1,0:T(8,128)(2,1)} %collective-permute-done.14.refs_1_, bf16[768,256]{1,0:T(8,128)(2,1)} %collective-permute-done.12.refs_2_, ...), custom_call_target="tpu_custom_call" | custom-call | tf_op jit(solution)/shard_map/pallas_call | solution.py:197
  80.7 1.1 all-gather.3.cloned.1.call-done
  81.7 0.9 collective-permute-start.17
  82.6 5.3 %all-to-all-start.1 = ((bf16[8,96,256]{2,1,0:T(8,128)(2,1)}), bf16[8,96,256]{2,1,0:T(8,128)(2,1)S(1)}, u32[]{:S(2)}, u32[]{:S(2)}) async-start(bf16[8,96,256]{2,1,0:T(8,128)(2,1)} %bitcast.23), calls=%async_computation.1 | async-start | bytes 786432 | tf_op jit(solution)/shard_map/all_to_all | solution.py:142
  88.0 9.4 %all-to-all-done.1.mixed_ref = bf16[8,96,256]{2,1,0:T(8,128)(2,1)S(1)} async-done(((bf16[8,96,256]{2,1,0:T(8,128)(2,1)}), bf16[8,96,256]{2,1,0:T(8,128)(2,1)S(1)}, u32[]{:S(2)}, u32[]{:S(2)}) %all-to-all-start.1) | async-done | bytes 393248 | tf_op jit(solution)/shard_map/all_to_all | solution.py:142
  97.4 5.8 %shard_map.80 = (f32[8,96,256]{2,1,0:T(8,128)S(1)}, f32[128,1,128]{2,1,0:T(1,128)S(1)}) custom-call(s32[2]{0:T(128)S(1)} %pad_add_fusion.order_ref, bf16[8,96,256]{2,1,0:T(8,128)(2,1)S(1)} %all-to-all-done.1.mixed_ref, bf16[8,304,256]{2,1,0:T(8,128)(2,1)S(1)} %all-to-all-done.slab_ref, bf16[8,128,1280]{2,1,0:T(8,128)(2,1)} %bitcast.65, ...), custom_call_target="tpu_custom_call" | custom-call | flops 805306368 | bytes 8388608 | tf_op jit(solution)/shard_map/pallas_call | solution.py:273
  103.3 17.9 %all_to_all.30.sums_ref = f32[128,1,128]{2,1,0:T(1,128)S(1)} all-to-all(f32[128,1,128]{2,1,0:T(1,128)S(1)} %get-tuple-element.56), channel_id=1, replica_groups=mesh['geno'=16,'trial'=8] {'geno','trial'}, dimensions={0} | all-to-all | bytes 131072 | tf_op jit(solution)/shard_map/all_to_all | solution.py:146
  121.1 4.9 %shard_map.81 = (bf16[8,96,256]{2,1,0:T(8,128)(2,1)S(1)}, f32[1,128]{1,0:T(1,128)S(1)}) custom-call(s32[2]{0:T(128)S(1)} %pad_add_fusion.order_ref, f32[128,1,128]{2,1,0:T(1,128)S(1)} %all_to_all.30.sums_ref, bf16[8,304,256]{2,1,0:T(8,128)(2,1)S(1)} %all-to-all-done.slab_ref, f32[8,96,256]{2,1,0:T(8,128)S(1)} %get-tuple-element.60.image_ref, ...), custom_call_target="tpu_custom_call" | custom-call | flops 805306368 | bytes 8388608 | tf_op jit(solution)/shard_map/pallas_call | solution.py:273
  126.1 11.6 %all_to_all.31 = bf16[8,96,256]{2,1,0:T(8,128)(2,1)S(1)} all-to-all(bf16[8,96,256]{2,1,0:T(8,128)(2,1)S(1)} %get-tuple-element.58), channel_id=1, replica_groups=mesh['geno'=16,'trial'=8] {'trial'}, dimensions={0} | all-to-all | bytes 786432 | tf_op jit(solution)/shard_map/all_to_all | solution.py:142
  137.7 3.5 %all-to-all-start.4 = ((f32[8,96,256]{2,1,0:T(8,128)}), f32[8,96,256]{2,1,0:T(8,128)S(1)}, u32[]{:S(2)}, u32[]{:S(2)}) async-start(f32[8,96,256]{2,1,0:T(8,128)} %copy-done.7), calls=%async_computation.4 | async-start | bytes 1572864 | tf_op jit(solution)/shard_map/all_to_all | solution.py:142
  141.9 2.3 %collective-permute-start.20 = (bf16[768,256]{1,0:T(8,128)(2,1)S(1)}, bf16[768,256]{1,0:T(8,128)(2,1)}, u32[]{:S(2)}, u32[]{:S(2)}) collective-permute-start(bf16[768,256]{1,0:T(8,128)(2,1)S(1)} %bitcast.69), channel_id=1, source_target_pairs={{0,96},{1,97},{2,98},{3,99},{4,100},{5,101},{6,102},{7,103},{8,104... | collective-permute-start | bytes 1179656 | tf_op jit(solution)/shard_map/ppermute | solution.py:28
  144.2 0.7 fusion.18
  144.9 3.0 %collective-permute-start.22 = (bf16[768,256]{1,0:T(8,128)(2,1)S(1)}, bf16[768,256]{1,0:T(8,128)(2,1)}, u32[]{:S(2)}, u32[]{:S(2)}) collective-permute-start(bf16[768,256]{1,0:T(8,128)(2,1)S(1)} %bitcast.71), channel_id=1, source_target_pairs={{0,8},{1,9},{2,10},{3,11},{4,12},{5,13},{6,14},{7,15},{8,0},{9,1},... | collective-permute-start | bytes 1179656 | tf_op jit(solution)/shard_map/ppermute | solution.py:28
  147.8 5.0 %all-to-all-done.4 = f32[8,96,256]{2,1,0:T(8,128)S(1)} async-done(((f32[8,96,256]{2,1,0:T(8,128)}), f32[8,96,256]{2,1,0:T(8,128)S(1)}, u32[]{:S(2)}, u32[]{:S(2)}) %all-to-all-start.4) | async-done | bytes 786464 | tf_op jit(solution)/shard_map/all_to_all | solution.py:142
  152.8 2.1 fusion.14
  154.9 3.8 %collective-permute-done.18.refs_2_ = bf16[768,256]{1,0:T(8,128)(2,1)} collective-permute-done((bf16[768,256]{1,0:T(8,128)(2,1)S(1)}, bf16[768,256]{1,0:T(8,128)(2,1)}, u32[]{:S(2)}, u32[]{:S(2)}) %collective-permute-start.18) | collective-permute-done | bytes 393248 | tf_op jit(solution)/shard_map/ppermute | solution.py:28
  158.8 3.9 %collective-permute-start.23 = (bf16[768,256]{1,0:T(8,128)(2,1)}, bf16[768,256]{1,0:T(8,128)(2,1)S(1)}, u32[]{:S(2)}, u32[]{:S(2)}) collective-permute-start(bf16[768,256]{1,0:T(8,128)(2,1)} %collective-permute-done.18.refs_2_), channel_id=1, source_target_pairs={{0,8},{1,9},{2,10},{3,11},{4,12},{5,13},{6,14},{7,15},{8,0},{9,1},... | collective-permute-start | bytes 1179656 | tf_op jit(solution)/shard_map/ppermute | solution.py:28
  162.9 0.4 collective-permute-start.25
  163.5 0.6 collective-permute-start.27
  164.3 2.7 %collective-permute-start.28 = (bf16[768,256]{1,0:T(8,128)(2,1)}, bf16[768,256]{1,0:T(8,128)(2,1)S(1)}, u32[]{:S(2)}, u32[]{:S(2)}) collective-permute-start(bf16[768,256]{1,0:T(8,128)(2,1)} %collective-permute-done.18.refs_2_), channel_id=1, source_target_pairs={{0,96},{1,97},{2,98},{3,99},{4,100},{5,101},{6,102},{7,103},{8,104... | collective-permute-start | bytes 1179656 | tf_op jit(solution)/shard_map/ppermute | solution.py:28
  167.0 1.3 collective-permute-start.29
  168.3 2.9 %collective-permute-start.30 = (f32[1,256]{1,0:T(1,128)S(1)}, f32[1,256]{1,0:T(1,128)S(1)}, u32[]{:S(2)}, u32[]{:S(2)}) collective-permute-start(f32[1,256]{1,0:T(1,128)S(1)} %get-tuple-element.69), channel_id=1, source_target_pairs={{0,8},{8,16},{16,24},{24,32},{32,40},{40,48},{48,56},{56,64},{64,7... | collective-permute-start | bytes 3080 | tf_op jit(solution)/shard_map/ppermute | solution.py:64
  171.2 2.1 collective-permute-start.31
  173.4 7.3 %shard_map.82.refs_6_ = f32[768,256]{1,0:T(8,128)S(1)} custom-call(s32[10]{0:T(128)S(1)} %stack.99.order_ref, bf16[768,12288]{1,0:T(8,128)(2,1)} %kernel_ref.3, bf16[768,256]{1,0:T(8,128)(2,1)} %bitcast.72, bf16[768,256]{1,0:T(8,128)(2,1)} %collective-permute-done.22.refs_1_, bf16[768,256]{1,0:T(8,128)(2,1)} %collective-permute-done.18.refs_2_, ...), custom_call_target="tpu_custom_call" | custom-call | tf_op jit(solution)/shard_map/pallas_call | solution.py:197
  180.7 0.7 broadcast_multiply_fusion
  181.5 0.8 bitcast_subtract_fusion
  182.5 0.5 collective-permute-start.33
  183.6 0.5 collective-permute-done.32.refs_1_
  184.2 0.6 collective-permute-done.33.refs_3_
  184.7 0.6 collective-permute-done.34.refs_5_
  185.5 0.8 copy-done.28
  186.2 5.7 %shard_map.83 = (f32[768,256]{1,0:T(8,128)S(1)}, f32[128,1,128]{2,1,0:T(1,128)S(1)}) custom-call(s32[6]{0:T(128)S(1)} %stack.85.order_ref, bf16[768,12288]{1,0:T(8,128)(2,1)} %kernel_ref.3, bf16[768,256]{1,0:T(8,128)(2,1)} %copy-done.23, bf16[768,256]{1,0:T(8,128)(2,1)} %copy-done.26, bf16[768,256]{1,0:T(8,128)(2,1)} %copy-done.24, ...), custom_call_target="tpu_custom_call" | custom-call | tf_op jit(solution)/shard_map/pallas_call | solution.py:197
  192.0 19.4 %all_to_all.32.sums_ref = f32[128,1,128]{2,1,0:T(1,128)S(1)} all-to-all(f32[128,1,128]{2,1,0:T(1,128)S(1)} %get-tuple-element.78), channel_id=1, replica_groups=mesh['geno'=16,'trial'=8] {'geno','trial'}, dimensions={0} | all-to-all | bytes 131072 | tf_op jit(solution)/shard_map/all_to_all | solution.py:146
  211.3 2.0 shard_map.84
  (104 shorter events, 4.7 us)
Async XLA Ops:
  7.2 1.2 copy-start
  7.2 3.9 %copy-start.10 = (f32[768,1,256]{2,1,0:T(1,128)S(1)}, f32[768,1,256]{2,1,0:T(1,128)}, u32[]{:S(2)}) copy-start(f32[768,1,256]{2,1,0:T(1,128)} %param.6) | copy-start | bytes 2359300
  7.2 3.9 %copy-start.1 = (s32[768,256]{1,0:T(8,128)S(1)}, s32[768,256]{1,0:T(8,128)}, u32[]{:S(2)}) copy-start(s32[768,256]{1,0:T(8,128)} %seen_ref.1) | copy-start | bytes 2359300
  7.2 74.5 %all-gather.3.cloned.1.call-start = ((), (), s32[]{:S(2)}) async-start(), calls=%async_computation.6 | async-start | bytes 2949120 | tf_op jit(solution)/shard_map/all_gather | solution.py:409
  9.2 19.0 %copy-start.8 = (f32[256]{0:T(256)S(1)}, f32[256]{0:T(256)}, u32[]{:S(2)}) copy-start(f32[256]{0:T(256)} %param.9) | copy-start | bytes 3076
  9.3 19.0 %copy-start.9 = (s32[256]{0:T(256)S(1)}, s32[256]{0:T(256)}, u32[]{:S(2)}) copy-start(s32[256]{0:T(256)} %param.8) | copy-start | bytes 3076
  11.3 30.2 %copy-start.13 = (bf16[768,256]{1,0:T(8,128)(2,1)}, bf16[768,256]{1,0:T(8,128)(2,1)S(1)}, u32[]{:S(2)}) copy-start(bf16[768,256]{1,0:T(8,128)(2,1)S(1)} %multiply_convert_fusion.refs_0_) | copy-start | bytes 1179652
  11.3 18.2 %collective-permute-start = (bf16[768,256]{1,0:T(8,128)(2,1)S(1)}, bf16[768,256]{1,0:T(8,128)(2,1)S(1)}, u32[]{:S(2)}, u32[]{:S(2)}) collective-permute-start(bf16[768,256]{1,0:T(8,128)(2,1)S(1)} %multiply_convert_fusion.refs_0_), channel_id=1, source_target_pairs={{0,16},{1,17},{2,18},{3,19},{4,20},{5,21},{6,22},{7,23},{8,24},{9,... | collective-permute-start | bytes 1179656 | tf_op jit(solution)/shard_map/ppermute | solution.py:28
  13.8 15.7 %collective-permute-start.1 = (bf16[768,256]{1,0:T(8,128)(2,1)S(1)}, bf16[768,256]{1,0:T(8,128)(2,1)S(1)}, u32[]{:S(2)}, u32[]{:S(2)}) collective-permute-start(bf16[768,256]{1,0:T(8,128)(2,1)S(1)} %multiply_convert_fusion.refs_0_), channel_id=1, source_target_pairs={{0,32},{1,33},{2,34},{3,35},{4,36},{5,37},{6,38},{7,39},{8,40},{9,... | collective-permute-start | bytes 1179656 | tf_op jit(solution)/shard_map/ppermute | solution.py:28
  15.1 14.4 %collective-permute-start.2 = (bf16[768,256]{1,0:T(8,128)(2,1)S(1)}, bf16[768,256]{1,0:T(8,128)(2,1)S(1)}, u32[]{:S(2)}, u32[]{:S(2)}) collective-permute-start(bf16[768,256]{1,0:T(8,128)(2,1)S(1)} %multiply_convert_fusion.refs_0_), channel_id=1, source_target_pairs={{0,96},{1,97},{2,98},{3,99},{4,100},{5,101},{6,102},{7,103},{8,104... | collective-permute-start | bytes 1179656 | tf_op jit(solution)/shard_map/ppermute | solution.py:28
  16.6 17.9 %collective-permute-start.3 = (bf16[768,256]{1,0:T(8,128)(2,1)S(1)}, bf16[768,256]{1,0:T(8,128)(2,1)}, u32[]{:S(2)}, u32[]{:S(2)}) collective-permute-start(bf16[768,256]{1,0:T(8,128)(2,1)S(1)} %multiply_convert_fusion.refs_0_), channel_id=1, source_target_pairs={{0,64},{1,65},{2,66},{3,67},{4,68},{5,69},{6,70},{7,71},{8,72},{9,... | collective-permute-start | bytes 1179656 | tf_op jit(solution)/shard_map/ppermute | solution.py:28
  18.2 4.1 %collective-permute-start.4 = (f32[1,256]{1,0:T(1,128)S(1)}, f32[1,256]{1,0:T(1,128)S(1)}, u32[]{:S(2)}, u32[]{:S(2)}) collective-permute-start(f32[1,256]{1,0:T(1,128)S(1)} %get-tuple-element.85), channel_id=1, source_target_pairs={{0,8},{8,16},{16,24},{24,32},{32,40},{40,48},{48,56},{56,64},{64,7... | collective-permute-start | bytes 3080 | tf_op jit(solution)/shard_map/ppermute | solution.py:405
  22.3 5.9 %collective-permute-start.5 = (f32[1,256]{1,0:T(1,128)S(1)}, f32[1,256]{1,0:T(1,128)S(1)}, u32[]{:S(2)}, u32[]{:S(2)}) collective-permute-start(f32[1,256]{1,0:T(1,128)S(1)} %get-tuple-element.84), channel_id=1, source_target_pairs={{8,0},{16,8},{24,16},{32,24},{40,32},{48,40},{56,48},{64,56},{72,6... | collective-permute-start | bytes 3080 | tf_op jit(solution)/shard_map/ppermute | solution.py:406
  25.5 9.0 %copy-start.2 = (f32[768,1,256]{2,0,1:T(8,128)}, f32[768,1,256]{2,0,1:T(8,128)S(1)}, u32[]{:S(2)}) copy-start(f32[768,1,256]{2,0,1:T(8,128)S(1)} %copy.18) | copy-start | bytes 2359300
  28.4 1.1 copy-start.4
  29.5 5.0 %copy-start.14 = (bf16[768,256]{1,0:T(8,128)(2,1)}, bf16[768,256]{1,0:T(8,128)(2,1)S(1)}, u32[]{:S(2)}) copy-start(bf16[768,256]{1,0:T(8,128)(2,1)S(1)} %collective-permute-done.refs_2_) | copy-start | bytes 1179652
  30.3 0.8 copy-start.17
  34.5 34.8 %all-to-all-start = ((bf16[8,304,256]{2,1,0:T(8,128)(2,1)}), bf16[8,304,256]{2,1,0:T(8,128)(2,1)S(1)}, u32[]{:S(2)}, u32[]{:S(2)}) async-start(bf16[8,304,256]{2,1,0:T(8,128)(2,1)} %copy-done.4), calls=%async_computation | async-start | bytes 2490368 | tf_op jit(solution)/shard_map/all_to_all | solution.py:142
  41.5 3.6 %collective-permute-start.6 = (bf16[768,256]{1,0:T(8,128)(2,1)S(1)}, bf16[768,256]{1,0:T(8,128)(2,1)S(1)}, u32[]{:S(2)}, u32[]{:S(2)}) collective-permute-start(bf16[768,256]{1,0:T(8,128)(2,1)S(1)} %multiply_convert_fusion.refs_0_), channel_id=1, source_target_pairs={{0,8},{1,9},{2,10},{3,11},{4,12},{5,13},{6,14},{7,15},{8,0},{9,1},... | collective-permute-start | bytes 1179656 | tf_op jit(solution)/shard_map/ppermute | solution.py:28
  43.7 5.3 %collective-permute-start.7 = (bf16[768,256]{1,0:T(8,128)(2,1)}, bf16[768,256]{1,0:T(8,128)(2,1)}, u32[]{:S(2)}, u32[]{:S(2)}) collective-permute-start(bf16[768,256]{1,0:T(8,128)(2,1)} %copy-done.14), channel_id=1, source_target_pairs={{0,8},{1,9},{2,10},{3,11},{4,12},{5,13},{6,14},{7,15},{8,0},{9,1},... | collective-permute-start | bytes 1179656 | tf_op jit(solution)/shard_map/ppermute | solution.py:28
  43.8 6.8 %collective-permute-start.10 = (bf16[768,256]{1,0:T(8,128)(2,1)}, bf16[768,256]{1,0:T(8,128)(2,1)}, u32[]{:S(2)}, u32[]{:S(2)}) collective-permute-start(bf16[768,256]{1,0:T(8,128)(2,1)} %collective-permute-done.3.refs_8_), channel_id=1, source_target_pairs={{0,8},{1,9},{2,10},{3,11},{4,12},{5,13},{6,14},{7,15},{8,0},{9,1},... | collective-permute-start | bytes 1179656 | tf_op jit(solution)/shard_map/ppermute | solution.py:28
  44.2 7.6 %collective-permute-start.8 = (bf16[768,256]{1,0:T(8,128)(2,1)}, bf16[768,256]{1,0:T(8,128)(2,1)}, u32[]{:S(2)}, u32[]{:S(2)}) collective-permute-start(bf16[768,256]{1,0:T(8,128)(2,1)} %copy-done.16), channel_id=1, source_target_pairs={{0,8},{1,9},{2,10},{3,11},{4,12},{5,13},{6,14},{7,15},{8,0},{9,1},... | collective-permute-start | bytes 1179656 | tf_op jit(solution)/shard_map/ppermute | solution.py:28
  44.3 7.5 %collective-permute-start.9 = (bf16[768,256]{1,0:T(8,128)(2,1)}, bf16[768,256]{1,0:T(8,128)(2,1)}, u32[]{:S(2)}, u32[]{:S(2)}) collective-permute-start(bf16[768,256]{1,0:T(8,128)(2,1)} %copy-done.17), channel_id=1, source_target_pairs={{0,8},{1,9},{2,10},{3,11},{4,12},{5,13},{6,14},{7,15},{8,0},{9,1},... | collective-permute-start | bytes 1179656 | tf_op jit(solution)/shard_map/ppermute | solution.py:28
  45.8 14.2 %collective-permute-start.11 = (bf16[768,256]{1,0:T(8,128)(2,1)}, bf16[768,256]{1,0:T(8,128)(2,1)S(1)}, u32[]{:S(2)}, u32[]{:S(2)}) collective-permute-start(bf16[768,256]{1,0:T(8,128)(2,1)} %copy-done.14), channel_id=1, source_target_pairs={{0,32},{1,33},{2,34},{3,35},{4,36},{5,37},{6,38},{7,39},{8,40},{9,... | collective-permute-start | bytes 1179656 | tf_op jit(solution)/shard_map/ppermute | solution.py:28
  49.1 10.9 %collective-permute-start.12 = (bf16[768,256]{1,0:T(8,128)(2,1)}, bf16[768,256]{1,0:T(8,128)(2,1)}, u32[]{:S(2)}, u32[]{:S(2)}) collective-permute-start(bf16[768,256]{1,0:T(8,128)(2,1)} %copy-done.14), channel_id=1, source_target_pairs={{0,96},{1,97},{2,98},{3,99},{4,100},{5,101},{6,102},{7,103},{8,104... | collective-permute-start | bytes 1179656 | tf_op jit(solution)/shard_map/ppermute | solution.py:28
  50.6 18.7 %collective-permute-start.13 = (bf16[768,256]{1,0:T(8,128)(2,1)}, bf16[768,256]{1,0:T(8,128)(2,1)}, u32[]{:S(2)}, u32[]{:S(2)}) collective-permute-start(bf16[768,256]{1,0:T(8,128)(2,1)} %copy-done.14), channel_id=1, source_target_pairs={{0,64},{1,65},{2,66},{3,67},{4,68},{5,69},{6,70},{7,71},{8,72},{9,... | collective-permute-start | bytes 1179656 | tf_op jit(solution)/shard_map/ppermute | solution.py:28
  59.1 0.9 copy-start.5
  60.0 13.3 %copy-start.15 = (bf16[768,256]{1,0:T(8,128)(2,1)}, bf16[768,256]{1,0:T(8,128)(2,1)S(1)}, u32[]{:S(2)}) copy-start(bf16[768,256]{1,0:T(8,128)(2,1)S(1)} %collective-permute-done.11.refs_0_) | copy-start | bytes 1179652
  69.3 3.2 %collective-permute-start.14 = (bf16[768,256]{1,0:T(8,128)(2,1)S(1)}, bf16[768,256]{1,0:T(8,128)(2,1)}, u32[]{:S(2)}, u32[]{:S(2)}) collective-permute-start(bf16[768,256]{1,0:T(8,128)(2,1)S(1)} %collective-permute-done.11.refs_0_), channel_id=1, source_target_pairs={{0,8},{1,9},{2,10},{3,11},{4,12},{5,13},{6,14},{7,15},{8,0},{9,1},... | collective-permute-start | bytes 1179656 | tf_op jit(solution)/shard_map/ppermute | solution.py:28
  70.4 2.3 %collective-permute-start.15 = (bf16[768,256]{1,0:T(8,128)(2,1)}, bf16[768,256]{1,0:T(8,128)(2,1)}, u32[]{:S(2)}, u32[]{:S(2)}) collective-permute-start(bf16[768,256]{1,0:T(8,128)(2,1)} %collective-permute-done.12.refs_2_), channel_id=1, source_target_pairs={{0,8},{1,9},{2,10},{3,11},{4,12},{5,13},{6,14},{7,15},{8,0},{9,1},... | collective-permute-start | bytes 1179656 | tf_op jit(solution)/shard_map/ppermute | solution.py:28
  70.5 2.8 %collective-permute-start.16 = (bf16[768,256]{1,0:T(8,128)(2,1)}, bf16[768,256]{1,0:T(8,128)(2,1)}, u32[]{:S(2)}, u32[]{:S(2)}) collective-permute-start(bf16[768,256]{1,0:T(8,128)(2,1)} %collective-permute-done.13.refs_4_), channel_id=1, source_target_pairs={{0,8},{1,9},{2,10},{3,11},{4,12},{5,13},{6,14},{7,15},{8,0},{9,1},... | collective-permute-start | bytes 1179656 | tf_op jit(solution)/shard_map/ppermute | solution.py:28
  73.3 1.1 copy-start.6
  81.7 15.7 %collective-permute-start.17 = (bf16[8,128,1280]{2,1,0:T(8,128)(2,1)}, bf16[8,128,1280]{2,1,0:T(8,128)(2,1)}, u32[]{:S(2)}, u32[]{:S(2)}) collective-permute-start(bf16[8,128,1280]{2,1,0:T(8,128)(2,1)} %bitcast.64), channel_id=1, source_target_pairs={{0,8},{1,9},{2,10},{3,11},{4,12},{5,13},{6,14},{7,15},{8,0},{9,1},... | collective-permute-start | bytes 7864328 | tf_op jit(solution)/shard_map/ppermute | solution.py:28
  82.6 14.8 %all-to-all-start.1 = ((bf16[8,96,256]{2,1,0:T(8,128)(2,1)}), bf16[8,96,256]{2,1,0:T(8,128)(2,1)S(1)}, u32[]{:S(2)}, u32[]{:S(2)}) async-start(bf16[8,96,256]{2,1,0:T(8,128)(2,1)} %bitcast.23), calls=%async_computation.1 | async-start | bytes 786432 | tf_op jit(solution)/shard_map/all_to_all | solution.py:142
  103.2 22.8 %copy-start.7 = (f32[8,96,256]{2,1,0:T(8,128)}, f32[8,96,256]{2,1,0:T(8,128)S(1)}, u32[]{:S(2)}) copy-start(f32[8,96,256]{2,1,0:T(8,128)S(1)} %get-tuple-element.60.image_ref) | copy-start | bytes 2359300
  137.7 35.7 %copy-start.12 = (bf16[8,96,256]{2,1,0:T(8,128)(2,1)}, bf16[8,96,256]{2,1,0:T(8,128)(2,1)S(1)}, u32[]{:S(2)}) copy-start(bf16[8,96,256]{2,1,0:T(8,128)(2,1)S(1)} %all_to_all.31) | copy-start | bytes 1179652
  137.7 15.1 %all-to-all-start.4 = ((f32[8,96,256]{2,1,0:T(8,128)}), f32[8,96,256]{2,1,0:T(8,128)S(1)}, u32[]{:S(2)}, u32[]{:S(2)}) async-start(f32[8,96,256]{2,1,0:T(8,128)} %copy-done.7), calls=%async_computation.4 | async-start | bytes 1572864 | tf_op jit(solution)/shard_map/all_to_all | solution.py:142
  141.3 17.4 %collective-permute-start.18 = (bf16[768,256]{1,0:T(8,128)(2,1)S(1)}, bf16[768,256]{1,0:T(8,128)(2,1)}, u32[]{:S(2)}, u32[]{:S(2)}) collective-permute-start(bf16[768,256]{1,0:T(8,128)(2,1)S(1)} %bitcast.67), channel_id=1, source_target_pairs={{0,16},{1,17},{2,18},{3,19},{4,20},{5,21},{6,22},{7,23},{8,24},{9,... | collective-permute-start | bytes 1179656 | tf_op jit(solution)/shard_map/ppermute | solution.py:28
  141.5 17.2 %collective-permute-start.19 = (bf16[768,256]{1,0:T(8,128)(2,1)S(1)}, bf16[768,256]{1,0:T(8,128)(2,1)}, u32[]{:S(2)}, u32[]{:S(2)}) collective-permute-start(bf16[768,256]{1,0:T(8,128)(2,1)S(1)} %bitcast.68), channel_id=1, source_target_pairs={{0,32},{1,33},{2,34},{3,35},{4,36},{5,37},{6,38},{7,39},{8,40},{9,... | collective-permute-start | bytes 1179656 | tf_op jit(solution)/shard_map/ppermute | solution.py:28
  141.9 16.8 %collective-permute-start.20 = (bf16[768,256]{1,0:T(8,128)(2,1)S(1)}, bf16[768,256]{1,0:T(8,128)(2,1)}, u32[]{:S(2)}, u32[]{:S(2)}) collective-permute-start(bf16[768,256]{1,0:T(8,128)(2,1)S(1)} %bitcast.69), channel_id=1, source_target_pairs={{0,96},{1,97},{2,98},{3,99},{4,100},{5,101},{6,102},{7,103},{8,104... | collective-permute-start | bytes 1179656 | tf_op jit(solution)/shard_map/ppermute | solution.py:28
  144.2 14.7 %collective-permute-start.21 = (bf16[768,256]{1,0:T(8,128)(2,1)S(1)}, bf16[768,256]{1,0:T(8,128)(2,1)}, u32[]{:S(2)}, u32[]{:S(2)}) collective-permute-start(bf16[768,256]{1,0:T(8,128)(2,1)S(1)} %bitcast.70), channel_id=1, source_target_pairs={{0,64},{1,65},{2,66},{3,67},{4,68},{5,69},{6,70},{7,71},{8,72},{9,... | collective-permute-start | bytes 1179656 | tf_op jit(solution)/shard_map/ppermute | solution.py:28
  144.9 18.6 %collective-permute-start.22 = (bf16[768,256]{1,0:T(8,128)(2,1)S(1)}, bf16[768,256]{1,0:T(8,128)(2,1)}, u32[]{:S(2)}, u32[]{:S(2)}) collective-permute-start(bf16[768,256]{1,0:T(8,128)(2,1)S(1)} %bitcast.71), channel_id=1, source_target_pairs={{0,8},{1,9},{2,10},{3,11},{4,12},{5,13},{6,14},{7,15},{8,0},{9,1},... | collective-permute-start | bytes 1179656 | tf_op jit(solution)/shard_map/ppermute | solution.py:28
  158.8 5.5 %collective-permute-start.23 = (bf16[768,256]{1,0:T(8,128)(2,1)}, bf16[768,256]{1,0:T(8,128)(2,1)S(1)}, u32[]{:S(2)}, u32[]{:S(2)}) collective-permute-start(bf16[768,256]{1,0:T(8,128)(2,1)} %collective-permute-done.18.refs_2_), channel_id=1, source_target_pairs={{0,8},{1,9},{2,10},{3,11},{4,12},{5,13},{6,14},{7,15},{8,0},{9,1},... | collective-permute-start | bytes 1179656 | tf_op jit(solution)/shard_map/ppermute | solution.py:28
  162.8 4.2 %collective-permute-start.24 = (bf16[768,256]{1,0:T(8,128)(2,1)}, bf16[768,256]{1,0:T(8,128)(2,1)S(1)}, u32[]{:S(2)}, u32[]{:S(2)}) collective-permute-start(bf16[768,256]{1,0:T(8,128)(2,1)} %collective-permute-done.19.refs_4_), channel_id=1, source_target_pairs={{0,8},{1,9},{2,10},{3,11},{4,12},{5,13},{6,14},{7,15},{8,0},{9,1},... | collective-permute-start | bytes 1179656 | tf_op jit(solution)/shard_map/ppermute | solution.py:28
  162.9 5.5 %collective-permute-start.25 = (bf16[768,256]{1,0:T(8,128)(2,1)}, bf16[768,256]{1,0:T(8,128)(2,1)S(1)}, u32[]{:S(2)}, u32[]{:S(2)}) collective-permute-start(bf16[768,256]{1,0:T(8,128)(2,1)} %collective-permute-done.20.refs_6_), channel_id=1, source_target_pairs={{0,8},{1,9},{2,10},{3,11},{4,12},{5,13},{6,14},{7,15},{8,0},{9,1},... | collective-permute-start | bytes 1179656 | tf_op jit(solution)/shard_map/ppermute | solution.py:28
  163.3 7.9 %collective-permute-start.26 = (bf16[768,256]{1,0:T(8,128)(2,1)}, bf16[768,256]{1,0:T(8,128)(2,1)S(1)}, u32[]{:S(2)}, u32[]{:S(2)}) collective-permute-start(bf16[768,256]{1,0:T(8,128)(2,1)} %collective-permute-done.21.refs_8_), channel_id=1, source_target_pairs={{0,8},{1,9},{2,10},{3,11},{4,12},{5,13},{6,14},{7,15},{8,0},{9,1},... | collective-permute-start | bytes 1179656 | tf_op jit(solution)/shard_map/ppermute | solution.py:28
  163.5 18.0 %copy-start.11 = (f32[768,1,256]{2,1,0:T(1,128)S(1)}, f32[768,1,256]{2,1,0:T(1,128)}, u32[]{:S(2)}) copy-start(f32[768,1,256]{2,1,0:T(1,128)} %param.6) | copy-start | bytes 2359300
  163.5 18.8 %collective-permute-start.27 = (bf16[768,256]{1,0:T(8,128)(2,1)}, bf16[768,256]{1,0:T(8,128)(2,1)S(1)}, u32[]{:S(2)}, u32[]{:S(2)}) collective-permute-start(bf16[768,256]{1,0:T(8,128)(2,1)} %collective-permute-done.18.refs_2_), channel_id=1, source_target_pairs={{0,32},{1,33},{2,34},{3,35},{4,36},{5,37},{6,38},{7,39},{8,40},{9,... | collective-permute-start | bytes 1179656 | tf_op jit(solution)/shard_map/ppermute | solution.py:28
  164.3 9.1 %copy-start.19 = (bf16[768,256]{1,0:T(8,128)(2,1)}, bf16[768,256]{1,0:T(8,128)(2,1)S(1)}, u32[]{:S(2)}) copy-start(bf16[768,256]{1,0:T(8,128)(2,1)S(1)} %collective-permute-done.23.refs_3_) | copy-start | bytes 1179652
  164.3 18.0 %collective-permute-start.28 = (bf16[768,256]{1,0:T(8,128)(2,1)}, bf16[768,256]{1,0:T(8,128)(2,1)S(1)}, u32[]{:S(2)}, u32[]{:S(2)}) collective-permute-start(bf16[768,256]{1,0:T(8,128)(2,1)} %collective-permute-done.18.refs_2_), channel_id=1, source_target_pairs={{0,96},{1,97},{2,98},{3,99},{4,100},{5,101},{6,102},{7,103},{8,104... | collective-permute-start | bytes 1179656 | tf_op jit(solution)/shard_map/ppermute | solution.py:28
  167.0 6.4 %copy-start.20 = (bf16[768,256]{1,0:T(8,128)(2,1)}, bf16[768,256]{1,0:T(8,128)(2,1)S(1)}, u32[]{:S(2)}) copy-start(bf16[768,256]{1,0:T(8,128)(2,1)S(1)} %collective-permute-done.24.refs_5_) | copy-start | bytes 1179652
  167.0 15.3 %collective-permute-start.29 = (bf16[768,256]{1,0:T(8,128)(2,1)}, bf16[768,256]{1,0:T(8,128)(2,1)S(1)}, u32[]{:S(2)}, u32[]{:S(2)}) collective-permute-start(bf16[768,256]{1,0:T(8,128)(2,1)} %collective-permute-done.21.refs_8_), channel_id=1, source_target_pairs={{0,16},{1,17},{2,18},{3,19},{4,20},{5,21},{6,22},{7,23},{8,24},{9,... | collective-permute-start | bytes 1179656 | tf_op jit(solution)/shard_map/ppermute | solution.py:28
  168.3 5.1 %copy-start.21 = (bf16[768,256]{1,0:T(8,128)(2,1)}, bf16[768,256]{1,0:T(8,128)(2,1)S(1)}, u32[]{:S(2)}) copy-start(bf16[768,256]{1,0:T(8,128)(2,1)S(1)} %collective-permute-done.25.refs_7_) | copy-start | bytes 1179652
  168.3 14.0 %collective-permute-start.30 = (f32[1,256]{1,0:T(1,128)S(1)}, f32[1,256]{1,0:T(1,128)S(1)}, u32[]{:S(2)}, u32[]{:S(2)}) collective-permute-start(f32[1,256]{1,0:T(1,128)S(1)} %get-tuple-element.69), channel_id=1, source_target_pairs={{0,8},{8,16},{16,24},{24,32},{32,40},{40,48},{48,56},{56,64},{64,7... | collective-permute-start | bytes 3080 | tf_op jit(solution)/shard_map/ppermute | solution.py:64
  171.2 2.2 copy-start.22
  171.2 11.1 %collective-permute-start.31 = (f32[1,256]{1,0:T(1,128)S(1)}, f32[1,256]{1,0:T(1,128)S(1)}, u32[]{:S(2)}, u32[]{:S(2)}) collective-permute-start(f32[1,256]{1,0:T(1,128)S(1)} %get-tuple-element.70), channel_id=1, source_target_pairs={{8,0},{16,8},{24,16},{32,24},{40,32},{48,40},{56,48},{64,56},{72,6... | collective-permute-start | bytes 3080 | tf_op jit(solution)/shard_map/ppermute | solution.py:65
  182.3 3.0 %copy-start.23 = (bf16[768,256]{1,0:T(8,128)(2,1)}, bf16[768,256]{1,0:T(8,128)(2,1)S(1)}, u32[]{:S(2)}) copy-start(bf16[768,256]{1,0:T(8,128)(2,1)S(1)} %collective-permute-done.27.refs_0_) | copy-start | bytes 1179652
  182.3 3.0 %copy-start.24 = (bf16[768,256]{1,0:T(8,128)(2,1)}, bf16[768,256]{1,0:T(8,128)(2,1)S(1)}, u32[]{:S(2)}) copy-start(bf16[768,256]{1,0:T(8,128)(2,1)S(1)} %collective-permute-done.28.refs_2_) | copy-start | bytes 1179652
  182.4 2.9 %copy-start.25 = (bf16[768,256]{1,0:T(8,128)(2,1)}, bf16[768,256]{1,0:T(8,128)(2,1)S(1)}, u32[]{:S(2)}) copy-start(bf16[768,256]{1,0:T(8,128)(2,1)S(1)} %collective-permute-done.29.refs_4_) | copy-start | bytes 1179652
  182.4 1.8 collective-permute-start.32
  182.5 2.3 %collective-permute-start.33 = (bf16[768,256]{1,0:T(8,128)(2,1)S(1)}, bf16[768,256]{1,0:T(8,128)(2,1)S(1)}, u32[]{:S(2)}, u32[]{:S(2)}) collective-permute-start(bf16[768,256]{1,0:T(8,128)(2,1)S(1)} %collective-permute-done.28.refs_2_), channel_id=1, source_target_pairs={{0,8},{1,9},{2,10},{3,11},{4,12},{5,13},{6,14},{7,15},{8,0},{9,1},... | collective-permute-start | bytes 1179656 | tf_op jit(solution)/shard_map/ppermute | solution.py:28
  183.0 2.3 %collective-permute-start.34 = (bf16[768,256]{1,0:T(8,128)(2,1)S(1)}, bf16[768,256]{1,0:T(8,128)(2,1)S(1)}, u32[]{:S(2)}, u32[]{:S(2)}) collective-permute-start(bf16[768,256]{1,0:T(8,128)(2,1)S(1)} %collective-permute-done.29.refs_4_), channel_id=1, source_target_pairs={{0,8},{1,9},{2,10},{3,11},{4,12},{5,13},{6,14},{7,15},{8,0},{9,1},... | collective-permute-start | bytes 1179656 | tf_op jit(solution)/shard_map/ppermute | solution.py:28
  183.6 27.7 %copy-start.3 = (f32[768,1,256]{2,0,1:T(8,128)S(1)}, f32[768,1,256]{2,0,1:T(8,128)}, u32[]{:S(2)}) copy-start(f32[768,1,256]{2,0,1:T(8,128)} %copy-done.2) | copy-start | bytes 2359300
  184.2 1.1 copy-start.26
  (4 other events, 3.0 us)
Sparse Core Ops, SparseCore 0:
  11.2 70.4 all-gather.2
